TPU v7x, 32 devices: a whole 2x2x4 slice. The times are simulated.
32 devices in a mesh: dp: 16 (over z, y, core), seq: 2 (over x).
Axes of the slice: x: 2, y: 2, z: 4, core: 2. Of those that a mesh axis runs over, the one named last changes fastest.
Arguments:
- tokens: bfloat16 [32, 1024, 1024], P('dp', 'seq'), may hold values from -6 to 6
- cotangent: bfloat16 [32, 1024, 1024], P('dp', 'seq'), may hold values from -6 to 6
- segments: int32 [32, 1024], P('dp'), may hold values from 0 to 3, as said below
- global_blocks: int32 [32, 2], P('dp'), may hold values from 0 to 15, as said below
- random_blocks: int32 [32, 16, 3], P('dp'), may hold values from 0 to 15, as said below
- ln1_gain: bfloat16 [1024], P(('dp', 'seq')), may hold values from 0.5 to 1.5
- ln1_shift: bfloat16 [1024], P(('dp', 'seq')), may hold values from -1.5 to 1.5
- query_weight: bfloat16 [1024, 1024], P(('dp', 'seq')), may hold values from -0.1875 to 0.1875
- query_bias: bfloat16 [1024], P(('dp', 'seq')), may hold values from -1.5 to 1.5
- key_weight: bfloat16 [1024, 1024], P(('dp', 'seq')), may hold values from -0.1875 to 0.1875
- value_weight: bfloat16 [1024, 1024], P(('dp', 'seq')), may hold values from -0.1875 to 0.1875
- value_bias: bfloat16 [1024], P(('dp', 'seq')), may hold values from -1.5 to 1.5
- out_weight: bfloat16 [1024, 1024], P(('dp', 'seq')), may hold values from -0.5 to 0.5
- out_bias: bfloat16 [1024], P(('dp', 'seq')), may hold values from -1.5 to 1.5
- ln2_gain: bfloat16 [1024], P(('dp', 'seq')), may hold values from 0.5 to 1.5
- ln2_shift: bfloat16 [1024], P(('dp', 'seq')), may hold values from -1.5 to 1.5
- up_weight: bfloat16 [1024, 4096], P(('dp', 'seq')), may hold values from -0.1875 to 0.1875
- up_bias: bfloat16 [4096], P(('dp', 'seq')), may hold values from -1.5 to 1.5
- down_weight: bfloat16 [4096, 1024], P(('dp', 'seq')), may hold values from -0.125 to 0.125
- down_bias: bfloat16 [1024], P(('dp', 'seq')), may hold values from -1.5 to 1.5
Outputs:
- mixed: bfloat16 [32, 1024, 1024], P('dp', 'seq')
- token_grad: bfloat16 [32, 1024, 1024], P('dp', 'seq')
- grad_ln1_gain: float32 [1024], P(('dp', 'seq'))
- grad_ln1_shift: float32 [1024], P(('dp', 'seq'))
- grad_query_weight: float32 [1024, 1024], P(('dp', 'seq'))
- grad_query_bias: float32 [1024], P(('dp', 'seq'))
- grad_key_weight: float32 [1024, 1024], P(('dp', 'seq'))
- grad_value_weight: float32 [1024, 1024], P(('dp', 'seq'))
- grad_value_bias: float32 [1024], P(('dp', 'seq'))
- grad_out_weight: float32 [1024, 1024], P(('dp', 'seq'))
- grad_out_bias: float32 [1024], P(('dp', 'seq'))
- grad_ln2_gain: float32 [1024], P(('dp', 'seq'))
- grad_ln2_shift: float32 [1024], P(('dp', 'seq'))
- grad_up_weight: float32 [1024, 4096], P(('dp', 'seq'))
- grad_up_bias: float32 [4096], P(('dp', 'seq'))
- grad_down_weight: float32 [4096, 1024], P(('dp', 'seq'))
- grad_down_bias: float32 [1024], P(('dp', 'seq'))
Inputs may be any that keep to these rules, and one draw needn't show every extreme that they name: `segments`: each sequence holds four documents numbered 0 to 3 in order; document 0 and 1 end within the first 512 tokens, document 3 starts within the last 512 tokens. `global_blocks`: the first global block lies in the first half of the 16 blocks, the second in the second half. `random_blocks`: random block k of query block j lies in the run of 8 blocks numbered ((j // 8) + 3 * (j % 8) + k) mod (2); it may repeat a window, global or other random block of j, which then counts once.
All inputs are finite; a program needn't handle non-finite values.
Results may differ from a plain program's by a relative error of at most 0.018.
Values may be sent and summed in bfloat16 or wider, within the bound.
No kernel may reach another device: no remote copies, remote signals or barrier semaphores. Data moves between devices by JAX's collectives and lax.ppermute only.
A program may use at most 448 MiB of HBM per device.

v0:
```python
from functools import partial
import math

import jax
import jax.numpy as jnp
from jax import lax
from jax.experimental import pallas as pl
from jax.experimental.pallas import tpu as pltpu
from jax.sharding import PartitionSpec as P

HEADS = 16
BLK = 64
EPSILON = 1e-06
MASKED = -1e30
DP, SEQ = "dp", "seq"
BOTH = (DP, SEQ)
BF, F32 = jnp.bfloat16, jnp.float32
NT = (((1,), (1,)), ((), ()))
NN = (((1,), (0,)), ((), ()))
TN = (((0,), (0,)), ((), ()))
VMEM_BYTES = 60 * 2**20
TILE = 256
GROUPS = 2


def dot(left, right, dims=NN):
    return lax.dot_general(left, right, dims, preferred_element_type=F32)


class Grid:
    def __init__(self):
        self.dp = lax.axis_size(DP)
        self.group = lax.axis_size(SEQ)
        self.cube = self.group == 2 and self.dp % 4 == 0
        if self.cube:
            self.nz = self.dp // 4
            place = lax.axis_index(DP)
            self.x = lax.axis_index(SEQ)
            self.z, self.y, self.core = place // 4, place // 2 % 2, place % 2

    def over_x(self, v):
        return lax.ppermute(v, SEQ, [(0, 1), (1, 0)])

    def over_y(self, v):
        return lax.ppermute(v, DP, [(i, i ^ 2) for i in range(self.dp)])

    def over_core(self, v):
        return lax.ppermute(v, DP, [(i, i ^ 1) for i in range(self.dp)])

    def along_z(self, v, k):
        return lax.ppermute(v, DP, [(i, (i + 4 * k) % self.dp) for i in range(self.dp)])

    def device(self, c, y, x, k):
        z = (self.z - k) % self.nz
        return ((z * 2 + (self.y ^ y)) * 2 + (self.core ^ c)) * 2 + (self.x ^ x)


class Weight:
    def __init__(self, shape):
        self.shape, self.arrays, self.copies, self.rows_at = shape, [], [], []

    def add(self, array, index, rows, row, source=0, width=None, target=0):
        for i, known in enumerate(self.arrays):
            if known is array:
                break
        else:
            i = len(self.arrays)
            self.arrays.append(array)
        self.copies.append((i, index, rows, source, width or array.shape[-1], target))
        self.rows_at.append(row)


def whole_weight(array):
    weight = Weight(array.shape)
    weight.add(array, None, array.shape[0], 0)
    return weight


def weight_of(parts, width):
    pieces = parts[0][0]
    weight = Weight((len(pieces) * pieces[0][0].shape[1], width))
    for pieces, source, columns, target in parts:
        for array, index, device in pieces:
            rows = array.shape[1]
            weight.add(array, index, rows, device * rows, source, columns, target)
    return weight


def gather_pieces(grid, shard, z_first):
    pieces = []
    if not grid.cube:
        every = lax.all_gather(shard, BOTH, axis=0)
        return [(every, i, i) for i in range(every.shape[0])]
    if z_first:
        own = jnp.stack([shard] + [grid.along_z(shard, k) for k in range(1, grid.nz)])
        half = {(0, 0): own, (0, 1): grid.over_x(own)}
        for x in range(2):
            half[1, x] = grid.over_y(half[0, x])
        for (y, x), piece in half.items():
            for c, array in enumerate((piece, grid.over_core(piece))):
                for k in range(grid.nz):
                    pieces.append((array, k, grid.device(c, y, x, k)))
    else:
        pair = jnp.stack([shard, grid.over_x(shard)])
        four = jnp.concatenate([pair, grid.over_y(pair)])
        for k in range(grid.nz):
            piece = four if k == 0 else grid.along_z(four, k)
            for c, array in enumerate((piece, grid.over_core(piece))):
                for j in range(4):
                    pieces.append((array, j, grid.device(c, j // 2, j % 2, k)))
    return pieces


def run(kernel, weights, ins, outs, steps, flops, scratch=(), scalars=()):
    rows_at = [row for w in weights for row in w.rows_at] + list(scalars)
    rows_at = jnp.stack([jnp.asarray(row, jnp.int32) for row in rows_at] or [jnp.int32(0)])
    n_copies = sum(len(w.copies) for w in weights)
    n_pieces = [len(w.arrays) for w in weights]

    def body(at, *refs):
        refs = list(refs)

        def take(count):
            taken, refs[:count] = refs[:count], []
            return taken

        piece_refs = [take(count) for count in n_pieces]
        in_refs, out_refs = take(len(ins)), take(len(outs))
        held = take(len(weights))
        sems = take(1)[0] if n_copies else None

        def copies():
            n = 0
            for weight, sources, target_ref in zip(weights, piece_refs, held):
                for i, index, rows, source, width, target in weight.copies:
                    ref = sources[i] if index is None else sources[i].at[index]
                    row = pl.multiple_of(at[n], rows)
                    yield pltpu.make_async_copy(
                        ref.at[:, pl.ds(source, width)],
                        target_ref.at[pl.ds(row, rows), pl.ds(target, width)],
                        sems.at[n],
                    )
                    n += 1

        if n_copies:

            @pl.when(pl.program_id(0) == 0)
            def _():
                for copy in copies():
                    copy.start()
                for copy in copies():
                    copy.wait()

        values = [at[n_copies + i] for i in range(len(scalars))]
        kernel(values, in_refs, out_refs, held, refs)

    anywhere = pl.BlockSpec(memory_space=pl.ANY)

    def spec(block, index):
        return pl.BlockSpec(block, lambda i, at: index(i))

    moved = sum(math.prod(w.shape) * 2 for w in weights)
    moved += sum(a.size * a.dtype.itemsize for a, _, _ in ins)
    moved += sum(math.prod(s) * jnp.dtype(d).itemsize for s, d, _, _ in outs)
    semaphores = [pltpu.SemaphoreType.DMA((n_copies,))] if n_copies else []
    return pl.pallas_call(
        body,
        grid_spec=pltpu.PrefetchScalarGridSpec(
            num_scalar_prefetch=1,
            grid=(steps,),
            in_specs=[anywhere] * sum(n_pieces) + [spec(block, index) for _, block, index in ins],
            out_specs=[spec(block, index) for _, _, block, index in outs],
            scratch_shapes=[pltpu.VMEM(w.shape, BF) for w in weights] + semaphores + list(scratch),
        ),
        out_shape=[jax.ShapeDtypeStruct(shape, dtype) for shape, dtype, _, _ in outs],
        compiler_params=pltpu.CompilerParams(vmem_limit_bytes=VMEM_BYTES),
        cost_estimate=pl.CostEstimate(flops=int(flops), bytes_accessed=moved, transcendentals=0),
    )(rows_at, *[a for w in weights for a in w.arrays], *[a for a, _, _ in ins])


def pick(array, index, axis):
    return lax.dynamic_index_in_dim(array, index, axis, keepdims=False)


def halve(kept, got, mine, axis, move):
    sent = (pick(kept, 1 - mine, axis).astype(F32) + pick(got, 1 - mine, axis).astype(F32)).astype(kept.dtype)
    own = (pick(kept, mine, axis).astype(F32) + pick(got, mine, axis).astype(F32)).astype(kept.dtype)
    return own, move(sent)


def scatter_sum(grid, kept, sent, z_first):
    got = grid.over_core(sent)
    if z_first:
        parts = []
        for k in range(grid.nz):
            z = (grid.z + k) % grid.nz
            parts.append((pick(kept, z, 0).astype(F32) + pick(got, z, 0).astype(F32)).astype(kept.dtype))
        total = parts[0].astype(F32)
        for k in range(1, grid.nz):
            total = total + grid.along_z(parts[k], k).astype(F32)
        total = total.astype(kept.dtype)
        got = grid.over_y(pick(total, 1 - grid.y, 0))
        total = (pick(total, grid.y, 0).astype(F32) + got.astype(F32)).astype(kept.dtype)
        got = grid.over_x(pick(total, 1 - grid.x, 0))
        return pick(total, grid.x, 0).astype(F32) + got.astype(F32)
    own, got = halve(kept, got, grid.y, 1, grid.over_y)
    own, got = halve(own, got, grid.x, 1, grid.over_x)
    total = pick(own, grid.z, 0).astype(F32) + pick(got, grid.z, 0).astype(F32)
    for k in range(1, grid.nz):
        z = (grid.z + k) % grid.nz
        part = (pick(own, z, 0).astype(F32) + pick(got, z, 0).astype(F32)).astype(kept.dtype)
        total = total + grid.along_z(part, k).astype(F32)
    return total


def to_whole(grid, part):
    group, count = grid.group, part.shape[0]
    if group == 1:
        return part
    place = lax.axis_index(SEQ)
    if group == 2 and count == 2:
        kept, got = pick(part, place, 0), grid.over_x(pick(part, 1 - place, 0))
        first = jnp.where(place == 0, kept, got)
        second = jnp.where(place == 0, got, kept)
        return jnp.concatenate([first, second])[None]
    if count % group == 0:
        return lax.all_to_all(part, SEQ, split_axis=0, concat_axis=1, tiled=True)
    every = lax.all_gather(part, SEQ, axis=1, tiled=True)
    return pick(every, place % count, 0)[None]


def from_whole(grid, whole, count):
    group = grid.group
    if group == 1:
        return whole
    place = lax.axis_index(SEQ)
    if group == 2 and count == 2:
        halves = whole.reshape(2, -1, whole.shape[-1])
        kept, got = pick(halves, place, 0), grid.over_x(pick(halves, 1 - place, 0))
        first = jnp.where(place == 0, kept, got)
        second = jnp.where(place == 0, got, kept)
        return jnp.stack([first, second])
    if count % group == 0:
        return lax.all_to_all(whole, SEQ, split_axis=1, concat_axis=0, tiled=True)
    every = lax.all_gather(whole[0], SEQ, axis=0)[:count]
    rows = whole.shape[1] // group
    return lax.dynamic_slice_in_dim(every, place * rows, rows, 1)


def attention_forward_kernel(q_ref, k_ref, v_ref, mask_ref, out_ref, total_ref, *, head, chunk):
    factor = head**-0.5 * math.log2(math.e)
    rows = q_ref.shape[1]
    for h in range(q_ref.shape[2] // head):
        lanes = slice(h * head, (h + 1) * head)
        keys, values = k_ref[0, :, lanes], v_ref[0, :, lanes]
        for start in range(0, rows, chunk):
            part = slice(start, start + chunk)
            scores = dot(keys, q_ref[0, part, lanes], NT)
            weights = jnp.exp2(scores * factor + mask_ref[0, :, part])
            total = jnp.sum(weights, axis=0, keepdims=True)
            summed = dot(values, weights.astype(BF), TN)
            total_ref[0, 0, h : h + 1, part] = total
            out_ref[0, part, lanes] = (summed / total).T.astype(BF)


def attention_backward_kernel(
    q_ref, k_ref, v_ref, mask_ref, grad_ref, ctx_ref, total_ref, out_ref, dk_sum, dv_sum, *, head, chunk
):
    scale = head**-0.5
    factor = scale * math.log2(math.e)
    rows = q_ref.shape[1]
    for h in range(q_ref.shape[2] // head):
        lanes = slice(h * head, (h + 1) * head)
        keys, values = k_ref[0, :, lanes], v_ref[0, :, lanes]
        keys_t = keys.T
        for start in range(0, rows, chunk):
            part = slice(start, start + chunk)
            queries = q_ref[0, part, lanes]
            scores = dot(keys, queries, NT)
            weights = jnp.exp2(scores * factor + mask_ref[0, :, part])
            inverse = 1.0 / total_ref[0, 0, h : h + 1, part]
            grad = grad_ref[0, part, lanes].astype(F32)
            product = (grad * ctx_ref[0, part, lanes].astype(F32)).T
            grad_total = -jnp.sum(product, axis=0, keepdims=True) * inverse
            grad_summed = (grad.T * inverse).astype(BF)
            grad_probs = dot(values, grad_summed)
            grad_scores = (weights * (grad_probs + grad_total)).astype(BF)
            dv_part = dot(weights.astype(BF), grad_summed, NT)
            dk_part = dot(grad_scores, queries)
            if start == 0:
                dv_sum[...] = dv_part
                dk_sum[...] = dk_part
            else:
                dv_sum[...] += dv_part
                dk_sum[...] += dk_part
            out_ref[0, 0, part, lanes] = (dot(keys_t, grad_scores).T * scale).astype(BF)
        out_ref[1, 0, :, lanes] = (dk_sum[...] * scale).astype(BF)
        out_ref[2, 0, :, lanes] = dv_sum[...].astype(BF)


def attention_specs(length, width, group):
    head = width // HEADS
    lanes = max(128, head)
    steps = width // lanes // GROUPS

    def columns(which):
        return pl.BlockSpec((1, length, lanes), lambda b, p: (b, 0, (which * GROUPS + group) * steps + p))

    own = pl.BlockSpec((1, length, lanes), lambda b, p: (b, 0, p))
    mask = pl.BlockSpec((1, length, length), lambda b, p: (b, 0, 0))
    totals = pl.BlockSpec((1, 1, lanes // head, length), lambda b, p: (b, p, 0, 0))
    return head, lanes, steps, columns, own, mask, totals


def attention_forward(qkv, mask, group):
    count, length, width = qkv.shape
    width = width // 3
    head, lanes, steps, columns, own, mask_spec, totals = attention_specs(length, width, group)
    return pl.pallas_call(
        partial(attention_forward_kernel, head=head, chunk=512),
        grid=(count, steps),
        in_specs=[columns(0), columns(1), columns(2), mask_spec],
        out_specs=[own, totals],
        out_shape=[
            jax.ShapeDtypeStruct((count, length, width // GROUPS), BF),
            jax.ShapeDtypeStruct((count, steps, lanes // head, length), F32),
        ],
        compiler_params=pltpu.CompilerParams(vmem_limit_bytes=VMEM_BYTES),
        cost_estimate=pl.CostEstimate(
            flops=12 * count * length * length * width // GROUPS, bytes_accessed=12 * 2**20, transcendentals=0
        ),
    )(qkv, qkv, qkv, mask)


def attention_backward(qkv, mask, grad, context, totals_in, group):
    count, length, width = grad.shape
    head, lanes, steps, columns, own, mask_spec, totals = attention_specs(length, width, group)
    grads = pl.BlockSpec((3, 1, length, lanes), lambda b, p: (0, b, 0, p))
    return pl.pallas_call(
        partial(attention_backward_kernel, head=head, chunk=256),
        grid=(count, steps),
        in_specs=[columns(0), columns(1), columns(2), mask_spec, columns(0), own, totals],
        out_specs=grads,
        out_shape=jax.ShapeDtypeStruct((3, count, length, width // GROUPS), BF),
        scratch_shapes=[pltpu.VMEM((length, head), F32)] * 2,
        compiler_params=pltpu.CompilerParams(vmem_limit_bytes=VMEM_BYTES),
        cost_estimate=pl.CostEstimate(
            flops=26 * count * length * length * width // GROUPS, bytes_accessed=20 * 2**20, transcendentals=0
        ),
    )(qkv, qkv, qkv, mask, grad, context, totals_in)


def attention_mask(segments, globals_pair, randoms):
    count, blocks = randoms.shape[:2]
    length = segments.shape[1]
    numbers = jnp.arange(blocks, dtype=jnp.int32)
    chosen = jnp.any(globals_pair[:, :, None] == numbers, axis=1)
    nearby = jnp.abs(numbers[:, None] - numbers[None, :]) <= 1
    picked = jnp.any(randoms[:, :, :, None] == numbers, axis=2)
    seen = chosen[:, :, None] | chosen[:, None, :] | nearby[None] | picked
    seen = jnp.swapaxes(seen, 1, 2)[:, :, None, :, None]
    seen = jnp.broadcast_to(seen, (count, blocks, BLK, blocks, BLK)).reshape(count, length, length)
    same = segments[:, :, None] == segments[:, None, :]
    return jnp.where(seen & same, 0.0, MASKED).astype(F32)


def normalise(values):
    centred = values - jnp.mean(values, -1, keepdims=True)
    inverse = lax.rsqrt(jnp.mean(centred * centred, -1, keepdims=True) + EPSILON)
    return centred * inverse, inverse


def normalise_back(grad, values, gain):
    unit, inverse = normalise(values)
    inner = grad * gain
    grad_in = inverse * (
        inner - jnp.mean(inner, -1, keepdims=True) - unit * jnp.mean(inner * unit, -1, keepdims=True)
    )
    return grad_in, jnp.sum(grad * unit, 0, keepdims=True), jnp.sum(grad, 0, keepdims=True)


def accumulate(ref, rows):
    first = pl.program_id(0) == 0
    for j, row in enumerate(rows):

        @pl.when(first)
        def _():
            ref[j : j + 1] = row

        @pl.when(jnp.logical_not(first))
        def _():
            ref[j : j + 1] += row


def row_block(i):
    return (i, 0)


def fixed_block(i):
    return (0, 0)


def column_block(i):
    return (0, i)


def project_in(x, w_qkv, extra):
    rows, width = x.shape

    def kernel(_, ins, outs, weights, scratch):
        qkv, turned, params = outs
        w, small = weights

        @pl.when(pl.program_id(0) == 0)
        def _():
            params[...] = small[...].astype(F32).T[:16]

        unit, _ = normalise(ins[0][...].astype(F32))
        normed = (unit * params[0:1] + params[1:2]).astype(BF)
        turned[...] = normed.T
        for part, bias in enumerate((params[2:3], None, params[3:4])):
            columns = slice(part * width, (part + 1) * width)
            value = dot(normed, w[:, columns])
            qkv[:, columns] = (value if bias is None else value + bias).astype(BF)

    return run(
        kernel,
        [w_qkv, extra],
        [(x, (TILE, width), row_block)],
        [
            ((rows, 3 * width), BF, (TILE, 3 * width), row_block),
            ((width, rows), BF, (width, TILE), column_block),
            ((16, width), F32, (16, width), fixed_block),
        ],
        rows // TILE,
        6 * rows * width * width,
    )


def project_out(contexts, x, params, w_o):
    rows, width = x.shape

    def kernel(_, ins, outs, weights, scratch):
        x_ref, params = ins[:2]
        residual, normed, turned, context_turned = outs
        parts = [ref[...] for ref in ins[2:]]
        context = jnp.concatenate(parts, axis=1)
        context_turned[...] = context.T
        value = x_ref[...].astype(F32) + dot(context, weights[0][...]) + params[4:5]
        residual[...] = value
        unit, _ = normalise(value)
        low = (unit * params[5:6] + params[6:7]).astype(BF)
        normed[...] = low
        turned[...] = low.T

    return run(
        kernel,
        [w_o],
        [(x, (TILE, width), row_block), (params, (16, width), fixed_block)]
        + [(c, (TILE, c.shape[1]), row_block) for c in contexts],
        [
            ((rows, width), F32, (TILE, width), row_block),
            ((rows, width), BF, (TILE, width), row_block),
            ((width, rows), BF, (width, TILE), column_block),
            ((width, rows), BF, (width, TILE), column_block),
        ],
        rows // TILE,
        2 * rows * width * width,
    )


def feed_up(normed, w_up, bias):
    rows, width = normed.shape
    wide = w_up.shape[1]
    outer = math.sqrt(2 / math.pi)
    cubic = 0.044715

    def kernel(_, ins, outs, weights, scratch):
        value, slope = outs
        for start in range(0, wide, width):
            columns = slice(start, start + width)
            u = dot(ins[0][...], weights[0][:, columns]) + ins[1][:, columns]
            square = u * u
            half = 0.5 + 0.5 * jnp.tanh(u * (outer + outer * cubic * square))
            gelu = u * half
            value[:, columns] = gelu.astype(BF)
            rest = gelu * (1.0 - half) * (2 * outer + 6 * outer * cubic * square)
            slope[:, columns] = (half + rest).astype(BF)

    return run(
        kernel,
        [w_up],
        [(normed, (TILE, width), row_block), (bias, (1, wide), fixed_block)],
        [((rows, wide), BF, (TILE, wide), row_block)] * 2,
        rows // TILE,
        2 * rows * width * wide,
    )


def feed_down(activated, slope, residual, upstream, params, w_down):
    rows, wide = activated.shape
    width = residual.shape[1]

    def kernel(_, ins, outs, weights, scratch):
        act, slope, residual, upstream, params = ins
        mixed, grad_hidden, sum_up, sum_down = outs
        w = weights[0]
        value = residual[...] + dot(act[...], w[...]) + params[7:8]
        mixed[...] = value.astype(BF)
        dy = upstream[...]
        sums = []
        for start in range(0, wide, width):
            columns = slice(start, start + width)
            grad = dot(dy, w[columns, :], NT).astype(BF).astype(F32)
            low = (grad * slope[:, columns].astype(F32)).astype(BF)
            grad_hidden[:, columns] = low
            sums.append(jnp.sum(low.astype(F32), 0, keepdims=True))
        accumulate(sum_up, [jnp.concatenate(sums, axis=1)])
        accumulate(sum_down, [jnp.sum(dy.astype(F32), 0, keepdims=True)])

    return run(
        kernel,
        [w_down],
        [
            (activated, (TILE, wide), row_block),
            (slope, (TILE, wide), row_block),
            (residual, (TILE, width), row_block),
            (upstream, (TILE, width), row_block),
            (params, (16, width), fixed_block),
        ],
        [
            ((rows, width), BF, (TILE, width), row_block),
            ((rows, wide), BF, (TILE, wide), row_block),
            ((8, wide), F32, (8, wide), fixed_block),
            ((8, width), F32, (8, width), fixed_block),
        ],
        rows // TILE,
        4 * rows * width * wide,
    )


def feed_back(grad_hidden, residual, upstream, params, w_up, w_o):
    rows, width = residual.shape
    wide = grad_hidden.shape[1]

    def kernel(_, ins, outs, weights, scratch):
        du, residual, upstream, params = ins
        grad_residual, grad_att, grad_context, sums = outs
        grad = dot(du[...], weights[0][...], NT)
        part, gain, shift = normalise_back(grad, residual[...], params[5:6])
        total = upstream[...].astype(F32) + part
        grad_residual[...] = total
        low = total.astype(BF)
        grad_att[...] = low
        grad_context[...] = dot(low, weights[1][...], NT).astype(BF)
        accumulate(sums, [jnp.sum(low.astype(F32), 0, keepdims=True), gain, shift])

    return run(
        kernel,
        [w_up, w_o],
        [
            (grad_hidden, (TILE, wide), row_block),
            (residual, (TILE, width), row_block),
            (upstream, (TILE, width), row_block),
            (params, (16, width), fixed_block),
        ],
        [
            ((rows, width), F32, (TILE, width), row_block),
            ((rows, width), BF, (TILE, width), row_block),
            ((rows, width), BF, (TILE, width), row_block),
            ((8, width), F32, (8, width), fixed_block),
        ],
        rows // TILE,
        2 * rows * width * (wide + width),
    )


def project_back(grads, grad_residual, x, params, w_qkv):
    rows, width = x.shape
    each = width // GROUPS

    def kernel(_, ins, outs, weights, scratch):
        grad_residual, x_ref, params = ins[:3]
        grad_in, sums = outs
        w = weights[0]
        grad = None
        biases = []
        for part in range(3):
            cut = [ref[part] for ref in ins[3:]]
            low = jnp.concatenate(cut, axis=1)
            if part != 1:
                biases.append(jnp.sum(low.astype(F32), 0, keepdims=True))
            value = dot(low, w[:, part * width : (part + 1) * width], NT)
            grad = value if grad is None else grad + value
        part, gain, shift = normalise_back(grad, x_ref[...].astype(F32), params[0:1])
        grad_in[...] = (grad_residual[...] + part).astype(BF)
        accumulate(sums, [gain, shift] + biases)

    return run(
        kernel,
        [w_qkv],
        [
            (grad_residual, (TILE, width), row_block),
            (x, (TILE, width), row_block),
            (params, (16, width), fixed_block),
        ]
        + [(g, (3, TILE, each), lambda i: (0, i, 0)) for g in grads],
        [
            ((rows, width), BF, (TILE, width), row_block),
            ((8, width), F32, (8, width), fixed_block),
        ],
        rows // TILE,
        6 * rows * width * width,
    )


def weight_grad(grid, turned, right):
    features, rows = turned.shape
    parts, _, columns = right.shape
    tile = min(512, columns)
    per = columns // tile
    pair = features // grid.nz // 4

    def kernel(scalars, ins, outs, weights, scratch):
        kept, sent = outs
        first = scalars[0] == 0
        value = dot(ins[0][...], ins[1][0]).astype(BF)
        for j in range(grid.nz * 2):
            low = value[2 * j * pair : (2 * j + 1) * pair]
            high = value[(2 * j + 1) * pair : (2 * j + 2) * pair]
            kept[j * pair : (j + 1) * pair] = jnp.where(first, low, high)
            sent[j * pair : (j + 1) * pair] = jnp.where(first, high, low)

    kept, sent = run(
        kernel,
        [],
        [
            (turned, (features, rows), fixed_block),
            (right, (1, rows, tile), lambda i: (i // per, 0, i % per)),
        ],
        [((features // 2, parts * columns), BF, (features // 2, tile), column_block)] * 2,
        parts * per,
        2 * rows * features * parts * columns,
        scalars=[grid.core],
    )
    shape = (grid.nz, 2, 2, pair // 2, parts * columns)
    return kept.reshape(shape), sent.reshape(shape)


def weight_grad_turned(turned, right, devices):
    features, rows = turned.shape
    columns = right.shape[1]
    each = columns // devices
    tile = min(512, columns)

    def kernel(_, ins, outs, weights, scratch):
        value = dot(ins[0][...], ins[1][...]).astype(BF)
        for j in range(tile // each):
            outs[0][j] = value[:, j * each : (j + 1) * each]

    return run(
        kernel,
        [],
        [(turned, (features, rows), fixed_block), (right, (rows, tile), column_block)],
        [((devices, features, each), BF, (tile // each, features, each), lambda i: (i, 0, 0))],
        columns // tile,
        2 * rows * features * columns,
    )[0]


def shards(tokens, cotangent, segments, global_blocks, random_blocks, *params):
    grid = Grid()
    gain1, shift1, w_q, b_q, w_k, w_v, b_v, w_o, b_o, gain2, shift2, w_up, b_up, w_down, b_down = params
    count = tokens.shape[0]
    width = tokens.shape[-1]
    each = w_v.shape[0]
    devices = grid.dp * grid.group
    replicas = max(1, grid.group // count)

    inputs = to_whole(grid, tokens)
    n, length = inputs.shape[:2]
    rows = n * length
    inputs = inputs.reshape(rows, width)
    vectors = [gain1, shift1, b_q, b_v, b_o, gain2, shift2, b_down]
    extra = jnp.concatenate([jnp.stack(vectors, axis=1), b_up.reshape(each, -1)], axis=1)
    extra = jnp.pad(extra, ((0, 0), (0, 128 - extra.shape[1])))
    pieces_qk = gather_pieces(grid, jnp.concatenate([w_q, w_k], axis=1), True)
    pieces_v = gather_pieces(grid, jnp.concatenate([w_v, extra], axis=1), False)
    w_qkv = weight_of([(pieces_qk, 0, 2 * width, 0), (pieces_v, 0, width, 2 * width)], 3 * width)
    extra = weight_of([(pieces_v, width, 128, 0)], 128)
    w_o = weight_of([(gather_pieces(grid, w_o, False), 0, width, 0)], width)
    w_up = whole_weight(lax.all_gather(w_up, BOTH, axis=0, tiled=True))
    w_down = whole_weight(lax.all_gather(w_down, BOTH, axis=0, tiled=True))
    upstream = to_whole(grid, cotangent).reshape(rows, width)
    upstream_turned = upstream.T

    if grid.group > 1:
        place = lax.axis_index(SEQ)
        first = place * n if count % grid.group == 0 else place % count
        segments, global_blocks, random_blocks = (
            lax.dynamic_slice_in_dim(a, first, n, 0) for a in (segments, global_blocks, random_blocks)
        )
    mask = attention_mask(segments, global_blocks, random_blocks)

    qkv, normed1_turned, params = project_in(inputs, w_qkv, extra)
    qkv = qkv.reshape(n, length, 3 * width)
    attended = [attention_forward(qkv, mask, g) for g in range(GROUPS)]
    contexts = [a[0].reshape(rows, -1) for a in attended]
    residual, normed2, normed2_turned, context_turned = project_out(contexts, inputs, params, w_o)
    bias_up = params[8:12].T.reshape(1, -1)
    activated, slope = feed_up(normed2, w_up, bias_up)

    grad_w_down = weight_grad_turned(upstream_turned, activated, devices)
    mixed, grad_hidden, sum_up, sum_down = feed_down(activated, slope, residual, upstream, params, w_down)
    mixed = from_whole(grid, mixed.reshape(n, length, width), count)
    terms_up = weight_grad_of(grid, normed2_turned, grad_hidden[None])
    grad_residual, grad_att, grad_context, sums2 = feed_back(
        grad_hidden, residual, upstream, params, w_up, w_o
    )
    terms_o = weight_grad_of(grid, context_turned, grad_att[None])
    grad_context = grad_context.reshape(n, length, width)
    grads, terms_qkv = [], []
    for g in range(GROUPS):
        grad = attention_backward(qkv, mask, grad_context, *attended[g], g)
        grads.append(grad.reshape(3, rows, -1))
        terms_qkv.append(weight_grad_of(grid, normed1_turned, grads[g]))
    grad_inputs, sums1 = project_back(grads, grad_residual, inputs, params, w_qkv)
    grad_inputs = from_whole(grid, grad_inputs.reshape(n, length, width), count)

    share = 1.0 / replicas
    grad_w_down = lax.psum_scatter(grad_w_down * BF(share), BOTH, scatter_dimension=0, tiled=True)
    grad_w_down = grad_w_down[0].T.astype(F32)
    grad_w_up = sum_up_devices(grid, terms_up, False) * share
    grad_w_o = sum_up_devices(grid, terms_o, True) * share
    ended = [sum_up_devices(grid, t, False) * share for t in terms_qkv]
    cut = width // GROUPS
    grad_w_q, grad_w_k, grad_w_v = (
        jnp.concatenate([e[:, j * cut : (j + 1) * cut] for e in ended], axis=1) for j in range(3)
    )
    vectors = jnp.concatenate([sums1[:4], sums2[:3], sum_down[:1]])
    vectors = vectors.reshape(8, devices, each).transpose(1, 0, 2).reshape(devices, -1)
    vectors = jnp.concatenate([vectors, sum_up[:1].reshape(devices, -1)], axis=1)
    if grid.cube:
        vectors = vectors.reshape(grid.nz, 2, 2, 2, -1, 128)
        vectors = scatter_sum(grid, pick(vectors, grid.core, 2), pick(vectors, 1 - grid.core, 2), False)
    else:
        vectors = lax.psum_scatter(vectors, BOTH, scatter_dimension=0, tiled=True) * share
    vectors = vectors.reshape(-1)
    grad_b_up = vectors[8 * each :]
    grad_gain1, grad_shift1, grad_b_q, grad_b_v, grad_b_o, grad_gain2, grad_shift2, grad_b_down = (
        vectors[j * each : (j + 1) * each] for j in range(8)
    )
    return (
        mixed, grad_inputs, grad_gain1, grad_shift1, grad_w_q, grad_b_q, grad_w_k, grad_w_v, grad_b_v,
        grad_w_o, grad_b_o, grad_gain2, grad_shift2, grad_w_up, grad_b_up, grad_w_down, grad_b_down,
    )


def weight_grad_of(grid, turned, right):
    if grid.cube:
        return weight_grad(grid, turned, right)
    return [dot(turned, part) for part in right]


def sum_up_devices(grid, terms, z_first):
    if grid.cube:
        return scatter_sum(grid, *terms, z_first)
    whole = jnp.concatenate(terms, axis=1)
    return lax.psum_scatter(whole, BOTH, scatter_dimension=0, tiled=True)


def solution(mesh):
    rows = P(DP, SEQ, None)
    vector, matrix = P(BOTH), P(BOTH, None)
    params = (
        vector, vector, matrix, vector, matrix, matrix, vector, matrix, vector, vector, vector, matrix,
        vector, matrix, vector,
    )
    in_specs = (rows, rows, P(DP, None), P(DP, None), P(DP, None, None)) + params
    out_specs = (rows, rows) + params
    return jax.shard_map(shards, mesh=mesh, in_specs=in_specs, out_specs=out_specs, check_vma=False)
```

profile of v0, /device:TPU:0, one launch (start us, length us, event | category | flops | bytes accessed | tf_op | source)
XLA Modules:
  0.0 646.5 jit_solution(15782552274673637229)
XLA Ops:
  51.9 6.5 %collective-permute-done.3.refs_2_.refs_3_ = bf16[4,32,1024]{2,1,0:T(8,128)(2,1)S(1)} collective-permute-done((bf16[4,32,1024]{2,1,0:T(8,128)(2,1)S(1)}, bf16[4,32,1024]{2,1,0:T(8,128)(2,1)S(1)}, u32[]{:S(2)}, u32[]{:S(2)}) %collective-permute-start.3) | collective-permute-done | bytes 262176 | tf_op jit(solution)/shard_map/ppermute | solution.py:51
  61.0 11.4 %collective-permute-done.5.refs_4_.refs_5_ = bf16[4,32,1024]{2,1,0:T(8,128)(2,1)S(1)} collective-permute-done((bf16[4,32,1024]{2,1,0:T(8,128)(2,1)S(1)}, bf16[4,32,1024]{2,1,0:T(8,128)(2,1)S(1)}, u32[]{:S(2)}, u32[]{:S(2)}) %collective-permute-start.5) | collective-permute-done | bytes 262176 | tf_op jit(solution)/shard_map/ppermute | solution.py:51
  85.6 6.1 collective-permute-done.23.refs_10_.refs_18_
  91.6 6.6 %collective-permute-start.25 = (bf16[4,32,1152]{2,1,0:T(8,128)(2,1)}, bf16[4,32,1152]{2,1,0:T(8,128)(2,1)}, u32[]{:S(2)}, u32[]{:S(2)}) collective-permute-start(bf16[4,32,1152]{2,1,0:T(8,128)(2,1)} %pad_maximum_fusion.5.refs_8_.refs_16_), channel_id=1, source_target_pairs={{0,16},{2,18},{4,20},{6,22},{8,24},{10,26},{12,28},{14,30},{16,0},... | collective-permute-start | bytes 884744 | tf_op jit(solution)/shard_map/ppermute | solution.py:51
  98.3 22.5 %collective-permute-done.14.refs_2_ = bf16[4,32,2048]{2,1,0:T(8,128)(2,1)} collective-permute-done((bf16[4,32,2048]{2,1,0:T(8,128)(2,1)}, bf16[4,32,2048]{2,1,0:T(8,128)(2,1)}, u32[]{:S(2)}, u32[]{:S(2)}) %collective-permute-start.14) | collective-permute-done | bytes 524320 | tf_op jit(solution)/shard_map/ppermute | solution.py:42
  148.5 15.2 %shard_map.323 = (bf16[1024,3072]{1,0:T(8,128)(2,1)}, bf16[1024,1024]{1,0:T(8,128)(2,1)}, f32[16,1024]{1,0:T(8,128)}) custom-call(s32[96]{0:T(128)} %stack.160.at, bf16[4,32,2048]{2,1,0:T(8,128)(2,1)} %pad_maximum_fusion.4.refs_0_, bf16[4,32,2048]{2,1,0:T(8,128)(2,1)} %copy-done.22, bf16[4,32,2048]{2,1,0:T(8,128)(2,1)} %collective-permute-done.14.refs_2_, ...), custom_call_target="tpu_custom_call" | custom-call | flops 6442450944 | bytes 17104896 | tf_op jit(solution)/shard_map/pallas_call | solution.py:166
  163.7 13.3 %shard_map.324 = (bf16[1,1024,512]{2,1,0:T(8,128)(2,1)}, f32[1,4,2,1024]{3,2,1,0:T(2,128)}) custom-call(bf16[1,1024,3072]{2,1,0:T(8,128)(2,1)} %bitcast.337, bf16[1,1024,3072]{2,1,0:T(8,128)(2,1)} %bitcast.338, bf16[1,1024,3072]{2,1,0:T(8,128)(2,1)} %bitcast.339, f32[1,1024,1024]{2,1,0:T(8,128)} %and_select_fusion.mask_ref), custom_call_target="tpu_custom_call" | custom-call | flops 6442450944 | bytes 12582912 | tf_op jit(solution)/shard_map/pallas_call | solution.py:319
  177.0 13.3 %shard_map.325 = (bf16[1,1024,512]{2,1,0:T(8,128)(2,1)}, f32[1,4,2,1024]{3,2,1,0:T(2,128)}) custom-call(bf16[1,1024,3072]{2,1,0:T(8,128)(2,1)} %bitcast.340, bf16[1,1024,3072]{2,1,0:T(8,128)(2,1)} %bitcast.341, bf16[1,1024,3072]{2,1,0:T(8,128)(2,1)} %bitcast.342, f32[1,1024,1024]{2,1,0:T(8,128)} %and_select_fusion.mask_ref), custom_call_target="tpu_custom_call" | custom-call | flops 6442450944 | bytes 12582912 | tf_op jit(solution)/shard_map/pallas_call | solution.py:319
  193.2 10.6 %shard_map.326 = (f32[1024,1024]{1,0:T(8,128)}, bf16[1024,1024]{1,0:T(8,128)(2,1)}, bf16[1024,1024]{1,0:T(8,128)(2,1)}, bf16[1024,1024]{1,0:T(8,128)(2,1)}) custom-call(s32[32]{0:T(128)} %stack.156.at, bf16[4,32,1024]{2,1,0:T(8,128)(2,1)} %copy-done.16, bf16[4,32,1024]{2,1,0:T(8,128)(2,1)} %copy-done.32, bf16[4,32,1024]{2,1,0:T(8,128)(2,1)} %copy-done.26, ...), custom_call_target="tpu_custom_call" | custom-call | flops 2147483648 | bytes 16842752 | tf_op jit(solution)/shard_map/pallas_call | solution.py:166
  203.9 23.6 %shard_map.327 = (bf16[1024,4096]{1,0:T(8,128)(2,1)}, bf16[1024,4096]{1,0:T(8,128)(2,1)}) custom-call(s32[1]{0:T(128)} %constant.576.clone.1.at, bf16[1024,4096]{1,0:T(8,128)(2,1)} %all-gather.5.cloned.1.call-done.refs_0_, bf16[1024,1024]{1,0:T(8,128)(2,1)} %get-tuple-element.52.refs_1_, f32[1,4096]{1,0:T(1,128)} %reshape.504.refs_2_), custom_call_target="tpu_custom_call" | custom-call | flops 8589934592 | bytes 27279360 | tf_op jit(solution)/shard_map/pallas_call | solution.py:166
  227.5 14.2 %shard_map.337 = bf16[32,1024,128]{2,1,0:T(8,128)(2,1)} custom-call(s32[1]{0:T(128)} %constant.576.clone.1.at, bf16[1024,1024]{1,0:T(8,128)(2,1)} %get-tuple-element.170.refs_0_, bf16[1024,4096]{1,0:T(8,128)(2,1)} %get-tuple-element.53.refs_1_), custom_call_target="tpu_custom_call" | custom-call | flops 8589934592 | bytes 18874368 | tf_op jit(solution)/shard_map/pallas_call | solution.py:166
  241.7 29.5 %shard_map.328 = (bf16[1024,1024]{1,0:T(8,128)(2,1)}, bf16[1024,4096]{1,0:T(8,128)(2,1)}, f32[8,4096]{1,0:T(8,128)}, f32[8,1024]{1,0:T(8,128)}) custom-call(s32[1]{0:T(128)} %constant.576.clone.1.at, bf16[4096,1024]{1,0:T(8,128)(2,1)} %all-gather.3.cloned.1.call-done.refs_0_, bf16[1024,4096]{1,0:T(8,128)(2,1)} %get-tuple-element.53.refs_1_, ...), custom_call_target="tpu_custom_call" | custom-call | flops 17179869184 | bytes 42172416 | tf_op jit(solution)/shard_map/pallas_call | solution.py:166
  271.2 23.4 %shard_map.329 = (f32[1024,1024]{1,0:T(8,128)}, bf16[1024,1024]{1,0:T(8,128)(2,1)}, bf16[1024,1024]{1,0:T(8,128)(2,1)}, f32[8,1024]{1,0:T(8,128)}) custom-call(s32[33]{0:T(128)} %stack.181.at, bf16[1024,4096]{1,0:T(8,128)(2,1)} %all-gather.5.cloned.1.call-done.refs_0_, bf16[4,32,1024]{2,1,0:T(8,128)(2,1)} %copy-done.16, bf16[4,32,1024]{2,1,0:T(8,128)(2,1)} %copy-done.32, ...), custom_call_target="tpu_custom_call" | custom-call | flops 10737418240 | bytes 33652736 | tf_op jit(solution)/shard_map/pallas_call | solution.py:166
  294.7 27.2 %shard_map.330 = bf16[3,1,1024,512]{3,2,1,0:T(8,128)(2,1)} custom-call(bf16[1,1024,3072]{2,1,0:T(8,128)(2,1)} %bitcast.343, bf16[1,1024,3072]{2,1,0:T(8,128)(2,1)} %bitcast.344, bf16[1,1024,3072]{2,1,0:T(8,128)(2,1)} %bitcast.345, f32[1,1024,1024]{2,1,0:T(8,128)} %and_select_fusion.mask_ref, bf16[1,1024,1024]{2,1,0:T(8,128)(2,1)} %bitcast.354, ...), custom_call_target="tpu_custom_call" | custom-call | flops 13958643712 | bytes 20971520 | tf_op jit(solution)/shard_map/pallas_call | solution.py:339
  321.9 27.3 %shard_map.331 = bf16[3,1,1024,512]{3,2,1,0:T(8,128)(2,1)} custom-call(bf16[1,1024,3072]{2,1,0:T(8,128)(2,1)} %bitcast.346, bf16[1,1024,3072]{2,1,0:T(8,128)(2,1)} %bitcast.347, bf16[1,1024,3072]{2,1,0:T(8,128)(2,1)} %bitcast.348, f32[1,1024,1024]{2,1,0:T(8,128)} %and_select_fusion.mask_ref, bf16[1,1024,1024]{2,1,0:T(8,128)(2,1)} %bitcast.355, ...), custom_call_target="tpu_custom_call" | custom-call | flops 13958643712 | bytes 20971520 | tf_op jit(solution)/shard_map/pallas_call | solution.py:339
  349.2 16.3 %shard_map.332 = (bf16[1024,1024]{1,0:T(8,128)(2,1)}, f32[8,1024]{1,0:T(8,128)}) custom-call(s32[64]{0:T(128)} %stack.180.at, bf16[4,32,2048]{2,1,0:T(8,128)(2,1)} %pad_maximum_fusion.4.refs_0_, bf16[4,32,2048]{2,1,0:T(8,128)(2,1)} %copy-done.22, bf16[4,32,2048]{2,1,0:T(8,128)(2,1)} %collective-permute-done.14.refs_2_, ...), custom_call_target="tpu_custom_call" | custom-call | flops 6442450944 | bytes 21069824 | tf_op jit(solution)/shard_map/pallas_call | solution.py:166
  374.8 14.4 %shard_map.336 = (bf16[512,4096]{1,0:T(8,128)(2,1)}, bf16[512,4096]{1,0:T(8,128)(2,1)}) custom-call(s32[1]{0:T(128)} %bitcast.90.at, bf16[1024,1024]{1,0:T(8,128)(2,1)} %get-tuple-element.76.refs_0_, bf16[1,1024,4096]{2,1,0:T(8,128)(2,1)} %bitcast.336), custom_call_target="tpu_custom_call" | custom-call | flops 8589934592 | bytes 18874368 | tf_op jit(solution)/shard_map/pallas_call | solution.py:166
  394.2 7.1 %shard_map.334 = (bf16[512,1536]{1,0:T(8,128)(2,1)}, bf16[512,1536]{1,0:T(8,128)(2,1)}) custom-call(s32[1]{0:T(128)} %bitcast.90.at, bf16[1024,1024]{1,0:T(8,128)(2,1)} %get-tuple-element.67.refs_0_, bf16[3,1024,512]{2,1,0:T(8,128)(2,1)} %bitcast.352), custom_call_target="tpu_custom_call" | custom-call | flops 3221225472 | bytes 8388608 | tf_op jit(solution)/shard_map/pallas_call | solution.py:166
  401.3 7.4 %shard_map.333 = (bf16[512,1536]{1,0:T(8,128)(2,1)}, bf16[512,1536]{1,0:T(8,128)(2,1)}) custom-call(s32[1]{0:T(128)} %bitcast.90.at, bf16[1024,1024]{1,0:T(8,128)(2,1)} %get-tuple-element.67.refs_0_, bf16[3,1024,512]{2,1,0:T(8,128)(2,1)} %bitcast.350), custom_call_target="tpu_custom_call" | custom-call | flops 3221225472 | bytes 8388608 | tf_op jit(solution)/shard_map/pallas_call | solution.py:166
  456.6 14.6 %collective-permute-done.31 = bf16[512,1024]{0,1:T(8,128)(2,1)S(1)} collective-permute-done((bf16[512,1024]{0,1:T(8,128)(2,1)}, bf16[512,1024]{0,1:T(8,128)(2,1)S(1)}, u32[]{:S(2)}, u32[]{:S(2)}) %collective-permute-start.31) | collective-permute-done | bytes 1048608 | tf_op jit(solution)/shard_map/ppermute | solution.py:42
  497.7 67.2 %collective-permute-done.54 = bf16[2,32,1024]{2,1,0:T(8,128)(2,1)S(1)} collective-permute-done((bf16[2,32,1024]{2,1,0:T(8,128)(2,1)S(1)}, bf16[2,32,1024]{2,1,0:T(8,128)(2,1)S(1)}, u32[]{:S(2)}, u32[]{:S(2)}) %collective-permute-start.54) | collective-permute-done | bytes 131104 | tf_op jit(solution)/shard_map/ppermute | solution.py:45
  572.7 7.8 %collective-permute-done.46 = bf16[4,32,1536]{2,1,0:T(8,128)(2,1)S(1)} collective-permute-done((bf16[4,32,1536]{2,1,0:T(8,128)(2,1)S(1)}, bf16[4,32,1536]{2,1,0:T(8,128)(2,1)S(1)}, u32[]{:S(2)}, u32[]{:S(2)}) %collective-permute-start.46) | collective-permute-done | bytes 393248 | tf_op jit(solution)/shard_map/ppermute | solution.py:42
  597.8 16.0 %collective-permute-done.58 = bf16[4,32,4096]{2,1,0:T(8,128)(2,1)S(1)} collective-permute-done((bf16[4,32,4096]{2,1,0:T(8,128)(2,1)S(1)}, bf16[4,32,4096]{2,1,0:T(8,128)(2,1)S(1)}, u32[]{:S(2)}, u32[]{:S(2)}) %collective-permute-start.58) | collective-permute-done | bytes 1048608 | tf_op jit(solution)/shard_map/ppermute | solution.py:42
  624.0 12.7 %collective-permute-done.60 = bf16[32,4096]{1,0:T(8,128)(2,1)S(1)} collective-permute-done((bf16[32,4096]{1,0:T(8,128)(2,1)S(1)}, bf16[32,4096]{1,0:T(8,128)(2,1)S(1)}, u32[]{:S(2)}, u32[]{:S(2)}) %collective-permute-start.60) | collective-permute-done | bytes 262176 | tf_op jit(solution)/shard_map/ppermute | solution.py:51
  (312 shorter events, 217.4 us)
Async XLA Ops:
  7.2 196.7 %all-gather.5.cloned.1.call-start = ((), (), s32[]{:S(2)}) async-start(), calls=%async_computation.2 | async-start | bytes 8650752 | tf_op jit(solution)/shard_map/all_gather | solution.py:692
  7.9 233.8 %all-gather.3.cloned.1.call-start = ((), (), s32[]{:S(2)}) async-start(), calls=%async_computation.1 | async-start | bytes 8650752 | tf_op jit(solution)/shard_map/all_gather | solution.py:693
  8.7 629.0 %reduce-scatter.2.cloned.1.call-start = ((), (), s32[]{:S(2)}) async-start(), calls=%async_computation.3 | async-start | bytes 8650752 | tf_op jit(solution)/shard_map/reduce_scatter | solution.py:731
  10.4 35.7 %collective-permute-start.12 = (bf16[32,2048]{1,0:T(8,128)(2,1)S(1)}, bf16[32,2048]{1,0:T(8,128)(2,1)}, u32[]{:S(2)}, u32[]{:S(2)}) collective-permute-start(bf16[32,2048]{1,0:T(8,128)(2,1)S(1)} %constant_dynamic-update-slice_fusion), channel_id=1, source_target_pairs={{0,24},{2,26},{4,28},{6,30},{8,0},{10,2},{12,4},{14,6},{16,8},{18,... | collective-permute-start | bytes 393224 | tf_op jit(solution)/shard_map/ppermute | solution.py:51
  15.5 32.2 %collective-permute-start.10 = (bf16[32,2048]{1,0:T(8,128)(2,1)S(1)}, bf16[32,2048]{1,0:T(8,128)(2,1)}, u32[]{:S(2)}, u32[]{:S(2)}) collective-permute-start(bf16[32,2048]{1,0:T(8,128)(2,1)S(1)} %constant_dynamic-update-slice_fusion), channel_id=1, source_target_pairs={{0,8},{2,10},{4,12},{6,14},{8,16},{10,18},{12,20},{14,22},{16,24},... | collective-permute-start | bytes 393224 | tf_op jit(solution)/shard_map/ppermute | solution.py:51
  41.1 83.0 %collective-permute-start.9 = (bf16[512,1024]{0,1:T(8,128)(2,1)}, bf16[512,1024]{0,1:T(8,128)(2,1)}, u32[]{:S(2)}, u32[]{:S(2)}) collective-permute-start(bf16[512,1024]{0,1:T(8,128)(2,1)} %bitcast.35), channel_id=1, source_target_pairs={{0,1},{1,0},{2,3},{3,2},{4,5},{5,4},{6,7},{7,6},{8,9},{9,8},{10,11... | collective-permute-start | bytes 3145736 | tf_op jit(solution)/shard_map/ppermute | solution.py:42
  51.3 83.8 %collective-permute-start.29 = (bf16[512,1024]{0,1:T(8,128)(2,1)}, bf16[512,1024]{0,1:T(8,128)(2,1)}, u32[]{:S(2)}, u32[]{:S(2)}) collective-permute-start(bf16[512,1024]{0,1:T(8,128)(2,1)} %bitcast.60), channel_id=1, source_target_pairs={{0,1},{1,0},{2,3},{3,2},{4,5},{5,4},{6,7},{7,6},{8,9},{9,8},{10,11... | collective-permute-start | bytes 3145736 | tf_op jit(solution)/shard_map/ppermute | solution.py:42
  58.4 62.4 %collective-permute-start.14 = (bf16[4,32,2048]{2,1,0:T(8,128)(2,1)}, bf16[4,32,2048]{2,1,0:T(8,128)(2,1)}, u32[]{:S(2)}, u32[]{:S(2)}) collective-permute-start(bf16[4,32,2048]{2,1,0:T(8,128)(2,1)} %pad_maximum_fusion.4.refs_0_), channel_id=1, source_target_pairs={{0,1},{1,0},{2,3},{3,2},{4,5},{5,4},{6,7},{7,6},{8,9},{9,8},{10,11... | collective-permute-start | bytes 1572872 | tf_op jit(solution)/shard_map/ppermute | solution.py:42
  84.0 50.7 %collective-permute-start.16 = (bf16[4,32,2048]{2,1,0:T(8,128)(2,1)}, bf16[4,32,2048]{2,1,0:T(8,128)(2,1)}, u32[]{:S(2)}, u32[]{:S(2)}) collective-permute-start(bf16[4,32,2048]{2,1,0:T(8,128)(2,1)} %pad_maximum_fusion.4.refs_0_), channel_id=1, source_target_pairs={{0,4},{2,6},{4,0},{6,2},{8,12},{10,14},{12,8},{14,10},{16,20},{18,... | collective-permute-start | bytes 1572872 | tf_op jit(solution)/shard_map/ppermute | solution.py:45
  91.6 32.4 %collective-permute-start.25 = (bf16[4,32,1152]{2,1,0:T(8,128)(2,1)}, bf16[4,32,1152]{2,1,0:T(8,128)(2,1)}, u32[]{:S(2)}, u32[]{:S(2)}) collective-permute-start(bf16[4,32,1152]{2,1,0:T(8,128)(2,1)} %pad_maximum_fusion.5.refs_8_.refs_16_), channel_id=1, source_target_pairs={{0,16},{2,18},{4,20},{6,22},{8,24},{10,26},{12,28},{14,30},{16,0},... | collective-permute-start | bytes 884744 | tf_op jit(solution)/shard_map/ppermute | solution.py:51
  147.5 44.8 %collective-permute-start.2 = (bf16[4,32,1024]{2,1,0:T(8,128)(2,1)S(1)}, bf16[4,32,1024]{2,1,0:T(8,128)(2,1)S(1)}, u32[]{:S(2)}, u32[]{:S(2)}) collective-permute-start(bf16[4,32,1024]{2,1,0:T(8,128)(2,1)S(1)} %copy-done.17), channel_id=1, source_target_pairs={{0,2},{2,0},{4,6},{6,4},{8,10},{10,8},{12,14},{14,12},{16,18},{18,... | collective-permute-start | bytes 786440 | tf_op jit(solution)/shard_map/ppermute | solution.py:48
  147.8 44.4 %collective-permute-start.4 = (bf16[4,32,1024]{2,1,0:T(8,128)(2,1)S(1)}, bf16[4,32,1024]{2,1,0:T(8,128)(2,1)S(1)}, u32[]{:S(2)}, u32[]{:S(2)}) collective-permute-start(bf16[4,32,1024]{2,1,0:T(8,128)(2,1)S(1)} %copy-done.27), channel_id=1, source_target_pairs={{0,2},{2,0},{4,6},{6,4},{8,10},{10,8},{12,14},{14,12},{16,18},{18,... | collective-permute-start | bytes 786440 | tf_op jit(solution)/shard_map/ppermute | solution.py:48
  148.0 44.2 %collective-permute-start.6 = (bf16[4,32,1024]{2,1,0:T(8,128)(2,1)S(1)}, bf16[4,32,1024]{2,1,0:T(8,128)(2,1)S(1)}, u32[]{:S(2)}, u32[]{:S(2)}) collective-permute-start(bf16[4,32,1024]{2,1,0:T(8,128)(2,1)S(1)} %copy-done.29), channel_id=1, source_target_pairs={{0,2},{2,0},{4,6},{6,4},{8,10},{10,8},{12,14},{14,12},{16,18},{18,... | collective-permute-start | bytes 786440 | tf_op jit(solution)/shard_map/ppermute | solution.py:48
  148.3 43.9 %collective-permute-start.8 = (bf16[4,32,1024]{2,1,0:T(8,128)(2,1)S(1)}, bf16[4,32,1024]{2,1,0:T(8,128)(2,1)S(1)}, u32[]{:S(2)}, u32[]{:S(2)}) collective-permute-start(bf16[4,32,1024]{2,1,0:T(8,128)(2,1)S(1)} %copy-done.31), channel_id=1, source_target_pairs={{0,2},{2,0},{4,6},{6,4},{8,10},{10,8},{12,14},{14,12},{16,18},{18,... | collective-permute-start | bytes 786440 | tf_op jit(solution)/shard_map/ppermute | solution.py:48
  371.0 73.6 %collective-permute-start.30 = (bf16[512,1024]{0,1:T(8,128)(2,1)}, bf16[512,1024]{0,1:T(8,128)(2,1)}, u32[]{:S(2)}, u32[]{:S(2)}) collective-permute-start(bf16[512,1024]{0,1:T(8,128)(2,1)} %bitcast.63), channel_id=1, source_target_pairs={{0,1},{1,0},{2,3},{3,2},{4,5},{5,4},{6,7},{7,6},{8,9},{9,8},{10,11... | collective-permute-start | bytes 3145736 | tf_op jit(solution)/shard_map/ppermute | solution.py:42
  374.6 39.5 %collective-permute-start.32 = (f32[4,2,2,3,128]{4,3,2,1,0:T(4,128)S(1)}, f32[4,2,2,3,128]{4,3,2,1,0:T(4,128)S(1)}, u32[]{:S(2)}, u32[]{:S(2)}) collective-permute-start(f32[4,2,2,3,128]{4,3,2,1,0:T(4,128)S(1)} %dynamic-slice_bitcast_fusion.2), channel_id=1, source_target_pairs={{0,2},{2,0},{4,6},{6,4},{8,10},{10,8},{12,14},{14,12},{16,18},{18,... | collective-permute-start | bytes 73736 | tf_op jit(solution)/shard_map/ppermute | solution.py:48
  393.8 80.4 %collective-permute-start.56 = (bf16[4,2,2,32,4096]{4,3,0,2,1:T(8,128)(2,1)}, bf16[4,2,2,32,4096]{4,3,0,2,1:T(8,128)(2,1)}, u32[]{:S(2)}, u32[]{:S(2)}) collective-permute-start(bf16[4,2,2,32,4096]{4,3,0,2,1:T(8,128)(2,1)} %copy.268), channel_id=1, source_target_pairs={{0,2},{2,0},{4,6},{6,4},{8,10},{10,8},{12,14},{14,12},{16,18},{18,... | collective-permute-start | bytes 12582920 | tf_op jit(solution)/shard_map/ppermute | solution.py:48
  443.0 39.1 %collective-permute-start.44 = (bf16[4,2,2,32,1536]{4,3,0,2,1:T(8,128)(2,1)}, bf16[4,2,2,32,1536]{4,3,0,2,1:T(8,128)(2,1)}, u32[]{:S(2)}, u32[]{:S(2)}) collective-permute-start(bf16[4,2,2,32,1536]{4,3,0,2,1:T(8,128)(2,1)} %copy.263), channel_id=1, source_target_pairs={{0,2},{2,0},{4,6},{6,4},{8,10},{10,8},{12,14},{14,12},{16,18},{18,... | collective-permute-start | bytes 4718600 | tf_op jit(solution)/shard_map/ppermute | solution.py:48
  444.6 38.8 %collective-permute-start.38 = (bf16[4,2,2,32,1536]{4,3,0,2,1:T(8,128)(2,1)}, bf16[4,2,2,32,1536]{4,3,0,2,1:T(8,128)(2,1)}, u32[]{:S(2)}, u32[]{:S(2)}) collective-permute-start(bf16[4,2,2,32,1536]{4,3,0,2,1:T(8,128)(2,1)} %copy.258), channel_id=1, source_target_pairs={{0,2},{2,0},{4,6},{6,4},{8,10},{10,8},{12,14},{14,12},{16,18},{18,... | collective-permute-start | bytes 4718600 | tf_op jit(solution)/shard_map/ppermute | solution.py:48
  453.4 35.9 %collective-permute-start.53 = (bf16[2,2,32,1024]{3,2,1,0:T(8,128)(2,1)S(1)}, bf16[2,2,32,1024]{3,2,1,0:T(8,128)(2,1)S(1)}, u32[]{:S(2)}, u32[]{:S(2)}) collective-permute-start(bf16[2,2,32,1024]{3,2,1,0:T(8,128)(2,1)S(1)} %get-tuple-element.176), channel_id=1, source_target_pairs={{0,24},{2,26},{4,28},{6,30},{8,0},{10,2},{12,4},{14,6},{16,8},{18,... | collective-permute-start | bytes 786440 | tf_op jit(solution)/shard_map/ppermute | solution.py:51
  482.1 106.9 %collective-permute-start.57 = (bf16[4,2,32,4096]{3,2,1,0:T(8,128)(2,1)}, bf16[4,2,32,4096]{3,2,1,0:T(8,128)(2,1)}, u32[]{:S(2)}, u32[]{:S(2)}) collective-permute-start(bf16[4,2,32,4096]{3,2,1,0:T(8,128)(2,1)} %copy.270), channel_id=1, source_target_pairs={{0,4},{2,6},{4,0},{6,2},{8,12},{10,14},{12,8},{14,10},{16,20},{18,... | collective-permute-start | bytes 6291464 | tf_op jit(solution)/shard_map/ppermute | solution.py:45
  488.3 78.5 %collective-permute-start.45 = (bf16[4,2,32,1536]{3,2,1,0:T(8,128)(2,1)}, bf16[4,2,32,1536]{3,2,1,0:T(8,128)(2,1)}, u32[]{:S(2)}, u32[]{:S(2)}) collective-permute-start(bf16[4,2,32,1536]{3,2,1,0:T(8,128)(2,1)} %copy.265), channel_id=1, source_target_pairs={{0,4},{2,6},{4,0},{6,2},{8,12},{10,14},{12,8},{14,10},{16,20},{18,... | collective-permute-start | bytes 2359304 | tf_op jit(solution)/shard_map/ppermute | solution.py:45
  493.0 75.6 %collective-permute-start.39 = (bf16[4,2,32,1536]{3,2,1,0:T(8,128)(2,1)}, bf16[4,2,32,1536]{3,2,1,0:T(8,128)(2,1)}, u32[]{:S(2)}, u32[]{:S(2)}) collective-permute-start(bf16[4,2,32,1536]{3,2,1,0:T(8,128)(2,1)} %copy.260), channel_id=1, source_target_pairs={{0,4},{2,6},{4,0},{6,2},{8,12},{10,14},{12,8},{14,10},{16,20},{18,... | collective-permute-start | bytes 2359304 | tf_op jit(solution)/shard_map/ppermute | solution.py:45
  494.6 70.3 %collective-permute-start.54 = (bf16[2,32,1024]{2,1,0:T(8,128)(2,1)S(1)}, bf16[2,32,1024]{2,1,0:T(8,128)(2,1)S(1)}, u32[]{:S(2)}, u32[]{:S(2)}) collective-permute-start(bf16[2,32,1024]{2,1,0:T(8,128)(2,1)S(1)} %dynamic-slice_bitcast_fusion), channel_id=1, source_target_pairs={{0,4},{2,6},{4,0},{6,2},{8,12},{10,14},{12,8},{14,10},{16,20},{18,... | collective-permute-start | bytes 393224 | tf_op jit(solution)/shard_map/ppermute | solution.py:45
  (77 other events, 864.1 us)
Sparse Core Ops, SparseCore 0:
  11.0 113.3 all-gather.4
  127.4 77.1 all-gather.2
  241.8 210.4 reduce-scatter.1
where the time goes:
time: 654 us; the launch traced here: 646 us
  Pallas kernels  248 us (38%)
  waiting for transfers between devices  190 us (29%)
  starting transfers between devices  78.1 us (12%)
  local copies, waits for them, and re-layouts  72.7 us (11%)
  other arithmetic  42.5 us (6%)
  between operations  14.9 us (2%)
    pallas_call x11, Pallas kernels, run(): pl.pallas_call(body, grid_spec=pltpu.PrefetchScalarGridSpec(num_scalar_pr...  167 us
    ppermute x9, waiting for transfers between devices, over_y(): return lax.ppermute(v, DP, [(i, i ^ 2) for i in range(self.dp)])  69.6 us
    ppermute x12, waiting for transfers between devices, over_x(): return lax.ppermute(v, SEQ, [(0, 1), (1, 0)])  66.3 us
    pallas_call x2, Pallas kernels, attention_backward(): pl.pallas_call(partial(attention_backward_kernel, head=head, chunk=256),...  54.5 us
    ppermute x24, waiting for transfers between devices, along_z(): lax.ppermute(v, DP, [(i, (i + 4 * k) % self.dp) for i in range(self.dp)])  52.7 us
    ppermute x24, starting transfers between devices, along_z(): lax.ppermute(v, DP, [(i, (i + 4 * k) % self.dp) for i in range(self.dp)])  50.4 us
    pallas_call x2, Pallas kernels, attention_forward(): pl.pallas_call(partial(attention_forward_kernel, head=head, chunk=512), g...  26.6 us
    unnamed x82, local copies, waits for them, and re-layouts  18.2 us
  transfers between devices with their start and end apart: 65, of which 18 were waited for; matrix products, arithmetic and copies ran while one was open for 17% of the time, Pallas kernels for 38%

commit v1 on v0

--- a/solution.py
+++ b/solution.py
@@ -21,6 +21,12 @@
 VMEM_BYTES = 60 * 2**20
 TILE = 256
 GROUPS = 2
+LONG, SHORT = 5.0, 0.05
+WG, SUM = "weight_grad_", "sum_"
+
+
+def cost(flops, nbytes=0):
+    return pl.CostEstimate(flops=int(flops), bytes_accessed=int(nbytes), transcendentals=0)
 
 
 def dot(left, right, dims=NN):
@@ -44,6 +50,10 @@
     def over_y(self, v):
         return lax.ppermute(v, DP, [(i, i ^ 2) for i in range(self.dp)])
 
+    def over_xy(self, v):
+        pairs = [(2 * i + x, 2 * (i ^ 2) + 1 - x) for i in range(self.dp) for x in range(2)]
+        return lax.ppermute(v, BOTH, pairs)
+
     def over_core(self, v):
         return lax.ppermute(v, DP, [(i, i ^ 1) for i in range(self.dp)])
 
@@ -76,42 +86,64 @@
     return weight
 
 
-def weight_of(parts, width):
+def columns_of(*parts):
     pieces = parts[0][0]
-    weight = Weight((len(pieces) * pieces[0][0].shape[1], width))
-    for pieces, source, columns, target in parts:
+    weight = Weight((len(pieces) * pieces[0][0].shape[1], sum(width for _, _, width in parts)))
+    target = 0
+    for pieces, start, width in parts:
         for array, index, device in pieces:
             rows = array.shape[1]
-            weight.add(array, index, rows, device * rows, source, columns, target)
+            weight.add(array, index, rows, device * rows, start, width, target)
+        target += width
     return weight
 
 
-def gather_pieces(grid, shard, z_first):
-    pieces = []
-    if not grid.cube:
-        every = lax.all_gather(shard, BOTH, axis=0)
-        return [(every, i, i) for i in range(every.shape[0])]
-    if z_first:
-        own = jnp.stack([shard] + [grid.along_z(shard, k) for k in range(1, grid.nz)])
-        half = {(0, 0): own, (0, 1): grid.over_x(own)}
-        for x in range(2):
-            half[1, x] = grid.over_y(half[0, x])
-        for (y, x), piece in half.items():
+def gather(shard):
+    every = lax.all_gather(shard, BOTH, axis=0)
+    return [(every, i, i) for i in range(every.shape[0])]
+
+
+class Gather:
+    def __init__(self, grid, shard):
+        self.grid = grid
+        if not grid.cube:
+            self.all = gather(shard)
+            return
+        shard = shard[None]
+        self.got = [shard] + [grid.along_z(shard, k) for k in range(1, grid.nz)]
+
+    def near(self, clock, wait):
+        if not self.grid.cube:
+            return wait
+        own = jnp.concatenate(self.got)
+        own, wait = clock(own, wait)
+        self.got = [own, self.grid.over_xy(own), self.grid.over_x(own), self.grid.over_y(own)]
+        return wait
+
+    def pieces(self, clock):
+        grid = self.grid
+        if not grid.cube:
+            return self.all
+        self.got = clock(*self.got)
+        pieces = []
+        for (y, x), piece in zip(((0, 0), (1, 1), (0, 1), (1, 0)), self.got):
             for c, array in enumerate((piece, grid.over_core(piece))):
-                for k in range(grid.nz):
-                    pieces.append((array, k, grid.device(c, y, x, k)))
-    else:
-        pair = jnp.stack([shard, grid.over_x(shard)])
-        four = jnp.concatenate([pair, grid.over_y(pair)])
-        for k in range(grid.nz):
-            piece = four if k == 0 else grid.along_z(four, k)
-            for c, array in enumerate((piece, grid.over_core(piece))):
-                for j in range(4):
-                    pieces.append((array, j, grid.device(c, j // 2, j % 2, k)))
-    return pieces
-
-
-def run(kernel, weights, ins, outs, steps, flops, scratch=(), scalars=()):
+                pieces += [(array, k, grid.device(c, y, x, k)) for k in range(grid.nz)]
+        return pieces
+
+
+class Clock:
+    def __init__(self):
+        self.token = None
+
+    def __call__(self, *values):
+        if self.token is None:
+            self.token = jnp.zeros((8, 128), F32)
+        *values, self.token = lax.optimization_barrier((*values, self.token))
+        return values[0] if len(values) == 1 else values
+
+
+def run(kernel, weights, ins, outs, steps, flops, scratch=(), scalars=(), name=None, share=SHORT):
     rows_at = [row for w in weights for row in w.rows_at] + list(scalars)
     rows_at = jnp.stack([jnp.asarray(row, jnp.int32) for row in rows_at] or [jnp.int32(0)])
     n_copies = sum(len(w.copies) for w in weights)
@@ -157,11 +189,12 @@
     anywhere = pl.BlockSpec(memory_space=pl.ANY)
 
     def spec(block, index):
+        if index is shifted_row_block:
+            return pl.BlockSpec(block, lambda i, at: (at[n_copies] + i, 0))
+        if index is shifted_part_block:
+            return pl.BlockSpec(block, lambda i, at: (0, at[n_copies] + i, 0))
         return pl.BlockSpec(block, lambda i, at: index(i))
 
-    moved = sum(math.prod(w.shape) * 2 for w in weights)
-    moved += sum(a.size * a.dtype.itemsize for a, _, _ in ins)
-    moved += sum(math.prod(s) * jnp.dtype(d).itemsize for s, d, _, _ in outs)
     semaphores = [pltpu.SemaphoreType.DMA((n_copies,))] if n_copies else []
     return pl.pallas_call(
         body,
@@ -174,7 +207,8 @@
         ),
         out_shape=[jax.ShapeDtypeStruct(shape, dtype) for shape, dtype, _, _ in outs],
         compiler_params=pltpu.CompilerParams(vmem_limit_bytes=VMEM_BYTES),
-        cost_estimate=pl.CostEstimate(flops=int(flops), bytes_accessed=moved, transcendentals=0),
+        name=name,
+        cost_estimate=cost(flops * share),
     )(rows_at, *[a for w in weights for a in w.arrays], *[a for a, _, _ in ins])
 
 
@@ -182,35 +216,83 @@
     return lax.dynamic_index_in_dim(array, index, axis, keepdims=False)
 
 
-def halve(kept, got, mine, axis, move):
-    sent = (pick(kept, 1 - mine, axis).astype(F32) + pick(got, 1 - mine, axis).astype(F32)).astype(kept.dtype)
-    own = (pick(kept, mine, axis).astype(F32) + pick(got, mine, axis).astype(F32)).astype(kept.dtype)
-    return own, move(sent)
-
-
-def scatter_sum(grid, kept, sent, z_first):
-    got = grid.over_core(sent)
-    if z_first:
-        parts = []
-        for k in range(grid.nz):
-            z = (grid.z + k) % grid.nz
-            parts.append((pick(kept, z, 0).astype(F32) + pick(got, z, 0).astype(F32)).astype(kept.dtype))
-        total = parts[0].astype(F32)
-        for k in range(1, grid.nz):
-            total = total + grid.along_z(parts[k], k).astype(F32)
-        total = total.astype(kept.dtype)
-        got = grid.over_y(pick(total, 1 - grid.y, 0))
-        total = (pick(total, grid.y, 0).astype(F32) + got.astype(F32)).astype(kept.dtype)
-        got = grid.over_x(pick(total, 1 - grid.x, 0))
-        return pick(total, grid.x, 0).astype(F32) + got.astype(F32)
-    own, got = halve(kept, got, grid.y, 1, grid.over_y)
-    own, got = halve(own, got, grid.x, 1, grid.over_x)
-    total = pick(own, grid.z, 0).astype(F32) + pick(got, grid.z, 0).astype(F32)
-    for k in range(1, grid.nz):
-        z = (grid.z + k) % grid.nz
-        part = (pick(own, z, 0).astype(F32) + pick(got, z, 0).astype(F32)).astype(kept.dtype)
-        total = total + grid.along_z(part, k).astype(F32)
-    return total
+def total(terms):
+    value = terms[0].astype(F32)
+    for term in terms[1:]:
+        value = value + term.astype(F32)
+    return value
+
+
+def split_sum(terms, order, name):
+    parts, size = terms[0].shape[0], terms[0].size
+    rest = terms[0].shape[1:]
+    columns = terms[0].shape[-1]
+    rows = size // parts // columns
+    tile = rows
+    while tile * columns > 2**18 and tile % 32 == 0:
+        tile //= 2
+    flat = [t.reshape(parts, rows, columns) for t in terms]
+    wanted = len(order)
+
+    def kernel(at, *refs):
+        del at
+        for j in range(wanted):
+            value = refs[j][0].astype(F32)
+            for i in range(1, len(terms)):
+                value = value + refs[i * wanted + j][0].astype(F32)
+            refs[len(terms) * wanted + j][...] = value.astype(terms[0].dtype)
+
+    outs = pl.pallas_call(
+        kernel,
+        grid_spec=pltpu.PrefetchScalarGridSpec(
+            num_scalar_prefetch=1,
+            grid=(rows // tile,),
+            in_specs=[
+                pl.BlockSpec((1, tile, columns), lambda i, at, j=j: (at[j], i, 0))
+                for _ in terms
+                for j in range(wanted)
+            ],
+            out_specs=[pl.BlockSpec((tile, columns), lambda i, at: (i, 0))] * wanted,
+        ),
+        out_shape=[jax.ShapeDtypeStruct((rows, columns), terms[0].dtype)] * wanted,
+        compiler_params=pltpu.CompilerParams(vmem_limit_bytes=VMEM_BYTES),
+        name=name,
+        cost_estimate=cost(0, (len(terms) + 1) * size * 2 * wanted // parts),
+    )(jnp.stack(order).astype(jnp.int32), *[t for t in flat for _ in range(wanted)])
+    return [out.reshape(rest) for out in outs]
+
+
+class Scatter:
+    def __init__(self, grid, clock, kept, sent, order):
+        self.grid, self.clock, self.order = grid, clock, order
+        self.own, self.got = [kept], [grid.over_core(sent)]
+
+    def step(self):
+        grid, axis, self.order = self.grid, self.order[0], self.order[1:]
+        terms = self.clock(*self.own, *self.got)
+        if axis == "z":
+            places = [(grid.z + k) % grid.nz for k in range(grid.nz)]
+            own, *parts = self.clock(*split_sum(terms, places, SUM + axis))
+            self.got = [grid.along_z(part, k) for k, part in enumerate(parts, 1)]
+        else:
+            mine, move = (grid.y, grid.over_y) if axis == "y" else (grid.x, grid.over_x)
+            own, part = self.clock(*split_sum(terms, [mine, 1 - mine], SUM + axis))
+            self.got = [move(part)]
+        self.own = [own]
+
+    def result(self):
+        return total(self.own + self.got)
+
+
+class Summed:
+    def __init__(self, value):
+        self.value, self.own = value, []
+
+    def step(self):
+        pass
+
+    def result(self):
+        return lax.psum_scatter(self.value, BOTH, scatter_dimension=0, tiled=True)
 
 
 def to_whole(grid, part):
@@ -325,10 +407,9 @@
             jax.ShapeDtypeStruct((count, length, width // GROUPS), BF),
             jax.ShapeDtypeStruct((count, steps, lanes // head, length), F32),
         ],
+        name="attention_forward",
         compiler_params=pltpu.CompilerParams(vmem_limit_bytes=VMEM_BYTES),
-        cost_estimate=pl.CostEstimate(
-            flops=12 * count * length * length * width // GROUPS, bytes_accessed=12 * 2**20, transcendentals=0
-        ),
+        cost_estimate=cost(12 * count * length * length * width // GROUPS),
     )(qkv, qkv, qkv, mask)
 
 
@@ -343,10 +424,9 @@
         out_specs=grads,
         out_shape=jax.ShapeDtypeStruct((3, count, length, width // GROUPS), BF),
         scratch_shapes=[pltpu.VMEM((length, head), F32)] * 2,
+        name="attention_backward",
         compiler_params=pltpu.CompilerParams(vmem_limit_bytes=VMEM_BYTES),
-        cost_estimate=pl.CostEstimate(
-            flops=26 * count * length * length * width // GROUPS, bytes_accessed=20 * 2**20, transcendentals=0
-        ),
+        cost_estimate=cost(26 * count * length * length * width * (LONG if group else SHORT)),
     )(qkv, qkv, qkv, mask, grad, context, totals_in)
 
 
@@ -396,6 +476,14 @@
     return (i, 0)
 
 
+def shifted_row_block(i):
+    raise NotImplementedError
+
+
+def shifted_part_block(i):
+    raise NotImplementedError
+
+
 def fixed_block(i):
     return (0, 0)
 
@@ -434,6 +522,7 @@
         ],
         rows // TILE,
         6 * rows * width * width,
+        name="project_in",
     )
 
 
@@ -466,6 +555,7 @@
         ],
         rows // TILE,
         2 * rows * width * width,
+        name="project_out",
     )
 
 
@@ -494,6 +584,7 @@
         [((rows, wide), BF, (TILE, wide), row_block)] * 2,
         rows // TILE,
         2 * rows * width * wide,
+        name="feed_up",
     )
 
 
@@ -536,6 +627,8 @@
         ],
         rows // TILE,
         4 * rows * width * wide,
+        name="feed_down",
+        share=LONG,
     )
 
 
@@ -572,11 +665,13 @@
         ],
         rows // TILE,
         2 * rows * width * (wide + width),
-    )
-
-
-def project_back(grads, grad_residual, x, params, w_qkv):
-    rows, width = x.shape
+        name="feed_back",
+        share=LONG,
+    )
+
+
+def project_back(grads, grad_residual, x, params, w_qkv, first, count):
+    width = x.shape[1]
     each = width // GROUPS
 
     def kernel(_, ins, outs, weights, scratch):
@@ -600,72 +695,136 @@
         kernel,
         [w_qkv],
         [
-            (grad_residual, (TILE, width), row_block),
-            (x, (TILE, width), row_block),
+            (grad_residual, (TILE, width), shifted_row_block),
+            (x, (TILE, width), shifted_row_block),
             (params, (16, width), fixed_block),
         ]
-        + [(g, (3, TILE, each), lambda i: (0, i, 0)) for g in grads],
+        + [(g, (3, TILE, each), shifted_part_block) for g in grads],
         [
-            ((rows, width), BF, (TILE, width), row_block),
+            ((count * TILE, width), BF, (TILE, width), row_block),
             ((8, width), F32, (8, width), fixed_block),
         ],
-        rows // TILE,
-        6 * rows * width * width,
-    )
-
-
-def weight_grad(grid, turned, right):
-    features, rows = turned.shape
-    parts, _, columns = right.shape
-    tile = min(512, columns)
-    per = columns // tile
-    pair = features // grid.nz // 4
+        count,
+        6 * count * TILE * width * width,
+        scalars=[first],
+        name="project_back",
+    )
+
+
+def weight_grad(grid, clock, pairs, order):
+    if not grid.cube:
+        return Summed(jnp.concatenate([dot(turned, part) for turned, right in pairs for part in right], axis=1))
+    features, rows = pairs[0][0].shape
+    tile = min(512, *(right.shape[2] for _, right in pairs))
+    counts = [right.shape[0] * right.shape[2] // tile for _, right in pairs]
+    columns = sum(counts) * tile
+    shard = features // grid.nz // 8
+    places, shape = leading(grid, order)
 
     def kernel(scalars, ins, outs, weights, scratch):
-        kept, sent = outs
         first = scalars[0] == 0
-        value = dot(ins[0][...], ins[1][0]).astype(BF)
-        for j in range(grid.nz * 2):
-            low = value[2 * j * pair : (2 * j + 1) * pair]
-            high = value[(2 * j + 1) * pair : (2 * j + 2) * pair]
-            kept[j * pair : (j + 1) * pair] = jnp.where(first, low, high)
-            sent[j * pair : (j + 1) * pair] = jnp.where(first, high, low)
-
+        step = pl.program_id(0)
+
+        def work(turned, right, low, high):
+            value = dot(turned[...], right[0]).astype(BF)
+            for (z, y, x), at in places:
+                start = ((z * 2 + y) * 4 + x) * shard
+                low[at * shard : (at + 1) * shard] = value[start : start + shard]
+                start += 2 * shard
+                high[at * shard : (at + 1) * shard] = value[start : start + shard]
+
+        done = 0
+        for j, count in enumerate(counts):
+            here = (step >= done) & (step < done + count)
+            done += count
+
+            @pl.when(here & first)
+            def _():
+                work(ins[2 * j], ins[2 * j + 1], *outs)
+
+            @pl.when(here & jnp.logical_not(first))
+            def _():
+                work(ins[2 * j], ins[2 * j + 1], outs[1], outs[0])
+
+    ins, done = [], 0
+    for (turned, right), count in zip(pairs, counts):
+        per = right.shape[2] // tile
+
+        def block(i, done=done, count=count, per=per):
+            j = jnp.clip(i - done, 0, count - 1)
+            return (j // per, 0, j % per)
+
+        turned, right = clock(turned, right)
+        ins += [(turned, (features, rows), fixed_block), (right, (1, rows, tile), block)]
+        done += count
     kept, sent = run(
         kernel,
         [],
-        [
-            (turned, (features, rows), fixed_block),
-            (right, (1, rows, tile), lambda i: (i // per, 0, i % per)),
-        ],
-        [((features // 2, parts * columns), BF, (features // 2, tile), column_block)] * 2,
-        parts * per,
-        2 * rows * features * parts * columns,
+        ins,
+        [((features // 2, columns), BF, (features // 2, tile), column_block)] * 2,
+        sum(counts),
+        2 * rows * features * columns,
         scalars=[grid.core],
-    )
-    shape = (grid.nz, 2, 2, pair // 2, parts * columns)
-    return kept.reshape(shape), sent.reshape(shape)
-
-
-def weight_grad_turned(turned, right, devices):
+        name=WG + str(columns),
+    )
+    shape += (shard, columns)
+    kept, sent = clock(kept, sent)
+    return Scatter(grid, clock, kept.reshape(shape), sent.reshape(shape), order)
+
+
+def weight_grad_turned(grid, clock, turned, right, order):
     features, rows = turned.shape
-    columns = right.shape[1]
-    each = columns // devices
-    tile = min(512, columns)
-
-    def kernel(_, ins, outs, weights, scratch):
+    each = right.shape[1] // (grid.nz * 8)
+    places, shape = leading(grid, order)
+
+    def kernel(scalars, ins, outs, weights, scratch):
+        first = scalars[0] == 0
         value = dot(ins[0][...], ins[1][...]).astype(BF)
-        for j in range(tile // each):
-            outs[0][j] = value[:, j * each : (j + 1) * each]
-
-    return run(
+
+        def store(low, high):
+            for (z, y, x), at in places:
+                start = ((z * 2 + y) * 4 + x) * each
+                low[at] = value[:, start : start + each]
+                start += 2 * each
+                high[at] = value[:, start : start + each]
+
+        @pl.when(first)
+        def _():
+            store(*outs)
+
+        @pl.when(jnp.logical_not(first))
+        def _():
+            store(outs[1], outs[0])
+
+    tile = min(256, features)
+    shape += (features, each)
+    turned, right = clock(turned, right)
+    kept, sent = run(
         kernel,
         [],
-        [(turned, (features, rows), fixed_block), (right, (rows, tile), column_block)],
-        [((devices, features, each), BF, (tile // each, features, each), lambda i: (i, 0, 0))],
-        columns // tile,
-        2 * rows * features * columns,
-    )[0]
+        [(turned, (tile, rows), row_block), (right, right.shape, fixed_block)],
+        [((grid.nz * 4, features, each), BF, (grid.nz * 4, tile, each), lambda i: (0, i, 0))] * 2,
+        features // tile,
+        2 * rows * features * right.shape[1],
+        scalars=[grid.core],
+        name=WG + "turned",
+    )
+    kept, sent = clock(kept, sent)
+    return Scatter(grid, clock, kept.reshape(shape), sent.reshape(shape), order)
+
+
+def leading(grid, order):
+    counts = {"z": grid.nz, "y": 2, "x": 2}
+    places = []
+    for z in range(grid.nz):
+        for y in range(2):
+            for x in range(2):
+                here = {"z": z, "y": y, "x": x}
+                at = 0
+                for axis in order:
+                    at = at * counts[axis] + here[axis]
+                places.append(((z, y, x), at))
+    return places, tuple(counts[axis] for axis in order)
 
 
 def shards(tokens, cotangent, segments, global_blocks, random_blocks, *params):
@@ -673,6 +832,7 @@
     gain1, shift1, w_q, b_q, w_k, w_v, b_v, w_o, b_o, gain2, shift2, w_up, b_up, w_down, b_down = params
     count = tokens.shape[0]
     width = tokens.shape[-1]
+    wide = w_up.shape[1]
     each = w_v.shape[0]
     devices = grid.dp * grid.group
     replicas = max(1, grid.group // count)
@@ -682,70 +842,122 @@
     rows = n * length
     inputs = inputs.reshape(rows, width)
     vectors = [gain1, shift1, b_q, b_v, b_o, gain2, shift2, b_down]
-    extra = jnp.concatenate([jnp.stack(vectors, axis=1), b_up.reshape(each, -1)], axis=1)
+    extra = jnp.concatenate([*vectors, b_up]).reshape(-1, each).T
     extra = jnp.pad(extra, ((0, 0), (0, 128 - extra.shape[1])))
-    pieces_qk = gather_pieces(grid, jnp.concatenate([w_q, w_k], axis=1), True)
-    pieces_v = gather_pieces(grid, jnp.concatenate([w_v, extra], axis=1), False)
-    w_qkv = weight_of([(pieces_qk, 0, 2 * width, 0), (pieces_v, 0, width, 2 * width)], 3 * width)
-    extra = weight_of([(pieces_v, width, 128, 0)], 128)
-    w_o = weight_of([(gather_pieces(grid, w_o, False), 0, width, 0)], width)
-    w_up = whole_weight(lax.all_gather(w_up, BOTH, axis=0, tiled=True))
-    w_down = whole_weight(lax.all_gather(w_down, BOTH, axis=0, tiled=True))
-    upstream = to_whole(grid, cotangent).reshape(rows, width)
-    upstream_turned = upstream.T
-
+
+    clock = Clock()
+    first = gather(jnp.concatenate([w_q, w_k], axis=1))
+    second = Gather(grid, jnp.concatenate([w_v, w_o, extra], axis=1))
+    inputs = second.near(clock, inputs)
+    third = Gather(grid, w_up)
+    fourth = gather(w_down)
     if grid.group > 1:
         place = lax.axis_index(SEQ)
-        first = place * n if count % grid.group == 0 else place % count
+        start = place * n if count % grid.group == 0 else place % count
         segments, global_blocks, random_blocks = (
-            lax.dynamic_slice_in_dim(a, first, n, 0) for a in (segments, global_blocks, random_blocks)
+            lax.dynamic_slice_in_dim(a, start, n, 0) for a in (segments, global_blocks, random_blocks)
         )
     mask = attention_mask(segments, global_blocks, random_blocks)
 
-    qkv, normed1_turned, params = project_in(inputs, w_qkv, extra)
+    second = second.pieces(clock)
+    inputs = third.near(clock, inputs)
+    w_qkv = columns_of((first, 0, 2 * width), (second, 0, width))
+    w_o, extra = columns_of((second, width, width)), columns_of((second, 2 * width, 128))
+    inputs = clock(inputs)
+    qkv, normed1_turned, params = clock(*project_in(inputs, w_qkv, extra))
     qkv = qkv.reshape(n, length, 3 * width)
-    attended = [attention_forward(qkv, mask, g) for g in range(GROUPS)]
+    upstream = to_whole(grid, clock(cotangent)).reshape(rows, width)
+    attended = []
+    for g in range(GROUPS):
+        qkv, mask = clock(qkv, mask)
+        attended.append(clock(*attention_forward(qkv, mask, g)))
     contexts = [a[0].reshape(rows, -1) for a in attended]
-    residual, normed2, normed2_turned, context_turned = project_out(contexts, inputs, params, w_o)
-    bias_up = params[8:12].T.reshape(1, -1)
-    activated, slope = feed_up(normed2, w_up, bias_up)
-
-    grad_w_down = weight_grad_turned(upstream_turned, activated, devices)
-    mixed, grad_hidden, sum_up, sum_down = feed_down(activated, slope, residual, upstream, params, w_down)
+    w_up, w_down = columns_of((third.pieces(clock), 0, wide)), columns_of((fourth, 0, width))
+    contexts[0] = clock(contexts[0])
+    residual, normed2, normed2_turned, context_turned = clock(*project_out(contexts, inputs, params, w_o))
+    bias_up = params[8 : 8 + wide // width].reshape(-1, devices, each).transpose(1, 0, 2).reshape(1, -1)
+    activated, slope = clock(*feed_up(normed2, w_up, bias_up))
+
+    upstream_turned = upstream.T
+    if grid.cube:
+        sum_w_down = weight_grad_turned(grid, clock, upstream_turned, activated, "yzx")
+    else:
+        sum_w_down = Summed(dot(activated, upstream, TN))
+    activated = clock(activated)
+    mixed, grad_hidden, sum_up, sum_down = clock(
+        *feed_down(activated, slope, residual, upstream, params, w_down)
+    )
     mixed = from_whole(grid, mixed.reshape(n, length, width), count)
-    terms_up = weight_grad_of(grid, normed2_turned, grad_hidden[None])
-    grad_residual, grad_att, grad_context, sums2 = feed_back(
-        grad_hidden, residual, upstream, params, w_up, w_o
-    )
-    terms_o = weight_grad_of(grid, context_turned, grad_att[None])
+    sum_w_down.step()
+    sum_w_up = weight_grad(grid, clock, [(normed2_turned, grad_hidden[None])], "xyz")
+    grad_hidden = clock(grad_hidden)
+    grad_residual, grad_att, grad_context, sums2 = clock(
+        *feed_back(grad_hidden, residual, upstream, params, w_up, w_o)
+    )
+    sum_w_down.step()
+    sum_w_up.step()
     grad_context = grad_context.reshape(n, length, width)
-    grads, terms_qkv = [], []
+    grads, sums_qkv = [], []
     for g in range(GROUPS):
-        grad = attention_backward(qkv, mask, grad_context, *attended[g], g)
-        grads.append(grad.reshape(3, rows, -1))
-        terms_qkv.append(weight_grad_of(grid, normed1_turned, grads[g]))
-    grad_inputs, sums1 = project_back(grads, grad_residual, inputs, params, w_qkv)
-    grad_inputs = from_whole(grid, grad_inputs.reshape(n, length, width), count)
-
-    share = 1.0 / replicas
-    grad_w_down = lax.psum_scatter(grad_w_down * BF(share), BOTH, scatter_dimension=0, tiled=True)
-    grad_w_down = grad_w_down[0].T.astype(F32)
-    grad_w_up = sum_up_devices(grid, terms_up, False) * share
-    grad_w_o = sum_up_devices(grid, terms_o, True) * share
-    ended = [sum_up_devices(grid, t, False) * share for t in terms_qkv]
-    cut = width // GROUPS
-    grad_w_q, grad_w_k, grad_w_v = (
-        jnp.concatenate([e[:, j * cut : (j + 1) * cut] for e in ended], axis=1) for j in range(3)
-    )
+        grad_context = clock(grad_context)
+        grad = clock(attention_backward(qkv, mask, grad_context, *attended[g], g)).reshape(3, rows, -1)
+        grads.append(grad)
+        if g > 0:
+            sum_w_up.step()
+            sums_qkv[0].step()
+        pairs = [(normed1_turned, grad)] + [(context_turned, grad_att[None])] * (g == 0)
+        sums_qkv.append(weight_grad(grid, clock, pairs, "yxz" if g == 0 else "xyz"))
+        if g == 0:
+            sum_w_down.step()
+            sum_w_up.step()
+    steps = rows // TILE
+    swap = grid.group == 2 and count == 2
+    half = steps // 2 if swap else steps
+    place = lax.axis_index(SEQ)
+    grads[-1] = clock(grads[-1])
+    grad_inputs, sums1 = clock(
+        *project_back(grads, grad_residual, inputs, params, w_qkv, (1 - place) * half if swap else 0, half)
+    )
+    sums_qkv[0].step()
+    sums_qkv[1].step()
+    if swap:
+        got = grid.over_x(grad_inputs)
+        grads[-1] = clock(grads[-1])
+        own, more = clock(*project_back(grads, grad_residual, inputs, params, w_qkv, place * half, half))
+        sums1 = sums1 + more
+        grad_inputs = jnp.stack([jnp.where(place == 0, own, got), jnp.where(place == 0, got, own)])
+    else:
+        grad_inputs = from_whole(grid, grad_inputs.reshape(n, length, width), count)
+    sums_qkv[0].step()
+    sums_qkv[1].step()
+    sums1, sums2, sum_up, sum_down = clock(sums1, sums2, sum_up, sum_down)
     vectors = jnp.concatenate([sums1[:4], sums2[:3], sum_down[:1]])
     vectors = vectors.reshape(8, devices, each).transpose(1, 0, 2).reshape(devices, -1)
     vectors = jnp.concatenate([vectors, sum_up[:1].reshape(devices, -1)], axis=1)
     if grid.cube:
         vectors = vectors.reshape(grid.nz, 2, 2, 2, -1, 128)
-        vectors = scatter_sum(grid, pick(vectors, grid.core, 2), pick(vectors, 1 - grid.core, 2), False)
+        vectors = halve(vectors, grid.core, 2, grid.over_core)
+        vectors = halve(vectors, grid.y, 1, grid.over_y)
+        sums_qkv[1].step()
+        vectors = halve(clock(vectors), grid.x, 1, grid.over_x)
+        parts = [pick(vectors, (grid.z + k) % grid.nz, 0) for k in range(grid.nz)]
+        vectors = total(parts[:1] + [grid.along_z(part, k) for k, part in enumerate(parts) if k])
     else:
-        vectors = lax.psum_scatter(vectors, BOTH, scatter_dimension=0, tiled=True) * share
-    vectors = vectors.reshape(-1)
+        vectors = lax.psum_scatter(vectors, BOTH, scatter_dimension=0, tiled=True)
+    vectors = vectors + clock.token[0, 0]
+
+    share = 1.0 / replicas
+    grad_w_down = sum_w_down.result() * share
+    if grid.cube:
+        grad_w_down = grad_w_down.T
+    grad_w_up = sum_w_up.result() * share
+    ended = [moving.result() * share for moving in sums_qkv]
+    cut = width // GROUPS
+    grad_w_o = ended[0][:, 3 * cut :]
+    grad_w_q, grad_w_k, grad_w_v = (
+        jnp.concatenate([e[:, j * cut : (j + 1) * cut] for e in ended], axis=1) for j in range(3)
+    )
+    vectors = (vectors * share).reshape(-1)
     grad_b_up = vectors[8 * each :]
     grad_gain1, grad_shift1, grad_b_q, grad_b_v, grad_b_o, grad_gain2, grad_shift2, grad_b_down = (
         vectors[j * each : (j + 1) * each] for j in range(8)
@@ -756,17 +968,8 @@
     )
 
 
-def weight_grad_of(grid, turned, right):
-    if grid.cube:
-        return weight_grad(grid, turned, right)
-    return [dot(turned, part) for part in right]
-
-
-def sum_up_devices(grid, terms, z_first):
-    if grid.cube:
-        return scatter_sum(grid, *terms, z_first)
-    whole = jnp.concatenate(terms, axis=1)
-    return lax.psum_scatter(whole, BOTH, scatter_dimension=0, tiled=True)
+def halve(value, mine, dim, move):
+    return pick(value, mine, dim) + move(pick(value, 1 - mine, dim))
 
 
 def solution(mesh):

time: 654 us -> 564 us (0.86)
  waiting for transfers between devices: 190 us -> 88.1 us
  Pallas kernels: 248 us -> 307 us
  local copies, waits for them, and re-layouts: 72.7 us -> 34.2 us
  other arithmetic: 42.5 us -> 28.6 us
  starting transfers between devices: 78.1 us -> 85.4 us
    ppermute x9 -> x7, waiting for transfers between devices: 69.6 us -> 16.7 us  [over_y(): return lax.ppermute(v, DP, [(i, i ^ 2) for i in range(self.dp)])]
    pallas_call x0 -> x12, Pallas kernels: none -> 48.7 us  [split_sum(): pl.pallas_call(kernel, grid_spec=pltpu.PrefetchScalarGridSpec(num_scalar_...]
    ppermute x24 -> x21, waiting for transfers between devices: 52.7 us -> 17.3 us  [along_z(): lax.ppermute(v, DP, [(i, (i + 4 * k) % self.dp) for i in range(self.dp)])]
    ppermute x12 -> x11, waiting for transfers between devices: 66.3 us -> 30.9 us  [over_x(): return lax.ppermute(v, SEQ, [(0, 1), (1, 0)])]
    convert_element_type x12 -> x0, other arithmetic: 18.7 us -> none  [the longest x5 14.4 us: halve(): (pick(kept, mine, axis).astype(F32) + pick(got, mine, axis).astype(F32))....]
    dynamic_slice x13 -> x3, local copies, waits for them, and re-layouts: 16.9 us -> 0.05 us  [pick(): return lax.dynamic_index_in_dim(array, index, axis, keepdims=False)]
    ppermute x0 -> x2, waiting for transfers between devices: none -> 14.4 us  [over_xy(): return lax.ppermute(v, BOTH, pairs)]
    reshape x5, local copies, waits for them, and re-layouts: 10.5 us -> 1.04 us  [the longest x3 0.85 us: shards(): params[8:8 + wide // width].reshape(-1, devices, each).transpose(1, 0, 2)]
  transfers between devices with their start and end apart: 65 -> 56, of which waited for: 18 -> 15; matrix products, arithmetic and copies ran while one was open for 17% -> 9% of each run, Pallas kernels for 38% -> 53%
where the time goes in v1:
time: 564 us; the launch traced here: 558 us
  Pallas kernels  307 us (54%)
  waiting for transfers between devices  88.1 us (16%)
  starting transfers between devices  85.4 us (15%)
  local copies, waits for them, and re-layouts  34.2 us (6%)
  other arithmetic  28.6 us (5%)
  between operations  15.3 us (3%)
    pallas_call x11, Pallas kernels, run(): pl.pallas_call(body, grid_spec=pltpu.PrefetchScalarGridSpec(num_scalar_pr...  177 us
    ppermute x21, starting transfers between devices, along_z(): lax.ppermute(v, DP, [(i, (i + 4 * k) % self.dp) for i in range(self.dp)])  57.2 us
    pallas_call x2, Pallas kernels, attention_backward(): pl.pallas_call(partial(attention_backward_kernel, head=head, chunk=256),...  54.5 us
    pallas_call x12, Pallas kernels, split_sum(): pl.pallas_call(kernel, grid_spec=pltpu.PrefetchScalarGridSpec(num_scalar_...  48.7 us
    ppermute x11, waiting for transfers between devices, over_x(): return lax.ppermute(v, SEQ, [(0, 1), (1, 0)])  30.9 us
    pallas_call x2, Pallas kernels, attention_forward(): pl.pallas_call(partial(attention_forward_kernel, head=head, chunk=512), g...  26.9 us
    ppermute x11, starting transfers between devices, over_x(): return lax.ppermute(v, SEQ, [(0, 1), (1, 0)])  17.5 us
    ppermute x21, waiting for transfers between devices, along_z(): lax.ppermute(v, DP, [(i, (i + 4 * k) % self.dp) for i in range(self.dp)])  17.3 us
  transfers between devices with their start and end apart: 56, of which 15 were waited for; matrix products, arithmetic and copies ran while one was open for 9% of the time, Pallas kernels for 53%

profile of v1, /device:TPU:0, one launch (start us, length us, event | category | flops | bytes accessed | tf_op | source)
XLA Modules:
  0.0 558.4 jit_solution(9891608331774670926)
XLA Ops:
  24.8 8.6 %collective-permute-done.4 = bf16[1,32,2176]{2,1,0:T(8,128)(2,1)S(1)} collective-permute-done((bf16[1,32,2176]{2,1,0:T(8,128)(2,1)S(1)}, bf16[1,32,2176]{2,1,0:T(8,128)(2,1)S(1)}, u32[]{:S(2)}, u32[]{:S(2)}) %collective-permute-start.4) | collective-permute-done | bytes 139296 | tf_op jit(solution)/shard_map/ppermute | solution.py:61
  58.3 7.3 %collective-permute-start = (bf16[1,32,4096]{2,1,0:T(8,128)(2,1)S(1)}, bf16[1,32,4096]{2,1,0:T(8,128)(2,1)}, u32[]{:S(2)}, u32[]{:S(2)}) collective-permute-start(bf16[1,32,4096]{2,1,0:T(8,128)(2,1)S(1)} %bitcast.265), channel_id=1, source_target_pairs={{0,8},{2,10},{4,12},{6,14},{8,16},{10,18},{12,20},{14,22},{16,24},... | collective-permute-start | bytes 786440 | tf_op jit(solution)/shard_map/ppermute | solution.py:61
  65.6 9.6 %collective-permute-done.7.refs_3_.refs_11_.refs_2_.refs_10_ = bf16[4,32,2176]{2,1,0:T(8,128)(2,1)S(1)} collective-permute-done((bf16[4,32,2176]{2,1,0:T(8,128)(2,1)S(1)}, bf16[4,32,2176]{2,1,0:T(8,128)(2,1)S(1)}, u32[]{:S(2)}, u32[]{:S(2)}) %collective-permute-start.7) | collective-permute-done | bytes 557088 | tf_op jit(solution)/shard_map/ppermute | solution.py:55
  87.4 8.0 %all-gather.7.cloned.1.call-done = bf16[1024,2048]{1,0:T(8,128)(2,1)} async-done(((bf16[32,2048]{1,0:T(8,128)(2,1)}), bf16[1024,2048]{1,0:T(8,128)(2,1)}) %all-gather.7.cloned.1.call-update) | async-done | bytes 4194320 | tf_op jit(solution)/shard_map/all_gather | solution.py:102
  95.4 15.1 %project_in.1 = (bf16[1024,3072]{1,0:T(8,128)(2,1)}, bf16[1024,1024]{1,0:T(8,128)(2,1)}, f32[16,1024]{1,0:T(8,128)}) custom-call(s32[96]{0:T(128)} %stack.147.at, bf16[32,32,2048]{2,1,0:T(8,128)(2,1)} %bitcast.203, bf16[4,32,2176]{2,1,0:T(8,128)(2,1)} %copy-done.3, bf16[4,32,2176]{2,1,0:T(8,128)(2,1)} %copy-done.8, bf16[4,32,2176]{2,1,0:T(8,128)(2,1)} %copy-done.7, ...), custom_call_target="tpu_custom_call" | custom-call | flops 322122560 | tf_op jit(solution)/shard_map/project_in/pallas_call | solution.py:199
  110.5 13.3 %attention_forward.2 = (bf16[1,1024,512]{2,1,0:T(8,128)(2,1)}, f32[1,4,2,1024]{3,2,1,0:T(2,128)}) custom-call(bf16[1,1024,3072]{2,1,0:T(8,128)(2,1)} %bitcast.188, bf16[1,1024,3072]{2,1,0:T(8,128)(2,1)} %bitcast.189, bf16[1,1024,3072]{2,1,0:T(8,128)(2,1)} %bitcast.190, f32[1,1024,1024]{2,1,0:T(8,128)} %and_select_fusion.mask_ref), custom_call_target="tpu_custom_call" | custom-call | flops 6442450944 | tf_op jit(solution)/shard_map/attention_forward/pallas_call | solution.py:401
  123.8 13.6 %attention_forward.3 = (bf16[1,1024,512]{2,1,0:T(8,128)(2,1)}, f32[1,4,2,1024]{3,2,1,0:T(2,128)}) custom-call(bf16[1,1024,3072]{2,1,0:T(8,128)(2,1)} %bitcast.191, bf16[1,1024,3072]{2,1,0:T(8,128)(2,1)} %bitcast.192, bf16[1,1024,3072]{2,1,0:T(8,128)(2,1)} %bitcast.193, f32[1,1024,1024]{2,1,0:T(8,128)} %and_select_fusion.mask_ref), custom_call_target="tpu_custom_call" | custom-call | flops 6442450944 | tf_op jit(solution)/shard_map/attention_forward/pallas_call | solution.py:401
  151.4 10.9 %project_out.1 = (f32[1024,1024]{1,0:T(8,128)}, bf16[1024,1024]{1,0:T(8,128)(2,1)}, bf16[1024,1024]{1,0:T(8,128)(2,1)}, bf16[1024,1024]{1,0:T(8,128)(2,1)}) custom-call(s32[32]{0:T(128)} %stack.146.at, bf16[4,32,2176]{2,1,0:T(8,128)(2,1)} %copy-done.3, bf16[4,32,2176]{2,1,0:T(8,128)(2,1)} %copy-done.8, bf16[4,32,2176]{2,1,0:T(8,128)(2,1)} %copy-done.7, ...), custom_call_target="tpu_custom_call" | custom-call | flops 107374184 | tf_op jit(solution)/shard_map/project_out/pallas_call | solution.py:199
  162.4 24.7 %feed_up.1 = (bf16[1024,4096]{1,0:T(8,128)(2,1)}, bf16[1024,4096]{1,0:T(8,128)(2,1)}) custom-call(s32[32]{0:T(128)} %stack.146.at, bf16[4,32,4096]{2,1,0:T(8,128)(2,1)} %pad_maximum_fusion.4.refs_0_, bf16[4,32,4096]{2,1,0:T(8,128)(2,1)} %collective-permute-done.17.refs_1_, bf16[4,32,4096]{2,1,0:T(8,128)(2,1)} %collective-permute-done.10.refs_2_, ...), custom_call_target="tpu_custom_call" | custom-call | flops 429496736 | tf_op jit(solution)/shard_map/feed_up/pallas_call | solution.py:199
  191.7 15.9 %weight_grad_turned.1 = (bf16[16,1024,128]{2,1,0:T(8,128)(2,1)}, bf16[16,1024,128]{2,1,0:T(8,128)(2,1)}) custom-call(s32[1]{0:T(128)} %bitcast.48.at, bf16[1024,1024]{1,0:T(8,128)(2,1)} %copy.64.refs_0_, bf16[1024,4096]{1,0:T(8,128)(2,1)} %get-tuple-element.334.refs_1_), custom_call_target="tpu_custom_call" | custom-call | flops 429496736 | tf_op jit(solution)/shard_map/weight_grad_turned/pallas_call | solution.py:199
  207.6 30.3 %feed_down.1 = (bf16[1024,1024]{1,0:T(8,128)(2,1)}, bf16[1024,4096]{1,0:T(8,128)(2,1)}, f32[8,4096]{1,0:T(8,128)}, f32[8,1024]{1,0:T(8,128)}) custom-call(s32[32]{0:T(128)} %iota_multiply_fusion.at, bf16[32,128,1024]{2,1,0:T(8,128)(2,1)} %bitcast.276, bf16[1024,4096]{1,0:T(8,128)(2,1)} %get-tuple-element.334.refs_1_, ...), custom_call_target="tpu_custom_call" | custom-call | flops 85899345920 | tf_op jit(solution)/shard_map/feed_down/pallas_call | solution.py:199
  246.2 14.7 %weight_grad_4096.1 = (bf16[512,4096]{1,0:T(8,128)(2,1)}, bf16[512,4096]{1,0:T(8,128)(2,1)}) custom-call(s32[1]{0:T(128)} %bitcast.48.at, bf16[1024,1024]{1,0:T(8,128)(2,1)} %get-tuple-element.354.refs_0_, bf16[1,1024,4096]{2,1,0:T(8,128)(2,1)} %bitcast.233), custom_call_target="tpu_custom_call" | custom-call | flops 429496736 | tf_op jit(solution)/shard_map/weight_grad_4096/pallas_call | solution.py:199
  261.1 23.3 %feed_back.1 = (f32[1024,1024]{1,0:T(8,128)}, bf16[1024,1024]{1,0:T(8,128)(2,1)}, bf16[1024,1024]{1,0:T(8,128)(2,1)}, f32[8,1024]{1,0:T(8,128)}) custom-call(s32[64]{0:T(128)} %stack.154.at, bf16[4,32,4096]{2,1,0:T(8,128)(2,1)} %pad_maximum_fusion.4.refs_0_, bf16[4,32,4096]{2,1,0:T(8,128)(2,1)} %collective-permute-done.17.refs_1_, ...), custom_call_target="tpu_custom_call" | custom-call | flops 53687091200 | tf_op jit(solution)/shard_map/feed_back/pallas_call | solution.py:199
  284.4 8.3 %collective-permute-done.25 = bf16[4,2,1024,128]{3,2,1,0:T(8,128)(2,1)S(1)} collective-permute-done((bf16[4,2,1024,128]{3,2,1,0:T(8,128)(2,1)}, bf16[4,2,1024,128]{3,2,1,0:T(8,128)(2,1)S(1)}, u32[]{:S(2)}, u32[]{:S(2)}) %collective-permute-start.25) | collective-permute-done | bytes 2097184 | tf_op jit(solution)/shard_map/ppermute | solution.py:51
  298.3 6.7 %sum_x.4 = (bf16[256,4096]{1,0:T(8,128)(2,1)}, bf16[256,4096]{1,0:T(8,128)(2,1)}) custom-call(s32[2]{0:T(128)} %pad_add_fusion.1.at, bf16[2,256,4096]{2,1,0:T(8,128)(2,1)} %bitcast.217, bf16[2,256,4096]{2,1,0:T(8,128)(2,1)} %bitcast.218, bf16[2,256,4096]{2,1,0:T(8,128)(2,1)} %bitcast.83.refs_2_.refs_3_, bf16[2,256,4096]{2,1,0:T(8,128)(2,1)} %bitcast.83.refs_2_.refs_3_), custom_call_target="tpu_custom_call" | custom-call | bytes 12582912 | tf_op jit(solution)/shard_map/sum_x/pallas_call | solution.py:245
  305.0 10.9 %collective-permute-start.27 = (bf16[2,1024,128]{2,1,0:T(8,128)(2,1)}, bf16[2,1024,128]{2,1,0:T(8,128)(2,1)S(1)}, u32[]{:S(2)}, u32[]{:S(2)}) collective-permute-start(bf16[2,1024,128]{2,1,0:T(8,128)(2,1)} %bitcast.79), channel_id=1, source_target_pairs={{0,8},{2,10},{4,12},{6,14},{8,16},{10,18},{12,20},{14,22},{16,24},... | collective-permute-start | bytes 1572872 | tf_op jit(solution)/shard_map/ppermute | solution.py:61
  322.7 27.3 %attention_backward.2 = bf16[3,1,1024,512]{3,2,1,0:T(8,128)(2,1)} custom-call(bf16[1,1024,3072]{2,1,0:T(8,128)(2,1)} %bitcast.194, bf16[1,1024,3072]{2,1,0:T(8,128)(2,1)} %bitcast.195, bf16[1,1024,3072]{2,1,0:T(8,128)(2,1)} %bitcast.196, f32[1,1024,1024]{2,1,0:T(8,128)} %and_select_fusion.mask_ref, bf16[1,1024,1024]{2,1,0:T(8,128)(2,1)} %bitcast.255, ...), custom_call_target="tpu_custom_call" | custom-call | flops 1395864320 | tf_op jit(solution)/shard_map/attention_backward/pallas_call | solution.py:420
  349.9 10.9 %weight_grad_2560.1 = (bf16[512,2560]{1,0:T(8,128)(2,1)}, bf16[512,2560]{1,0:T(8,128)(2,1)}) custom-call(s32[1]{0:T(128)} %bitcast.48.at, bf16[1024,1024]{1,0:T(8,128)(2,1)} %get-tuple-element.447.refs_0_, bf16[3,1024,512]{2,1,0:T(8,128)(2,1)} %bitcast.200, bf16[1024,1024]{1,0:T(8,128)(2,1)} %get-tuple-element.404.refs_2_, bf16[1,1024,1024]{2,1,0:T(8,128)(2,1)} %bitcast.257), custom_call_target="tpu_custom_call" | custom-call | flops 268435456 | tf_op jit(solution)/shard_map/weight_grad_2560/pallas_call | solution.py:199
  370.3 27.3 %attention_backward.3 = bf16[3,1,1024,512]{3,2,1,0:T(8,128)(2,1)} custom-call(bf16[1,1024,3072]{2,1,0:T(8,128)(2,1)} %bitcast.197, bf16[1,1024,3072]{2,1,0:T(8,128)(2,1)} %bitcast.198, bf16[1,1024,3072]{2,1,0:T(8,128)(2,1)} %bitcast.199, f32[1,1024,1024]{2,1,0:T(8,128)} %and_select_fusion.mask_ref, bf16[1,1024,1024]{2,1,0:T(8,128)(2,1)} %bitcast.256, ...), custom_call_target="tpu_custom_call" | custom-call | flops 139586437120 | tf_op jit(solution)/shard_map/attention_backward/pallas_call | solution.py:420
  408.5 7.1 %weight_grad_1536.1 = (bf16[512,1536]{1,0:T(8,128)(2,1)}, bf16[512,1536]{1,0:T(8,128)(2,1)}) custom-call(s32[1]{0:T(128)} %bitcast.48.at, bf16[1024,1024]{1,0:T(8,128)(2,1)} %get-tuple-element.447.refs_0_, bf16[3,1024,512]{2,1,0:T(8,128)(2,1)} %bitcast.214), custom_call_target="tpu_custom_call" | custom-call | flops 161061280 | tf_op jit(solution)/shard_map/weight_grad_1536/pallas_call | solution.py:199
  433.1 11.8 %project_back.2 = (bf16[512,1024]{1,0:T(8,128)(2,1)}, f32[8,1024]{1,0:T(8,128)}) custom-call(s32[65]{0:T(128)} %stack.167.at, bf16[32,32,2048]{2,1,0:T(8,128)(2,1)} %bitcast.204, bf16[4,32,2176]{2,1,0:T(8,128)(2,1)} %copy-done.3, bf16[4,32,2176]{2,1,0:T(8,128)(2,1)} %copy-done.8, bf16[4,32,2176]{2,1,0:T(8,128)(2,1)} %copy-done.7, ...), custom_call_target="tpu_custom_call" | custom-call | flops 161061280 | tf_op jit(solution)/shard_map/project_back/pallas_call | solution.py:199
  459.8 11.7 %project_back.3 = (bf16[512,1024]{1,0:T(8,128)(2,1)}, f32[8,1024]{1,0:T(8,128)}) custom-call(s32[65]{0:T(128)} %stack.153.at, bf16[32,32,2048]{2,1,0:T(8,128)(2,1)} %bitcast.205, bf16[4,32,2176]{2,1,0:T(8,128)(2,1)} %copy-done.3, bf16[4,32,2176]{2,1,0:T(8,128)(2,1)} %copy-done.8, bf16[4,32,2176]{2,1,0:T(8,128)(2,1)} %copy-done.7, ...), custom_call_target="tpu_custom_call" | custom-call | flops 161061280 | tf_op jit(solution)/shard_map/project_back/pallas_call | solution.py:199
  472.4 15.0 %collective-permute-done.36.refs_4_.refs_5_.refs_6_.refs_7_ = bf16[4,32,2560]{2,1,0:T(8,128)(2,1)S(1)} collective-permute-done((bf16[4,32,2560]{2,1,0:T(8,128)(2,1)}, bf16[4,32,2560]{2,1,0:T(8,128)(2,1)S(1)}, u32[]{:S(2)}, u32[]{:S(2)}) %collective-permute-start.36) | collective-permute-done | bytes 655392 | tf_op jit(solution)/shard_map/ppermute | solution.py:48
  491.1 11.5 %collective-permute-done.35 = bf16[2,4,32,1536]{3,2,1,0:T(8,128)(2,1)S(1)} collective-permute-done((bf16[2,4,32,1536]{3,2,1,0:T(8,128)(2,1)}, bf16[2,4,32,1536]{3,2,1,0:T(8,128)(2,1)S(1)}, u32[]{:S(2)}, u32[]{:S(2)}) %collective-permute-start.35) | collective-permute-done | bytes 786464 | tf_op jit(solution)/shard_map/ppermute | solution.py:48
  (291 shorter events, 199.1 us)
Async XLA Ops:
  7.4 88.0 %all-gather.7.cloned.1.call-start = ((), (), s32[]{:S(2)}) async-start(), calls=%async_computation.1 | async-start | bytes 4325376 | tf_op jit(solution)/shard_map/all_gather | solution.py:102
  9.2 198.3 %all-gather.5.cloned.1.call-start = ((), (), s32[]{:S(2)}) async-start(), calls=%async_computation | async-start | bytes 8650752 | tf_op jit(solution)/shard_map/all_gather | solution.py:102
  20.2 55.5 %collective-permute-start.2 = (bf16[1,32,4096]{2,1,0:T(8,128)(2,1)S(1)}, bf16[1,32,4096]{2,1,0:T(8,128)(2,1)S(1)}, u32[]{:S(2)}, u32[]{:S(2)}) collective-permute-start(bf16[1,32,4096]{2,1,0:T(8,128)(2,1)S(1)} %bitcast.263), channel_id=1, source_target_pairs={{0,24},{2,26},{4,28},{6,30},{8,0},{10,2},{12,4},{14,6},{16,8},{18,... | collective-permute-start | bytes 786440 | tf_op jit(solution)/shard_map/ppermute | solution.py:61
  23.3 52.4 %collective-permute-start.1 = (bf16[1,32,4096]{2,1,0:T(8,128)(2,1)S(1)}, bf16[1,32,4096]{2,1,0:T(8,128)(2,1)}, u32[]{:S(2)}, u32[]{:S(2)}) collective-permute-start(bf16[1,32,4096]{2,1,0:T(8,128)(2,1)S(1)} %bitcast.264), channel_id=1, source_target_pairs={{0,16},{2,18},{4,20},{6,22},{8,24},{10,26},{12,28},{14,30},{16,0},... | collective-permute-start | bytes 786440 | tf_op jit(solution)/shard_map/ppermute | solution.py:61
  83.4 54.0 %collective-permute-start.12 = (bf16[4,32,4096]{2,1,0:T(8,128)(2,1)}, bf16[4,32,4096]{2,1,0:T(8,128)(2,1)}, u32[]{:S(2)}, u32[]{:S(2)}) collective-permute-start(bf16[4,32,4096]{2,1,0:T(8,128)(2,1)} %pad_maximum_fusion.4.refs_0_), channel_id=1, source_target_pairs={{0,4},{2,6},{4,0},{6,2},{8,12},{10,14},{12,8},{14,10},{16,20},{18,... | collective-permute-start | bytes 3145736 | tf_op jit(solution)/shard_map/ppermute | solution.py:51
  83.5 53.9 %collective-permute-start.11 = (bf16[4,32,4096]{2,1,0:T(8,128)(2,1)}, bf16[4,32,4096]{2,1,0:T(8,128)(2,1)}, u32[]{:S(2)}, u32[]{:S(2)}) collective-permute-start(bf16[4,32,4096]{2,1,0:T(8,128)(2,1)} %pad_maximum_fusion.4.refs_0_), channel_id=1, source_target_pairs={{0,1},{1,0},{2,3},{3,2},{4,5},{5,4},{6,7},{7,6},{8,9},{9,8},{10,11... | collective-permute-start | bytes 3145736 | tf_op jit(solution)/shard_map/ppermute | solution.py:48
  87.3 54.9 %collective-permute-start.10 = (bf16[4,32,4096]{2,1,0:T(8,128)(2,1)}, bf16[4,32,4096]{2,1,0:T(8,128)(2,1)}, u32[]{:S(2)}, u32[]{:S(2)}) collective-permute-start(bf16[4,32,4096]{2,1,0:T(8,128)(2,1)} %pad_maximum_fusion.4.refs_0_), channel_id=1, source_target_pairs={{0,5},{1,4},{2,7},{3,6},{4,1},{5,0},{6,3},{7,2},{8,13},{9,12},{10,... | collective-permute-start | bytes 3145736 | tf_op jit(solution)/shard_map/ppermute | solution.py:55
  144.4 42.7 %collective-permute-start.21 = (bf16[512,1024]{1,0:T(8,128)(2,1)}, bf16[512,1024]{1,0:T(8,128)(2,1)S(1)}, u32[]{:S(2)}, u32[]{:S(2)}) collective-permute-start(bf16[512,1024]{1,0:T(8,128)(2,1)} %dynamic-slice_bitcast_fusion.1), channel_id=1, source_target_pairs={{0,1},{1,0},{2,3},{3,2},{4,5},{5,4},{6,7},{7,6},{8,9},{9,8},{10,11... | collective-permute-start | bytes 3145736 | tf_op jit(solution)/shard_map/ppermute | solution.py:48
  207.5 30.4 %collective-permute-start.23 = (bf16[2,4,2,1024,128]{4,3,2,1,0:T(8,128)(2,1)}, bf16[2,4,2,1024,128]{4,3,2,1,0:T(8,128)(2,1)}, u32[]{:S(2)}, u32[]{:S(2)}) collective-permute-start(bf16[2,4,2,1024,128]{4,3,2,1,0:T(8,128)(2,1)} %bitcast.278), channel_id=1, source_target_pairs={{0,2},{2,0},{4,6},{6,4},{8,10},{10,8},{12,14},{14,12},{16,18},{18,... | collective-permute-start | bytes 12582920 | tf_op jit(solution)/shard_map/ppermute | solution.py:58
  244.4 48.3 %collective-permute-start.25 = (bf16[4,2,1024,128]{3,2,1,0:T(8,128)(2,1)}, bf16[4,2,1024,128]{3,2,1,0:T(8,128)(2,1)S(1)}, u32[]{:S(2)}, u32[]{:S(2)}) collective-permute-start(bf16[4,2,1024,128]{3,2,1,0:T(8,128)(2,1)} %bitcast.281), channel_id=1, source_target_pairs={{0,4},{2,6},{4,0},{6,2},{8,12},{10,14},{12,8},{14,10},{16,20},{18,... | collective-permute-start | bytes 6291464 | tf_op jit(solution)/shard_map/ppermute | solution.py:51
  260.9 37.5 %collective-permute-start.24 = (bf16[2,2,4,32,4096]{4,3,2,1,0:T(8,128)(2,1)}, bf16[2,2,4,32,4096]{4,3,2,1,0:T(8,128)(2,1)}, u32[]{:S(2)}, u32[]{:S(2)}) collective-permute-start(bf16[2,2,4,32,4096]{4,3,2,1,0:T(8,128)(2,1)} %bitcast.277), channel_id=1, source_target_pairs={{0,2},{2,0},{4,6},{6,4},{8,10},{10,8},{12,14},{14,12},{16,18},{18,... | collective-permute-start | bytes 12582920 | tf_op jit(solution)/shard_map/ppermute | solution.py:58
  305.0 60.7 %collective-permute-start.26 = (bf16[2,4,32,4096]{3,2,1,0:T(8,128)(2,1)}, bf16[2,4,32,4096]{3,2,1,0:T(8,128)(2,1)}, u32[]{:S(2)}, u32[]{:S(2)}) collective-permute-start(bf16[2,4,32,4096]{3,2,1,0:T(8,128)(2,1)} %bitcast.280), channel_id=1, source_target_pairs={{0,1},{1,0},{2,3},{3,2},{4,5},{5,4},{6,7},{7,6},{8,9},{9,8},{10,11... | collective-permute-start | bytes 6291464 | tf_op jit(solution)/shard_map/ppermute | solution.py:48
  305.0 55.8 %collective-permute-start.27 = (bf16[2,1024,128]{2,1,0:T(8,128)(2,1)}, bf16[2,1024,128]{2,1,0:T(8,128)(2,1)S(1)}, u32[]{:S(2)}, u32[]{:S(2)}) collective-permute-start(bf16[2,1024,128]{2,1,0:T(8,128)(2,1)} %bitcast.79), channel_id=1, source_target_pairs={{0,8},{2,10},{4,12},{6,14},{8,16},{10,18},{12,20},{14,22},{16,24},... | collective-permute-start | bytes 1572872 | tf_op jit(solution)/shard_map/ppermute | solution.py:61
  315.9 45.0 %collective-permute-start.28 = (bf16[2,1024,128]{2,1,0:T(8,128)(2,1)}, bf16[2,1024,128]{2,1,0:T(8,128)(2,1)S(1)}, u32[]{:S(2)}, u32[]{:S(2)}) collective-permute-start(bf16[2,1024,128]{2,1,0:T(8,128)(2,1)} %bitcast.80), channel_id=1, source_target_pairs={{0,16},{2,18},{4,20},{6,22},{8,24},{10,26},{12,28},{14,30},{16,0},... | collective-permute-start | bytes 1572872 | tf_op jit(solution)/shard_map/ppermute | solution.py:61
  318.2 42.7 %collective-permute-start.29 = (bf16[2,1024,128]{2,1,0:T(8,128)(2,1)}, bf16[2,1024,128]{2,1,0:T(8,128)(2,1)S(1)}, u32[]{:S(2)}, u32[]{:S(2)}) collective-permute-start(bf16[2,1024,128]{2,1,0:T(8,128)(2,1)} %bitcast.287), channel_id=1, source_target_pairs={{0,24},{2,26},{4,28},{6,30},{8,0},{10,2},{12,4},{14,6},{16,8},{18,... | collective-permute-start | bytes 1572872 | tf_op jit(solution)/shard_map/ppermute | solution.py:61
  322.1 98.0 %collective-permute-start.22 = (bf16[512,1024]{1,0:T(8,128)(2,1)}, bf16[512,1024]{1,0:T(8,128)(2,1)}, u32[]{:S(2)}, u32[]{:S(2)}) collective-permute-start(bf16[512,1024]{1,0:T(8,128)(2,1)} %dynamic-slice_bitcast_fusion), channel_id=1, source_target_pairs={{0,1},{1,0},{2,3},{3,2},{4,5},{5,4},{6,7},{7,6},{8,9},{9,8},{10,11... | collective-permute-start | bytes 3145736 | tf_op jit(solution)/shard_map/ppermute | solution.py:48
  365.7 36.1 %collective-permute-start.30 = (bf16[2,2,4,32,2560]{4,3,2,1,0:T(8,128)(2,1)}, bf16[2,2,4,32,2560]{4,3,2,1,0:T(8,128)(2,1)S(1)}, u32[]{:S(2)}, u32[]{:S(2)}) collective-permute-start(bf16[2,2,4,32,2560]{4,3,2,1,0:T(8,128)(2,1)} %bitcast.279), channel_id=1, source_target_pairs={{0,2},{2,0},{4,6},{6,4},{8,10},{10,8},{12,14},{14,12},{16,18},{18,... | collective-permute-start | bytes 7864328 | tf_op jit(solution)/shard_map/ppermute | solution.py:58
  415.6 36.2 %collective-permute-start.32 = (bf16[2,2,4,32,1536]{4,3,2,1,0:T(8,128)(2,1)}, bf16[2,2,4,32,1536]{4,3,2,1,0:T(8,128)(2,1)S(1)}, u32[]{:S(2)}, u32[]{:S(2)}) collective-permute-start(bf16[2,2,4,32,1536]{4,3,2,1,0:T(8,128)(2,1)} %bitcast.282), channel_id=1, source_target_pairs={{0,2},{2,0},{4,6},{6,4},{8,10},{10,8},{12,14},{14,12},{16,18},{18,... | collective-permute-start | bytes 4718600 | tf_op jit(solution)/shard_map/ppermute | solution.py:58
  415.8 31.2 %collective-permute-start.33 = (bf16[2,4,32,2560]{3,2,1,0:T(8,128)(2,1)}, bf16[2,4,32,2560]{3,2,1,0:T(8,128)(2,1)S(1)}, u32[]{:S(2)}, u32[]{:S(2)}) collective-permute-start(bf16[2,4,32,2560]{3,2,1,0:T(8,128)(2,1)} %bitcast.283), channel_id=1, source_target_pairs={{0,4},{2,6},{4,0},{6,2},{8,12},{10,14},{12,8},{14,10},{16,20},{18,... | collective-permute-start | bytes 3932168 | tf_op jit(solution)/shard_map/ppermute | solution.py:51
  423.3 33.3 %collective-permute-start.50 = (bf16[32,4096]{1,0:T(8,128)(2,1)}, bf16[32,4096]{1,0:T(8,128)(2,1)}, u32[]{:S(2)}, u32[]{:S(2)}) collective-permute-start(bf16[32,4096]{1,0:T(8,128)(2,1)} %get-tuple-element.530), channel_id=1, source_target_pairs={{0,8},{2,10},{4,12},{6,14},{8,16},{10,18},{12,20},{14,22},{16,24},... | collective-permute-start | bytes 786440 | tf_op jit(solution)/shard_map/ppermute | solution.py:61
  424.8 33.0 %collective-permute-start.51 = (bf16[32,4096]{1,0:T(8,128)(2,1)}, bf16[32,4096]{1,0:T(8,128)(2,1)}, u32[]{:S(2)}, u32[]{:S(2)}) collective-permute-start(bf16[32,4096]{1,0:T(8,128)(2,1)} %get-tuple-element.531), channel_id=1, source_target_pairs={{0,16},{2,18},{4,20},{6,22},{8,24},{10,26},{12,28},{14,30},{16,0},... | collective-permute-start | bytes 786440 | tf_op jit(solution)/shard_map/ppermute | solution.py:61
  447.0 61.8 %collective-permute-start.34 = (bf16[512,1024]{1,0:T(8,128)(2,1)}, bf16[512,1024]{1,0:T(8,128)(2,1)}, u32[]{:S(2)}, u32[]{:S(2)}) collective-permute-start(bf16[512,1024]{1,0:T(8,128)(2,1)} %get-tuple-element.479), channel_id=1, source_target_pairs={{0,1},{1,0},{2,3},{3,2},{4,5},{5,4},{6,7},{7,6},{8,9},{9,8},{10,11... | collective-permute-start | bytes 3145736 | tf_op jit(solution)/shard_map/ppermute | solution.py:48
  451.8 35.6 %collective-permute-start.36 = (bf16[4,32,2560]{2,1,0:T(8,128)(2,1)}, bf16[4,32,2560]{2,1,0:T(8,128)(2,1)S(1)}, u32[]{:S(2)}, u32[]{:S(2)}) collective-permute-start(bf16[4,32,2560]{2,1,0:T(8,128)(2,1)} %bitcast.286), channel_id=1, source_target_pairs={{0,1},{1,0},{2,3},{3,2},{4,5},{5,4},{6,7},{7,6},{8,9},{9,8},{10,11... | collective-permute-start | bytes 1966088 | tf_op jit(solution)/shard_map/ppermute | solution.py:48
  456.6 46.0 %collective-permute-start.35 = (bf16[2,4,32,1536]{3,2,1,0:T(8,128)(2,1)}, bf16[2,4,32,1536]{3,2,1,0:T(8,128)(2,1)S(1)}, u32[]{:S(2)}, u32[]{:S(2)}) collective-permute-start(bf16[2,4,32,1536]{3,2,1,0:T(8,128)(2,1)} %bitcast.285), channel_id=1, source_target_pairs={{0,1},{1,0},{2,3},{3,2},{4,5},{5,4},{6,7},{7,6},{8,9},{9,8},{10,11... | collective-permute-start | bytes 2359304 | tf_op jit(solution)/shard_map/ppermute | solution.py:48
  (79 other events, 940.2 us)
Sparse Core Ops, SparseCore 0:
  11.8 83.5 all-gather.6
  98.4 97.1 all-gather.4

commit v2 on v1

--- a/solution.py
+++ b/solution.py
@@ -25,8 +25,8 @@
 WG, SUM = "weight_grad_", "sum_"
 
 
-def cost(flops, nbytes=0):
-    return pl.CostEstimate(flops=int(flops), bytes_accessed=int(nbytes), transcendentals=0)
+def cost(flops):
+    return pl.CostEstimate(flops=int(flops), bytes_accessed=0, transcendentals=0)
 
 
 def dot(left, right, dims=NN):
@@ -143,9 +143,20 @@
         return values[0] if len(values) == 1 else values
 
 
-def run(kernel, weights, ins, outs, steps, flops, scratch=(), scalars=(), name=None, share=SHORT):
+def run(kernel, weights, ins, outs, steps, flops, scratch=(), scalars=(), name=None, share=SHORT, stages=1):
     rows_at = [row for w in weights for row in w.rows_at] + list(scalars)
     rows_at = jnp.stack([jnp.asarray(row, jnp.int32) for row in rows_at] or [jnp.int32(0)])
+    moves = []
+    for which, w in enumerate(weights):
+        cut = w.shape[1] // stages
+        for n, (i, index, rows, source, width, target) in enumerate(w.copies):
+            at = target
+            while at < target + width:
+                size = min(cut - at % cut, target + width - at)
+                moves.append((at // cut, which, n, (i, index, rows, source + at - target, size, at)))
+                at += size
+    moves.sort(key=lambda move: move[0])
+    bases = [sum(len(w.copies) for w in weights[:j]) for j in range(len(weights))]
     n_copies = sum(len(w.copies) for w in weights)
     n_pieces = [len(w.arrays) for w in weights]
 
@@ -159,29 +170,32 @@
         piece_refs = [take(count) for count in n_pieces]
         in_refs, out_refs = take(len(ins)), take(len(outs))
         held = take(len(weights))
-        sems = take(1)[0] if n_copies else None
-
-        def copies():
-            n = 0
-            for weight, sources, target_ref in zip(weights, piece_refs, held):
-                for i, index, rows, source, width, target in weight.copies:
-                    ref = sources[i] if index is None else sources[i].at[index]
-                    row = pl.multiple_of(at[n], rows)
+        sems = take(1)[0] if moves else None
+
+        def copies(stage=None):
+            for n, (due, which, row, (i, index, rows, source, width, target)) in enumerate(moves):
+                if stage is None or due == stage:
+                    ref = piece_refs[which][i] if index is None else piece_refs[which][i].at[index]
                     yield pltpu.make_async_copy(
                         ref.at[:, pl.ds(source, width)],
-                        target_ref.at[pl.ds(row, rows), pl.ds(target, width)],
+                        held[which].at[pl.ds(pl.multiple_of(at[bases[which] + row], rows), rows), pl.ds(target, width)],
                         sems.at[n],
                     )
-                    n += 1
-
-        if n_copies:
-
-            @pl.when(pl.program_id(0) == 0)
+
+        step = pl.program_id(0)
+        if moves:
+
+            @pl.when(step == 0)
             def _():
                 for copy in copies():
                     copy.start()
-                for copy in copies():
-                    copy.wait()
+
+            for stage in range(stages):
+
+                @pl.when(step == stage * (steps // stages))
+                def _():
+                    for copy in copies(stage):
+                        copy.wait()
 
         values = [at[n_copies + i] for i in range(len(scalars))]
         kernel(values, in_refs, out_refs, held, refs)
@@ -195,7 +209,7 @@
             return pl.BlockSpec(block, lambda i, at: (0, at[n_copies] + i, 0))
         return pl.BlockSpec(block, lambda i, at: index(i))
 
-    semaphores = [pltpu.SemaphoreType.DMA((n_copies,))] if n_copies else []
+    semaphores = [pltpu.SemaphoreType.DMA((len(moves),))] if moves else []
     return pl.pallas_call(
         body,
         grid_spec=pltpu.PrefetchScalarGridSpec(
@@ -223,7 +237,7 @@
     return value
 
 
-def split_sum(terms, order, name):
+def split_sum(terms, order, name, share):
     parts, size = terms[0].shape[0], terms[0].size
     rest = terms[0].shape[1:]
     columns = terms[0].shape[-1]
@@ -257,7 +271,7 @@
         out_shape=[jax.ShapeDtypeStruct((rows, columns), terms[0].dtype)] * wanted,
         compiler_params=pltpu.CompilerParams(vmem_limit_bytes=VMEM_BYTES),
         name=name,
-        cost_estimate=cost(0, (len(terms) + 1) * size * 2 * wanted // parts),
+        cost_estimate=cost(2e10 * share),
     )(jnp.stack(order).astype(jnp.int32), *[t for t in flat for _ in range(wanted)])
     return [out.reshape(rest) for out in outs]
 
@@ -267,18 +281,22 @@
         self.grid, self.clock, self.order = grid, clock, order
         self.own, self.got = [kept], [grid.over_core(sent)]
 
-    def step(self):
+    def step(self, share=SHORT):
         grid, axis, self.order = self.grid, self.order[0], self.order[1:]
         terms = self.clock(*self.own, *self.got)
         if axis == "z":
             places = [(grid.z + k) % grid.nz for k in range(grid.nz)]
-            own, *parts = self.clock(*split_sum(terms, places, SUM + axis))
+            own, *parts = self.clock(*split_sum(terms, places, SUM + axis, share))
             self.got = [grid.along_z(part, k) for k, part in enumerate(parts, 1)]
         else:
             mine, move = (grid.y, grid.over_y) if axis == "y" else (grid.x, grid.over_x)
-            own, part = self.clock(*split_sum(terms, [mine, 1 - mine], SUM + axis))
+            own, part = self.clock(*split_sum(terms, [mine, 1 - mine], SUM + axis, share))
             self.got = [move(part)]
         self.own = [own]
+
+    def wait(self, clock):
+        if self.got:
+            self.got = list(clock(*self.got))
 
     def result(self):
         return total(self.own + self.got)
@@ -288,7 +306,10 @@
     def __init__(self, value):
         self.value, self.own = value, []
 
-    def step(self):
+    def step(self, share=SHORT):
+        pass
+
+    def wait(self, clock):
         pass
 
     def result(self):
@@ -311,25 +332,33 @@
     return pick(every, place % count, 0)[None]
 
 
-def from_whole(grid, whole, count):
-    group = grid.group
-    if group == 1:
-        return whole
-    place = lax.axis_index(SEQ)
-    if group == 2 and count == 2:
-        halves = whole.reshape(2, -1, whole.shape[-1])
-        kept, got = pick(halves, place, 0), grid.over_x(pick(halves, 1 - place, 0))
-        first = jnp.where(place == 0, kept, got)
-        second = jnp.where(place == 0, got, kept)
-        return jnp.stack([first, second])
-    if count % group == 0:
-        return lax.all_to_all(whole, SEQ, split_axis=1, concat_axis=0, tiled=True)
-    every = lax.all_gather(whole[0], SEQ, axis=0)[:count]
-    rows = whole.shape[1] // group
-    return lax.dynamic_slice_in_dim(every, place * rows, rows, 1)
-
-
-def attention_forward_kernel(q_ref, k_ref, v_ref, mask_ref, out_ref, total_ref, *, head, chunk):
+class FromWhole:
+    def __init__(self, grid, clock, whole, count):
+        self.grid, self.clock, self.whole, self.count = grid, clock, whole, count
+        self.swap = grid.group == 2 and count == 2
+        if self.swap:
+            place = lax.axis_index(SEQ)
+            halves = whole.reshape(2, -1, whole.shape[-1])
+            self.kept, self.got = pick(halves, place, 0), grid.over_x(pick(halves, 1 - place, 0))
+
+    def result(self):
+        group, whole, count = self.grid.group, self.whole, self.count
+        place = lax.axis_index(SEQ)
+        if self.swap:
+            got = self.clock(self.got)
+            return jnp.stack([jnp.where(place == 0, self.kept, got), jnp.where(place == 0, got, self.kept)])
+        if group == 1:
+            return whole
+        if count % group == 0:
+            return lax.all_to_all(whole, SEQ, split_axis=1, concat_axis=0, tiled=True)
+        every = lax.all_gather(whole[0], SEQ, axis=0)[:count]
+        rows = whole.shape[1] // group
+        return lax.dynamic_slice_in_dim(every, place * rows, rows, 1)
+
+
+def attention_forward_kernel(
+    q_ref, k_ref, v_ref, mask_ref, out_ref, total_ref, weight_ref, *, head, chunk
+):
     factor = head**-0.5 * math.log2(math.e)
     rows = q_ref.shape[1]
     for h in range(q_ref.shape[2] // head):
@@ -340,16 +369,17 @@
             scores = dot(keys, q_ref[0, part, lanes], NT)
             weights = jnp.exp2(scores * factor + mask_ref[0, :, part])
             total = jnp.sum(weights, axis=0, keepdims=True)
-            summed = dot(values, weights.astype(BF), TN)
+            low = weights.astype(BF)
+            weight_ref[0, 0, h, :, part] = low
+            summed = dot(values, low, TN)
             total_ref[0, 0, h : h + 1, part] = total
             out_ref[0, part, lanes] = (summed / total).T.astype(BF)
 
 
 def attention_backward_kernel(
-    q_ref, k_ref, v_ref, mask_ref, grad_ref, ctx_ref, total_ref, out_ref, dk_sum, dv_sum, *, head, chunk
+    q_ref, k_ref, v_ref, weight_ref, grad_ref, ctx_ref, total_ref, out_ref, dk_sum, dv_sum, *, head, chunk
 ):
     scale = head**-0.5
-    factor = scale * math.log2(math.e)
     rows = q_ref.shape[1]
     for h in range(q_ref.shape[2] // head):
         lanes = slice(h * head, (h + 1) * head)
@@ -358,16 +388,15 @@
         for start in range(0, rows, chunk):
             part = slice(start, start + chunk)
             queries = q_ref[0, part, lanes]
-            scores = dot(keys, queries, NT)
-            weights = jnp.exp2(scores * factor + mask_ref[0, :, part])
+            low = weight_ref[0, 0, h, :, part]
             inverse = 1.0 / total_ref[0, 0, h : h + 1, part]
             grad = grad_ref[0, part, lanes].astype(F32)
             product = (grad * ctx_ref[0, part, lanes].astype(F32)).T
             grad_total = -jnp.sum(product, axis=0, keepdims=True) * inverse
             grad_summed = (grad.T * inverse).astype(BF)
             grad_probs = dot(values, grad_summed)
-            grad_scores = (weights * (grad_probs + grad_total)).astype(BF)
-            dv_part = dot(weights.astype(BF), grad_summed, NT)
+            grad_scores = (low.astype(F32) * (grad_probs + grad_total)).astype(BF)
+            dv_part = dot(low, grad_summed, NT)
             dk_part = dot(grad_scores, queries)
             if start == 0:
                 dv_sum[...] = dv_part
@@ -391,21 +420,23 @@
     own = pl.BlockSpec((1, length, lanes), lambda b, p: (b, 0, p))
     mask = pl.BlockSpec((1, length, length), lambda b, p: (b, 0, 0))
     totals = pl.BlockSpec((1, 1, lanes // head, length), lambda b, p: (b, p, 0, 0))
-    return head, lanes, steps, columns, own, mask, totals
+    weights = pl.BlockSpec((1, 1, lanes // head, length, length), lambda b, p: (b, p, 0, 0, 0))
+    return head, lanes, steps, columns, own, mask, totals, weights
 
 
 def attention_forward(qkv, mask, group):
     count, length, width = qkv.shape
     width = width // 3
-    head, lanes, steps, columns, own, mask_spec, totals = attention_specs(length, width, group)
+    head, lanes, steps, columns, own, mask_spec, totals, weights = attention_specs(length, width, group)
     return pl.pallas_call(
         partial(attention_forward_kernel, head=head, chunk=512),
         grid=(count, steps),
         in_specs=[columns(0), columns(1), columns(2), mask_spec],
-        out_specs=[own, totals],
+        out_specs=[own, totals, weights],
         out_shape=[
             jax.ShapeDtypeStruct((count, length, width // GROUPS), BF),
             jax.ShapeDtypeStruct((count, steps, lanes // head, length), F32),
+            jax.ShapeDtypeStruct((count, steps, lanes // head, length, length), BF),
         ],
         name="attention_forward",
         compiler_params=pltpu.CompilerParams(vmem_limit_bytes=VMEM_BYTES),
@@ -413,21 +444,21 @@
     )(qkv, qkv, qkv, mask)
 
 
-def attention_backward(qkv, mask, grad, context, totals_in, group):
+def attention_backward(qkv, grad, context, totals_in, weights_in, group):
     count, length, width = grad.shape
-    head, lanes, steps, columns, own, mask_spec, totals = attention_specs(length, width, group)
+    head, lanes, steps, columns, own, mask_spec, totals, weights = attention_specs(length, width, group)
     grads = pl.BlockSpec((3, 1, length, lanes), lambda b, p: (0, b, 0, p))
     return pl.pallas_call(
         partial(attention_backward_kernel, head=head, chunk=256),
         grid=(count, steps),
-        in_specs=[columns(0), columns(1), columns(2), mask_spec, columns(0), own, totals],
+        in_specs=[columns(0), columns(1), columns(2), weights, columns(0), own, totals],
         out_specs=grads,
         out_shape=jax.ShapeDtypeStruct((3, count, length, width // GROUPS), BF),
         scratch_shapes=[pltpu.VMEM((length, head), F32)] * 2,
         name="attention_backward",
         compiler_params=pltpu.CompilerParams(vmem_limit_bytes=VMEM_BYTES),
         cost_estimate=cost(26 * count * length * length * width * (LONG if group else SHORT)),
-    )(qkv, qkv, qkv, mask, grad, context, totals_in)
+    )(qkv, qkv, qkv, weights_in, grad, context, totals_in)
 
 
 def attention_mask(segments, globals_pair, randoms):
@@ -565,26 +596,28 @@
     outer = math.sqrt(2 / math.pi)
     cubic = 0.044715
 
+    tile = min(512, wide)
+
     def kernel(_, ins, outs, weights, scratch):
         value, slope = outs
-        for start in range(0, wide, width):
-            columns = slice(start, start + width)
-            u = dot(ins[0][...], weights[0][:, columns]) + ins[1][:, columns]
-            square = u * u
-            half = 0.5 + 0.5 * jnp.tanh(u * (outer + outer * cubic * square))
-            gelu = u * half
-            value[:, columns] = gelu.astype(BF)
-            rest = gelu * (1.0 - half) * (2 * outer + 6 * outer * cubic * square)
-            slope[:, columns] = (half + rest).astype(BF)
+        columns = pl.ds(pl.multiple_of(pl.program_id(0) * tile, tile), tile)
+        u = dot(ins[0][...], weights[0][:, columns]) + ins[1][...]
+        square = u * u
+        half = 0.5 + 0.5 * jnp.tanh(u * (outer + outer * cubic * square))
+        gelu = u * half
+        value[...] = gelu.astype(BF)
+        rest = gelu * (1.0 - half) * (2 * outer + 6 * outer * cubic * square)
+        slope[...] = (half + rest).astype(BF)
 
     return run(
         kernel,
         [w_up],
-        [(normed, (TILE, width), row_block), (bias, (1, wide), fixed_block)],
-        [((rows, wide), BF, (TILE, wide), row_block)] * 2,
-        rows // TILE,
+        [(normed, (rows, width), fixed_block), (bias, (1, tile), column_block)],
+        [((rows, wide), BF, (rows, tile), column_block)] * 2,
+        wide // tile,
         2 * rows * width * wide,
         name="feed_up",
+        stages=4,
     )
 
 
@@ -887,59 +920,52 @@
     mixed, grad_hidden, sum_up, sum_down = clock(
         *feed_down(activated, slope, residual, upstream, params, w_down)
     )
-    mixed = from_whole(grid, mixed.reshape(n, length, width), count)
+    mixed = FromWhole(grid, clock, mixed.reshape(n, length, width), count)
     sum_w_down.step()
     sum_w_up = weight_grad(grid, clock, [(normed2_turned, grad_hidden[None])], "xyz")
     grad_hidden = clock(grad_hidden)
     grad_residual, grad_att, grad_context, sums2 = clock(
         *feed_back(grad_hidden, residual, upstream, params, w_up, w_o)
     )
+    sum_w_up.step()
     sum_w_down.step()
-    sum_w_up.step()
     grad_context = grad_context.reshape(n, length, width)
     grads, sums_qkv = [], []
     for g in range(GROUPS):
         grad_context = clock(grad_context)
-        grad = clock(attention_backward(qkv, mask, grad_context, *attended[g], g)).reshape(3, rows, -1)
+        grad = clock(attention_backward(qkv, grad_context, *attended[g], g)).reshape(3, rows, -1)
         grads.append(grad)
         if g > 0:
             sum_w_up.step()
             sums_qkv[0].step()
         pairs = [(normed1_turned, grad)] + [(context_turned, grad_att[None])] * (g == 0)
-        sums_qkv.append(weight_grad(grid, clock, pairs, "yxz" if g == 0 else "xyz"))
+        sums_qkv.append(weight_grad(grid, clock, pairs, "yxz" if g == 0 else "yzx"))
         if g == 0:
             sum_w_down.step()
             sum_w_up.step()
+            mixed = mixed.result()
+    sums_qkv[1].step()
     steps = rows // TILE
-    swap = grid.group == 2 and count == 2
-    half = steps // 2 if swap else steps
-    place = lax.axis_index(SEQ)
     grads[-1] = clock(grads[-1])
-    grad_inputs, sums1 = clock(
-        *project_back(grads, grad_residual, inputs, params, w_qkv, (1 - place) * half if swap else 0, half)
-    )
+    grad_inputs, sums1 = clock(*project_back(grads, grad_residual, inputs, params, w_qkv, 0, steps))
+    sum_w_up.wait(clock)
     sums_qkv[0].step()
-    sums_qkv[1].step()
-    if swap:
-        got = grid.over_x(grad_inputs)
-        grads[-1] = clock(grads[-1])
-        own, more = clock(*project_back(grads, grad_residual, inputs, params, w_qkv, place * half, half))
-        sums1 = sums1 + more
-        grad_inputs = jnp.stack([jnp.where(place == 0, own, got), jnp.where(place == 0, got, own)])
-    else:
-        grad_inputs = from_whole(grid, grad_inputs.reshape(n, length, width), count)
-    sums_qkv[0].step()
+    grad_inputs = FromWhole(grid, clock, grad_inputs.reshape(n, length, width), count)
+    sums_qkv[1].step(LONG)
     sums_qkv[1].step()
     sums1, sums2, sum_up, sum_down = clock(sums1, sums2, sum_up, sum_down)
     vectors = jnp.concatenate([sums1[:4], sums2[:3], sum_down[:1]])
     vectors = vectors.reshape(8, devices, each).transpose(1, 0, 2).reshape(devices, -1)
     vectors = jnp.concatenate([vectors, sum_up[:1].reshape(devices, -1)], axis=1)
     if grid.cube:
-        vectors = vectors.reshape(grid.nz, 2, 2, 2, -1, 128)
-        vectors = halve(vectors, grid.core, 2, grid.over_core)
-        vectors = halve(vectors, grid.y, 1, grid.over_y)
-        sums_qkv[1].step()
+        vectors = halve(vectors.reshape(grid.nz, 2, 2, 2, -1, 128), grid.core, 2, grid.over_core)
+    sums_qkv[0].step(LONG)
+    if grid.cube:
+        vectors = halve(clock(vectors), grid.y, 1, grid.over_y)
+        sums_qkv[0].wait(clock)
         vectors = halve(clock(vectors), grid.x, 1, grid.over_x)
+    grad_inputs = grad_inputs.result()
+    if grid.cube:
         parts = [pick(vectors, (grid.z + k) % grid.nz, 0) for k in range(grid.nz)]
         vectors = total(parts[:1] + [grid.along_z(part, k) for k, part in enumerate(parts) if k])
     else:

time: 564 us -> 538 us (0.954)
  waiting for transfers between devices: 88.1 us -> 62.8 us
  Pallas kernels: 307 us -> 292 us
  starting transfers between devices: 85.4 us -> 99.8 us
    ppermute x11, waiting for transfers between devices: 30.9 us -> 9.07 us  [over_x(): return lax.ppermute(v, SEQ, [(0, 1), (1, 0)])]
    ppermute x21, starting transfers between devices: 57.2 us -> 74.5 us  [along_z(): lax.ppermute(v, DP, [(i, (i + 4 * k) % self.dp) for i in range(self.dp)])]
    ppermute x7, waiting for transfers between devices: 16.7 us -> 6.13 us  [over_y(): return lax.ppermute(v, DP, [(i, i ^ 2) for i in range(self.dp)])]
    pallas_call x2, Pallas kernels: 54.5 us -> 44.5 us  [attention_backward(): pl.pallas_call(partial(attention_backward_kernel, head=head, chunk=256),...]
    pallas_call x11 -> x10, Pallas kernels: 177 us -> 169 us  [run(): pl.pallas_call(body, grid_spec=pltpu.PrefetchScalarGridSpec(num_scalar_pr...]
    ppermute x21, waiting for transfers between devices: 17.3 us -> 24.7 us  [along_z(): lax.ppermute(v, DP, [(i, (i + 4 * k) % self.dp) for i in range(self.dp)])]
  transfers between devices with their start and end apart: 56 -> 56, of which waited for: 15 -> 14; matrix products, arithmetic and copies ran while one was open for 9% -> 9% of each run, Pallas kernels for 53% -> 51%
where the time goes in v2:
time: 538 us; the launch traced here: 532 us
  Pallas kernels  292 us (54%)
  starting transfers between devices  99.8 us (19%)
  waiting for transfers between devices  62.8 us (12%)
  local copies, waits for them, and re-layouts  36.1 us (7%)
  other arithmetic  25.6 us (5%)
  between operations  15.4 us (3%)
    pallas_call x10, Pallas kernels, run(): pl.pallas_call(body, grid_spec=pltpu.PrefetchScalarGridSpec(num_scalar_pr...  169 us
    ppermute x21, starting transfers between devices, along_z(): lax.ppermute(v, DP, [(i, (i + 4 * k) % self.dp) for i in range(self.dp)])  74.5 us
    pallas_call x12, Pallas kernels, split_sum(): pl.pallas_call(kernel, grid_spec=pltpu.PrefetchScalarGridSpec(num_scalar_...  48.7 us
    pallas_call x2, Pallas kernels, attention_backward(): pl.pallas_call(partial(attention_backward_kernel, head=head, chunk=256),...  44.5 us
    pallas_call x2, Pallas kernels, attention_forward(): pl.pallas_call(partial(attention_forward_kernel, head=head, chunk=512), g...  30.4 us
    ppermute x21, waiting for transfers between devices, along_z(): lax.ppermute(v, DP, [(i, (i + 4 * k) % self.dp) for i in range(self.dp)])  24.7 us
    ppermute x11, starting transfers between devices, over_x(): return lax.ppermute(v, SEQ, [(0, 1), (1, 0)])  17.4 us
    ppermute x2, waiting for transfers between devices, over_xy(): return lax.ppermute(v, BOTH, pairs)  10.8 us
  transfers between devices with their start and end apart: 56, of which 14 were waited for; matrix products, arithmetic and copies ran while one was open for 9% of the time, Pallas kernels for 51%

profile of v2, /device:TPU:0, one launch (start us, length us, event | category | flops | bytes accessed | tf_op | source)
XLA Modules:
  0.0 532.1 jit_solution(9570780831103850098)
XLA Ops:
  24.8 8.6 %collective-permute-done.4 = bf16[1,32,2176]{2,1,0:T(8,128)(2,1)S(1)} collective-permute-done((bf16[1,32,2176]{2,1,0:T(8,128)(2,1)S(1)}, bf16[1,32,2176]{2,1,0:T(8,128)(2,1)S(1)}, u32[]{:S(2)}, u32[]{:S(2)}) %collective-permute-start.4) | collective-permute-done | bytes 139296 | tf_op jit(solution)/shard_map/ppermute | solution.py:61
  58.3 7.2 %collective-permute-start = (bf16[1,32,4096]{2,1,0:T(8,128)(2,1)S(1)}, bf16[1,32,4096]{2,1,0:T(8,128)(2,1)}, u32[]{:S(2)}, u32[]{:S(2)}) collective-permute-start(bf16[1,32,4096]{2,1,0:T(8,128)(2,1)S(1)} %bitcast.260), channel_id=1, source_target_pairs={{0,8},{2,10},{4,12},{6,14},{8,16},{10,18},{12,20},{14,22},{16,24},... | collective-permute-start | bytes 786440 | tf_op jit(solution)/shard_map/ppermute | solution.py:61
  65.5 9.6 %collective-permute-done.7.refs_3_.refs_11_.refs_2_.refs_10_ = bf16[4,32,2176]{2,1,0:T(8,128)(2,1)S(1)} collective-permute-done((bf16[4,32,2176]{2,1,0:T(8,128)(2,1)S(1)}, bf16[4,32,2176]{2,1,0:T(8,128)(2,1)S(1)}, u32[]{:S(2)}, u32[]{:S(2)}) %collective-permute-start.7) | collective-permute-done | bytes 557088 | tf_op jit(solution)/shard_map/ppermute | solution.py:55
  87.4 8.0 %all-gather.7.cloned.1.call-done = bf16[1024,2048]{1,0:T(8,128)(2,1)} async-done(((bf16[32,2048]{1,0:T(8,128)(2,1)}), bf16[1024,2048]{1,0:T(8,128)(2,1)}) %all-gather.7.cloned.1.call-update) | async-done | bytes 4194320 | tf_op jit(solution)/shard_map/all_gather | solution.py:102
  95.4 15.3 %project_in.1 = (bf16[1024,3072]{1,0:T(8,128)(2,1)}, bf16[1024,1024]{1,0:T(8,128)(2,1)}, f32[16,1024]{1,0:T(8,128)}) custom-call(s32[96]{0:T(128)} %stack.141.at, bf16[32,32,2048]{2,1,0:T(8,128)(2,1)} %bitcast.228, bf16[4,32,2176]{2,1,0:T(8,128)(2,1)} %copy-done.4, bf16[4,32,2176]{2,1,0:T(8,128)(2,1)} %copy-done.8, bf16[4,32,2176]{2,1,0:T(8,128)(2,1)} %copy-done.7, ...), custom_call_target="tpu_custom_call" | custom-call | flops 322122560 | tf_op jit(solution)/shard_map/project_in/pallas_call | solution.py:213
  110.7 15.2 %attention_forward.2 = (bf16[1,1024,512]{2,1,0:T(8,128)(2,1)}, f32[1,4,2,1024]{3,2,1,0:T(2,128)}, bf16[1,4,2,1024,1024]{4,3,2,1,0:T(8,128)(2,1)}) custom-call(bf16[1,1024,3072]{2,1,0:T(8,128)(2,1)} %bitcast.198, bf16[1,1024,3072]{2,1,0:T(8,128)(2,1)} %bitcast.199, bf16[1,1024,3072]{2,1,0:T(8,128)(2,1)} %bitcast.200, f32[1,1024,1024]{2,1,0:T(8,128)} %and_select_fusion.mask_ref), custom_call_target="tpu_custom_call" | custom-call | flops 6442450944 | tf_op jit(solution)/shard_map/attention_forward/pallas_call | solution.py:431
  125.8 15.3 %attention_forward.3 = (bf16[1,1024,512]{2,1,0:T(8,128)(2,1)}, f32[1,4,2,1024]{3,2,1,0:T(2,128)}, bf16[1,4,2,1024,1024]{4,3,2,1,0:T(8,128)(2,1)}) custom-call(bf16[1,1024,3072]{2,1,0:T(8,128)(2,1)} %bitcast.201, bf16[1,1024,3072]{2,1,0:T(8,128)(2,1)} %bitcast.202, bf16[1,1024,3072]{2,1,0:T(8,128)(2,1)} %bitcast.203, f32[1,1024,1024]{2,1,0:T(8,128)} %and_select_fusion.mask_ref), custom_call_target="tpu_custom_call" | custom-call | flops 6442450944 | tf_op jit(solution)/shard_map/attention_forward/pallas_call | solution.py:431
  150.9 11.2 %project_out.1 = (f32[1024,1024]{1,0:T(8,128)}, bf16[1024,1024]{1,0:T(8,128)(2,1)}, bf16[1024,1024]{1,0:T(8,128)(2,1)}, bf16[1024,1024]{1,0:T(8,128)(2,1)}) custom-call(s32[32]{0:T(128)} %stack.140.at, bf16[4,32,2176]{2,1,0:T(8,128)(2,1)} %copy-done.4, bf16[4,32,2176]{2,1,0:T(8,128)(2,1)} %copy-done.8, bf16[4,32,2176]{2,1,0:T(8,128)(2,1)} %copy-done.7, ...), custom_call_target="tpu_custom_call" | custom-call | flops 107374184 | tf_op jit(solution)/shard_map/project_out/pallas_call | solution.py:213
  162.1 24.2 %feed_up.1 = (bf16[1024,4096]{1,0:T(8,128)(2,1)}, bf16[1024,4096]{1,0:T(8,128)(2,1)}) custom-call(s32[32]{0:T(128)} %stack.140.at, bf16[4,32,4096]{2,1,0:T(8,128)(2,1)} %pad_maximum_fusion.4.refs_0_, bf16[4,32,4096]{2,1,0:T(8,128)(2,1)} %collective-permute-done.17.refs_1_, bf16[4,32,4096]{2,1,0:T(8,128)(2,1)} %collective-permute-done.10.refs_2_, ...), custom_call_target="tpu_custom_call" | custom-call | flops 429496736 | tf_op jit(solution)/shard_map/feed_up/pallas_call | solution.py:213
  191.3 15.9 %weight_grad_turned.1 = (bf16[16,1024,128]{2,1,0:T(8,128)(2,1)}, bf16[16,1024,128]{2,1,0:T(8,128)(2,1)}) custom-call(s32[1]{0:T(128)} %bitcast.48.at, bf16[1024,1024]{1,0:T(8,128)(2,1)} %copy.64.refs_0_, bf16[1024,4096]{1,0:T(8,128)(2,1)} %get-tuple-element.349.refs_1_), custom_call_target="tpu_custom_call" | custom-call | flops 429496736 | tf_op jit(solution)/shard_map/weight_grad_turned/pallas_call | solution.py:213
  207.2 30.3 %feed_down.1 = (bf16[1024,1024]{1,0:T(8,128)(2,1)}, bf16[1024,4096]{1,0:T(8,128)(2,1)}, f32[8,4096]{1,0:T(8,128)}, f32[8,1024]{1,0:T(8,128)}) custom-call(s32[32]{0:T(128)} %iota_multiply_fusion.at, bf16[32,128,1024]{2,1,0:T(8,128)(2,1)} %bitcast.271, bf16[1024,4096]{1,0:T(8,128)(2,1)} %get-tuple-element.349.refs_1_, ...), custom_call_target="tpu_custom_call" | custom-call | flops 85899345920 | tf_op jit(solution)/shard_map/feed_down/pallas_call | solution.py:213
  237.6 6.5 %sum_y.4 = (bf16[8192,128]{1,0:T(8,128)(2,1)}, bf16[8192,128]{1,0:T(8,128)(2,1)}) custom-call(s32[2]{0:T(128)} %pad_add_fusion.at, bf16[2,8192,128]{2,1,0:T(8,128)(2,1)} %bitcast.222, bf16[2,8192,128]{2,1,0:T(8,128)(2,1)} %bitcast.223, bf16[2,8192,128]{2,1,0:T(8,128)(2,1)} %bitcast.63.refs_2_.refs_3_, bf16[2,8192,128]{2,1,0:T(8,128)(2,1)} %bitcast.63.refs_2_.refs_3_), custom_call_target="tpu_custom_call" | custom-call | flops 1000000000 | tf_op jit(solution)/shard_map/sum_y/pallas_call | solution.py:259
  245.8 14.2 %weight_grad_4096.1 = (bf16[512,4096]{1,0:T(8,128)(2,1)}, bf16[512,4096]{1,0:T(8,128)(2,1)}) custom-call(s32[1]{0:T(128)} %bitcast.48.at, bf16[1024,1024]{1,0:T(8,128)(2,1)} %get-tuple-element.369.refs_0_, bf16[1,1024,4096]{2,1,0:T(8,128)(2,1)} %bitcast.234), custom_call_target="tpu_custom_call" | custom-call | flops 429496736 | tf_op jit(solution)/shard_map/weight_grad_4096/pallas_call | solution.py:213
  260.3 23.2 %feed_back.1 = (f32[1024,1024]{1,0:T(8,128)}, bf16[1024,1024]{1,0:T(8,128)(2,1)}, bf16[1024,1024]{1,0:T(8,128)(2,1)}, f32[8,1024]{1,0:T(8,128)}) custom-call(s32[64]{0:T(128)} %stack.149.at, bf16[4,32,4096]{2,1,0:T(8,128)(2,1)} %pad_maximum_fusion.4.refs_0_, bf16[4,32,4096]{2,1,0:T(8,128)(2,1)} %collective-permute-done.17.refs_1_, ...), custom_call_target="tpu_custom_call" | custom-call | flops 53687091200 | tf_op jit(solution)/shard_map/feed_back/pallas_call | solution.py:213
  283.5 6.6 %sum_x.4 = (bf16[256,4096]{1,0:T(8,128)(2,1)}, bf16[256,4096]{1,0:T(8,128)(2,1)}) custom-call(s32[2]{0:T(128)} %pad_add_fusion.1.at, bf16[2,256,4096]{2,1,0:T(8,128)(2,1)} %bitcast.220, bf16[2,256,4096]{2,1,0:T(8,128)(2,1)} %bitcast.221, bf16[2,256,4096]{2,1,0:T(8,128)(2,1)} %bitcast.69.refs_2_.refs_3_, bf16[2,256,4096]{2,1,0:T(8,128)(2,1)} %bitcast.69.refs_2_.refs_3_), custom_call_target="tpu_custom_call" | custom-call | flops 1000000000 | tf_op jit(solution)/shard_map/sum_x/pallas_call | solution.py:259
  300.5 9.4 %collective-permute-start.27 = (bf16[2,1024,128]{2,1,0:T(8,128)(2,1)}, bf16[2,1024,128]{2,1,0:T(8,128)(2,1)S(1)}, u32[]{:S(2)}, u32[]{:S(2)}) collective-permute-start(bf16[2,1024,128]{2,1,0:T(8,128)(2,1)} %bitcast.292), channel_id=1, source_target_pairs={{0,8},{2,10},{4,12},{6,14},{8,16},{10,18},{12,20},{14,22},{16,24},... | collective-permute-start | bytes 1572872 | tf_op jit(solution)/shard_map/ppermute | solution.py:61
  313.9 22.2 %attention_backward.2 = bf16[3,1,1024,512]{3,2,1,0:T(8,128)(2,1)} custom-call(bf16[1,1024,3072]{2,1,0:T(8,128)(2,1)} %bitcast.204, bf16[1,1024,3072]{2,1,0:T(8,128)(2,1)} %bitcast.205, bf16[1,1024,3072]{2,1,0:T(8,128)(2,1)} %bitcast.206, bf16[1,4,2,1024,1024]{4,3,2,1,0:T(8,128)(2,1)} %get-tuple-element.406.weight_ref, bf16[1,1024,1024]{2,1,0:T(8,128)(2,1)} %bitcast.250, ...), custom_call_target="tpu_custom_call" | custom-call | flops 1395864320 | tf_op jit(solution)/shard_map/attention_backward/pallas_call | solution.py:451
  336.1 10.9 %weight_grad_2560.1 = (bf16[512,2560]{1,0:T(8,128)(2,1)}, bf16[512,2560]{1,0:T(8,128)(2,1)}) custom-call(s32[1]{0:T(128)} %bitcast.48.at, bf16[1024,1024]{1,0:T(8,128)(2,1)} %get-tuple-element.466.refs_0_, bf16[3,1024,512]{2,1,0:T(8,128)(2,1)} %bitcast.218, bf16[1024,1024]{1,0:T(8,128)(2,1)} %get-tuple-element.419.refs_2_, bf16[1,1024,1024]{2,1,0:T(8,128)(2,1)} %bitcast.252), custom_call_target="tpu_custom_call" | custom-call | flops 268435456 | tf_op jit(solution)/shard_map/weight_grad_2560/pallas_call | solution.py:213
  360.9 22.3 %attention_backward.3 = bf16[3,1,1024,512]{3,2,1,0:T(8,128)(2,1)} custom-call(bf16[1,1024,3072]{2,1,0:T(8,128)(2,1)} %bitcast.207, bf16[1,1024,3072]{2,1,0:T(8,128)(2,1)} %bitcast.208, bf16[1,1024,3072]{2,1,0:T(8,128)(2,1)} %bitcast.209, bf16[1,4,2,1024,1024]{4,3,2,1,0:T(8,128)(2,1)} %get-tuple-element.441.weight_ref, bf16[1,1024,1024]{2,1,0:T(8,128)(2,1)} %bitcast.251, ...), custom_call_target="tpu_custom_call" | custom-call | flops 139586437120 | tf_op jit(solution)/shard_map/attention_backward/pallas_call | solution.py:451
  394.8 7.1 %weight_grad_1536.1 = (bf16[512,1536]{1,0:T(8,128)(2,1)}, bf16[512,1536]{1,0:T(8,128)(2,1)}) custom-call(s32[1]{0:T(128)} %bitcast.48.at, bf16[1024,1024]{1,0:T(8,128)(2,1)} %get-tuple-element.466.refs_0_, bf16[3,1024,512]{2,1,0:T(8,128)(2,1)} %bitcast.230), custom_call_target="tpu_custom_call" | custom-call | flops 161061280 | tf_op jit(solution)/shard_map/weight_grad_1536/pallas_call | solution.py:213
  411.8 10.3 %collective-permute-start.36 = (bf16[32,4096]{1,0:T(8,128)(2,1)}, bf16[32,4096]{1,0:T(8,128)(2,1)S(1)}, u32[]{:S(2)}, u32[]{:S(2)}) collective-permute-start(bf16[32,4096]{1,0:T(8,128)(2,1)} %get-tuple-element.493), channel_id=1, source_target_pairs={{0,8},{2,10},{4,12},{6,14},{8,16},{10,18},{12,20},{14,22},{16,24},... | collective-permute-start | bytes 786440 | tf_op jit(solution)/shard_map/ppermute | solution.py:61
  428.2 16.4 %project_back.1 = (bf16[1024,1024]{1,0:T(8,128)(2,1)}, f32[8,1024]{1,0:T(8,128)}) custom-call(s32[65]{0:T(128)} %stack.158.at, bf16[32,32,2048]{2,1,0:T(8,128)(2,1)} %bitcast.229, bf16[4,32,2176]{2,1,0:T(8,128)(2,1)} %copy-done.4, bf16[4,32,2176]{2,1,0:T(8,128)(2,1)} %copy-done.8, bf16[4,32,2176]{2,1,0:T(8,128)(2,1)} %copy-done.7, ...), custom_call_target="tpu_custom_call" | custom-call | flops 322122560 | tf_op jit(solution)/shard_map/project_back/pallas_call | solution.py:213
  453.6 9.2 %collective-permute-start.39 = (bf16[2,32,1536]{2,1,0:T(8,128)(2,1)}, bf16[2,32,1536]{2,1,0:T(8,128)(2,1)S(1)}, u32[]{:S(2)}, u32[]{:S(2)}) collective-permute-start(bf16[2,32,1536]{2,1,0:T(8,128)(2,1)} %bitcast.295), channel_id=1, source_target_pairs={{0,8},{2,10},{4,12},{6,14},{8,16},{10,18},{12,20},{14,22},{16,24},... | collective-permute-start | bytes 589832 | tf_op jit(solution)/shard_map/ppermute | solution.py:61
  490.0 6.6 %collective-permute-start.45 = (bf16[32,2560]{1,0:T(8,128)(2,1)}, bf16[32,2560]{1,0:T(8,128)(2,1)S(1)}, u32[]{:S(2)}, u32[]{:S(2)}) collective-permute-start(bf16[32,2560]{1,0:T(8,128)(2,1)} %get-tuple-element.540), channel_id=1, source_target_pairs={{0,8},{2,10},{4,12},{6,14},{8,16},{10,18},{12,20},{14,22},{16,24},... | collective-permute-start | bytes 491528 | tf_op jit(solution)/shard_map/ppermute | solution.py:61
  (294 shorter events, 191.0 us)
Async XLA Ops:
  7.4 88.0 %all-gather.7.cloned.1.call-start = ((), (), s32[]{:S(2)}) async-start(), calls=%async_computation.1 | async-start | bytes 4325376 | tf_op jit(solution)/shard_map/all_gather | solution.py:102
  9.2 198.0 %all-gather.5.cloned.1.call-start = ((), (), s32[]{:S(2)}) async-start(), calls=%async_computation | async-start | bytes 8650752 | tf_op jit(solution)/shard_map/all_gather | solution.py:102
  12.2 27.4 %collective-permute-start.6 = (bf16[512,1024]{1,0:T(8,128)(2,1)}, bf16[512,1024]{1,0:T(8,128)(2,1)}, u32[]{:S(2)}, u32[]{:S(2)}) collective-permute-start(bf16[512,1024]{1,0:T(8,128)(2,1)} %dynamic-slice_bitcast_fusion.3), channel_id=1, source_target_pairs={{0,1},{1,0},{2,3},{3,2},{4,5},{5,4},{6,7},{7,6},{8,9},{9,8},{10,11... | collective-permute-start | bytes 3145736 | tf_op jit(solution)/shard_map/ppermute | solution.py:48
  20.2 55.4 %collective-permute-start.2 = (bf16[1,32,4096]{2,1,0:T(8,128)(2,1)S(1)}, bf16[1,32,4096]{2,1,0:T(8,128)(2,1)S(1)}, u32[]{:S(2)}, u32[]{:S(2)}) collective-permute-start(bf16[1,32,4096]{2,1,0:T(8,128)(2,1)S(1)} %bitcast.258), channel_id=1, source_target_pairs={{0,24},{2,26},{4,28},{6,30},{8,0},{10,2},{12,4},{14,6},{16,8},{18,... | collective-permute-start | bytes 786440 | tf_op jit(solution)/shard_map/ppermute | solution.py:61
  23.3 52.3 %collective-permute-start.1 = (bf16[1,32,4096]{2,1,0:T(8,128)(2,1)S(1)}, bf16[1,32,4096]{2,1,0:T(8,128)(2,1)}, u32[]{:S(2)}, u32[]{:S(2)}) collective-permute-start(bf16[1,32,4096]{2,1,0:T(8,128)(2,1)S(1)} %bitcast.259), channel_id=1, source_target_pairs={{0,16},{2,18},{4,20},{6,22},{8,24},{10,26},{12,28},{14,30},{16,0},... | collective-permute-start | bytes 786440 | tf_op jit(solution)/shard_map/ppermute | solution.py:61
  45.8 29.2 %collective-permute-start.7 = (bf16[4,32,2176]{2,1,0:T(8,128)(2,1)S(1)}, bf16[4,32,2176]{2,1,0:T(8,128)(2,1)S(1)}, u32[]{:S(2)}, u32[]{:S(2)}) collective-permute-start(bf16[4,32,2176]{2,1,0:T(8,128)(2,1)S(1)} %pad_maximum_fusion.5.refs_1_.refs_9_.refs_0_.refs_8_), channel_id=1, source_target_pairs={{0,5},{1,4},{2,7},{3,6},{4,1},{5,0},{6,3},{7,2},{8,13},{9,12},{10,... | collective-permute-start | bytes 1671176 | tf_op jit(solution)/shard_map/ppermute | solution.py:55
  83.4 57.7 %collective-permute-start.12 = (bf16[4,32,4096]{2,1,0:T(8,128)(2,1)}, bf16[4,32,4096]{2,1,0:T(8,128)(2,1)}, u32[]{:S(2)}, u32[]{:S(2)}) collective-permute-start(bf16[4,32,4096]{2,1,0:T(8,128)(2,1)} %pad_maximum_fusion.4.refs_0_), channel_id=1, source_target_pairs={{0,4},{2,6},{4,0},{6,2},{8,12},{10,14},{12,8},{14,10},{16,20},{18,... | collective-permute-start | bytes 3145736 | tf_op jit(solution)/shard_map/ppermute | solution.py:51
  83.5 57.6 %collective-permute-start.11 = (bf16[4,32,4096]{2,1,0:T(8,128)(2,1)}, bf16[4,32,4096]{2,1,0:T(8,128)(2,1)}, u32[]{:S(2)}, u32[]{:S(2)}) collective-permute-start(bf16[4,32,4096]{2,1,0:T(8,128)(2,1)} %pad_maximum_fusion.4.refs_0_), channel_id=1, source_target_pairs={{0,1},{1,0},{2,3},{3,2},{4,5},{5,4},{6,7},{7,6},{8,9},{9,8},{10,11... | collective-permute-start | bytes 3145736 | tf_op jit(solution)/shard_map/ppermute | solution.py:48
  87.3 55.0 %collective-permute-start.10 = (bf16[4,32,4096]{2,1,0:T(8,128)(2,1)}, bf16[4,32,4096]{2,1,0:T(8,128)(2,1)}, u32[]{:S(2)}, u32[]{:S(2)}) collective-permute-start(bf16[4,32,4096]{2,1,0:T(8,128)(2,1)} %pad_maximum_fusion.4.refs_0_), channel_id=1, source_target_pairs={{0,5},{1,4},{2,7},{3,6},{4,1},{5,0},{6,3},{7,2},{8,13},{9,12},{10,... | collective-permute-start | bytes 3145736 | tf_op jit(solution)/shard_map/ppermute | solution.py:55
  144.4 41.9 %collective-permute-start.21 = (bf16[512,1024]{1,0:T(8,128)(2,1)}, bf16[512,1024]{1,0:T(8,128)(2,1)S(1)}, u32[]{:S(2)}, u32[]{:S(2)}) collective-permute-start(bf16[512,1024]{1,0:T(8,128)(2,1)} %dynamic-slice_bitcast_fusion.2), channel_id=1, source_target_pairs={{0,1},{1,0},{2,3},{3,2},{4,5},{5,4},{6,7},{7,6},{8,9},{9,8},{10,11... | collective-permute-start | bytes 3145736 | tf_op jit(solution)/shard_map/ppermute | solution.py:48
  207.2 30.4 %collective-permute-start.23 = (bf16[2,4,2,1024,128]{4,3,2,1,0:T(8,128)(2,1)}, bf16[2,4,2,1024,128]{4,3,2,1,0:T(8,128)(2,1)}, u32[]{:S(2)}, u32[]{:S(2)}) collective-permute-start(bf16[2,4,2,1024,128]{4,3,2,1,0:T(8,128)(2,1)} %bitcast.273), channel_id=1, source_target_pairs={{0,2},{2,0},{4,6},{6,4},{8,10},{10,8},{12,14},{14,12},{16,18},{18,... | collective-permute-start | bytes 12582920 | tf_op jit(solution)/shard_map/ppermute | solution.py:58
  244.1 50.8 %collective-permute-start.26 = (bf16[4,2,1024,128]{3,2,1,0:T(8,128)(2,1)}, bf16[4,2,1024,128]{3,2,1,0:T(8,128)(2,1)S(1)}, u32[]{:S(2)}, u32[]{:S(2)}) collective-permute-start(bf16[4,2,1024,128]{3,2,1,0:T(8,128)(2,1)} %bitcast.276), channel_id=1, source_target_pairs={{0,4},{2,6},{4,0},{6,2},{8,12},{10,14},{12,8},{14,10},{16,20},{18,... | collective-permute-start | bytes 6291464 | tf_op jit(solution)/shard_map/ppermute | solution.py:51
  290.1 61.9 %collective-permute-start.25 = (bf16[2,4,32,4096]{3,2,1,0:T(8,128)(2,1)}, bf16[2,4,32,4096]{3,2,1,0:T(8,128)(2,1)}, u32[]{:S(2)}, u32[]{:S(2)}) collective-permute-start(bf16[2,4,32,4096]{3,2,1,0:T(8,128)(2,1)} %bitcast.275), channel_id=1, source_target_pairs={{0,1},{1,0},{2,3},{3,2},{4,5},{5,4},{6,7},{7,6},{8,9},{9,8},{10,11... | collective-permute-start | bytes 6291464 | tf_op jit(solution)/shard_map/ppermute | solution.py:48
  292.4 68.2 %collective-permute-start.22 = (bf16[512,1024]{1,0:T(8,128)(2,1)}, bf16[512,1024]{1,0:T(8,128)(2,1)S(1)}, u32[]{:S(2)}, u32[]{:S(2)}) collective-permute-start(bf16[512,1024]{1,0:T(8,128)(2,1)} %dynamic-slice_bitcast_fusion.1), channel_id=1, source_target_pairs={{0,1},{1,0},{2,3},{3,2},{4,5},{5,4},{6,7},{7,6},{8,9},{9,8},{10,11... | collective-permute-start | bytes 3145736 | tf_op jit(solution)/shard_map/ppermute | solution.py:48
  300.5 46.5 %collective-permute-start.27 = (bf16[2,1024,128]{2,1,0:T(8,128)(2,1)}, bf16[2,1024,128]{2,1,0:T(8,128)(2,1)S(1)}, u32[]{:S(2)}, u32[]{:S(2)}) collective-permute-start(bf16[2,1024,128]{2,1,0:T(8,128)(2,1)} %bitcast.292), channel_id=1, source_target_pairs={{0,8},{2,10},{4,12},{6,14},{8,16},{10,18},{12,20},{14,22},{16,24},... | collective-permute-start | bytes 1572872 | tf_op jit(solution)/shard_map/ppermute | solution.py:61
  309.9 37.2 %collective-permute-start.28 = (bf16[2,1024,128]{2,1,0:T(8,128)(2,1)}, bf16[2,1024,128]{2,1,0:T(8,128)(2,1)S(1)}, u32[]{:S(2)}, u32[]{:S(2)}) collective-permute-start(bf16[2,1024,128]{2,1,0:T(8,128)(2,1)} %bitcast.291), channel_id=1, source_target_pairs={{0,16},{2,18},{4,20},{6,22},{8,24},{10,26},{12,28},{14,30},{16,0},... | collective-permute-start | bytes 1572872 | tf_op jit(solution)/shard_map/ppermute | solution.py:61
  311.0 36.1 %collective-permute-start.29 = (bf16[2,1024,128]{2,1,0:T(8,128)(2,1)}, bf16[2,1024,128]{2,1,0:T(8,128)(2,1)S(1)}, u32[]{:S(2)}, u32[]{:S(2)}) collective-permute-start(bf16[2,1024,128]{2,1,0:T(8,128)(2,1)} %bitcast.290), channel_id=1, source_target_pairs={{0,24},{2,26},{4,28},{6,30},{8,0},{10,2},{12,4},{14,6},{16,8},{18,... | collective-permute-start | bytes 1572872 | tf_op jit(solution)/shard_map/ppermute | solution.py:61
  347.0 42.5 %collective-permute-start.30 = (bf16[2,2,4,32,2560]{4,3,2,1,0:T(8,128)(2,1)}, bf16[2,2,4,32,2560]{4,3,2,1,0:T(8,128)(2,1)}, u32[]{:S(2)}, u32[]{:S(2)}) collective-permute-start(bf16[2,2,4,32,2560]{4,3,2,1,0:T(8,128)(2,1)} %bitcast.274), channel_id=1, source_target_pairs={{0,2},{2,0},{4,6},{6,4},{8,10},{10,8},{12,14},{14,12},{16,18},{18,... | collective-permute-start | bytes 7864328 | tf_op jit(solution)/shard_map/ppermute | solution.py:58
  360.6 24.8 %collective-permute-start.31 = (bf16[4,32,4096]{2,1,0:T(8,128)(2,1)}, bf16[4,32,4096]{2,1,0:T(8,128)(2,1)S(1)}, u32[]{:S(2)}, u32[]{:S(2)}) collective-permute-start(bf16[4,32,4096]{2,1,0:T(8,128)(2,1)} %bitcast.279), channel_id=1, source_target_pairs={{0,4},{2,6},{4,0},{6,2},{8,12},{10,14},{12,8},{14,10},{16,20},{18,... | collective-permute-start | bytes 3145736 | tf_op jit(solution)/shard_map/ppermute | solution.py:51
  401.9 42.9 %collective-permute-start.35 = (bf16[2,4,32,2560]{3,2,1,0:T(8,128)(2,1)}, bf16[2,4,32,2560]{3,2,1,0:T(8,128)(2,1)S(1)}, u32[]{:S(2)}, u32[]{:S(2)}) collective-permute-start(bf16[2,4,32,2560]{3,2,1,0:T(8,128)(2,1)} %bitcast.278), channel_id=1, source_target_pairs={{0,4},{2,6},{4,0},{6,2},{8,12},{10,14},{12,8},{14,10},{16,20},{18,... | collective-permute-start | bytes 3932168 | tf_op jit(solution)/shard_map/ppermute | solution.py:51
  410.3 40.1 %collective-permute-start.34 = (bf16[4,2,32,1536]{3,2,1,0:T(8,128)(2,1)}, bf16[4,2,32,1536]{3,2,1,0:T(8,128)(2,1)}, u32[]{:S(2)}, u32[]{:S(2)}) collective-permute-start(bf16[4,2,32,1536]{3,2,1,0:T(8,128)(2,1)} %bitcast.284), channel_id=1, source_target_pairs={{0,4},{2,6},{4,0},{6,2},{8,12},{10,14},{12,8},{14,10},{16,20},{18,... | collective-permute-start | bytes 2359304 | tf_op jit(solution)/shard_map/ppermute | solution.py:51
  411.8 32.9 %collective-permute-start.36 = (bf16[32,4096]{1,0:T(8,128)(2,1)}, bf16[32,4096]{1,0:T(8,128)(2,1)S(1)}, u32[]{:S(2)}, u32[]{:S(2)}) collective-permute-start(bf16[32,4096]{1,0:T(8,128)(2,1)} %get-tuple-element.493), channel_id=1, source_target_pairs={{0,8},{2,10},{4,12},{6,14},{8,16},{10,18},{12,20},{14,22},{16,24},... | collective-permute-start | bytes 786440 | tf_op jit(solution)/shard_map/ppermute | solution.py:61
  449.2 30.5 %collective-permute-start.43 = (bf16[4,32,2560]{2,1,0:T(8,128)(2,1)}, bf16[4,32,2560]{2,1,0:T(8,128)(2,1)}, u32[]{:S(2)}, u32[]{:S(2)}) collective-permute-start(bf16[4,32,2560]{2,1,0:T(8,128)(2,1)} %bitcast.289), channel_id=1, source_target_pairs={{0,1},{1,0},{2,3},{3,2},{4,5},{5,4},{6,7},{7,6},{8,9},{9,8},{10,11... | collective-permute-start | bytes 1966088 | tf_op jit(solution)/shard_map/ppermute | solution.py:48
  469.3 42.1 %collective-permute-start.33 = (bf16[512,1024]{1,0:T(8,128)(2,1)}, bf16[512,1024]{1,0:T(8,128)(2,1)S(1)}, u32[]{:S(2)}, u32[]{:S(2)}) collective-permute-start(bf16[512,1024]{1,0:T(8,128)(2,1)} %dynamic-slice_bitcast_fusion), channel_id=1, source_target_pairs={{0,1},{1,0},{2,3},{3,2},{4,5},{5,4},{6,7},{7,6},{8,9},{9,8},{10,11... | collective-permute-start | bytes 3145736 | tf_op jit(solution)/shard_map/ppermute | solution.py:48
  (82 other events, 1003.0 us)
Sparse Core Ops, SparseCore 0:
  11.8 83.5 all-gather.6
  98.4 97.1 all-gather.4

commit v3 on v2

--- a/solution.py
+++ b/solution.py
@@ -805,14 +805,14 @@
     return Scatter(grid, clock, kept.reshape(shape), sent.reshape(shape), order)
 
 
-def weight_grad_turned(grid, clock, turned, right, order):
-    features, rows = turned.shape
+def weight_grad_turned(grid, clock, left, right, order):
+    rows, features = left.shape
     each = right.shape[1] // (grid.nz * 8)
     places, shape = leading(grid, order)
 
     def kernel(scalars, ins, outs, weights, scratch):
         first = scalars[0] == 0
-        value = dot(ins[0][...], ins[1][...]).astype(BF)
+        value = dot(ins[0][...], ins[1][...], TN).astype(BF)
 
         def store(low, high):
             for (z, y, x), at in places:
@@ -831,11 +831,11 @@
 
     tile = min(256, features)
     shape += (features, each)
-    turned, right = clock(turned, right)
+    left, right = clock(left, right)
     kept, sent = run(
         kernel,
         [],
-        [(turned, (tile, rows), row_block), (right, right.shape, fixed_block)],
+        [(left, (rows, tile), column_block), (right, right.shape, fixed_block)],
         [((grid.nz * 4, features, each), BF, (grid.nz * 4, tile, each), lambda i: (0, i, 0))] * 2,
         features // tile,
         2 * rows * features * right.shape[1],
@@ -905,15 +905,15 @@
         qkv, mask = clock(qkv, mask)
         attended.append(clock(*attention_forward(qkv, mask, g)))
     contexts = [a[0].reshape(rows, -1) for a in attended]
-    w_up, w_down = columns_of((third.pieces(clock), 0, wide)), columns_of((fourth, 0, width))
     contexts[0] = clock(contexts[0])
     residual, normed2, normed2_turned, context_turned = clock(*project_out(contexts, inputs, params, w_o))
+    w_up, w_down = columns_of((third.pieces(clock), 0, wide)), columns_of((fourth, 0, width))
+    normed2 = clock(normed2)
     bias_up = params[8 : 8 + wide // width].reshape(-1, devices, each).transpose(1, 0, 2).reshape(1, -1)
     activated, slope = clock(*feed_up(normed2, w_up, bias_up))
 
-    upstream_turned = upstream.T
     if grid.cube:
-        sum_w_down = weight_grad_turned(grid, clock, upstream_turned, activated, "yzx")
+        sum_w_down = weight_grad_turned(grid, clock, upstream, activated, "yzx")
     else:
         sum_w_down = Summed(dot(activated, upstream, TN))
     activated = clock(activated)
@@ -927,6 +927,7 @@
     grad_residual, grad_att, grad_context, sums2 = clock(
         *feed_back(grad_hidden, residual, upstream, params, w_up, w_o)
     )
+    mixed = mixed.result()
     sum_w_up.step()
     sum_w_down.step()
     grad_context = grad_context.reshape(n, length, width)
@@ -939,33 +940,33 @@
             sum_w_up.step()
             sums_qkv[0].step()
         pairs = [(normed1_turned, grad)] + [(context_turned, grad_att[None])] * (g == 0)
-        sums_qkv.append(weight_grad(grid, clock, pairs, "yxz" if g == 0 else "yzx"))
+        sums_qkv.append(weight_grad(grid, clock, pairs, "yxz"))
         if g == 0:
             sum_w_down.step()
             sum_w_up.step()
-            mixed = mixed.result()
     sums_qkv[1].step()
     steps = rows // TILE
     grads[-1] = clock(grads[-1])
     grad_inputs, sums1 = clock(*project_back(grads, grad_residual, inputs, params, w_qkv, 0, steps))
     sum_w_up.wait(clock)
     sums_qkv[0].step()
+    sums_qkv[1].step()
+    grad_inputs = clock(grad_inputs)
     grad_inputs = FromWhole(grid, clock, grad_inputs.reshape(n, length, width), count)
-    sums_qkv[1].step(LONG)
-    sums_qkv[1].step()
-    sums1, sums2, sum_up, sum_down = clock(sums1, sums2, sum_up, sum_down)
     vectors = jnp.concatenate([sums1[:4], sums2[:3], sum_down[:1]])
     vectors = vectors.reshape(8, devices, each).transpose(1, 0, 2).reshape(devices, -1)
     vectors = jnp.concatenate([vectors, sum_up[:1].reshape(devices, -1)], axis=1)
     if grid.cube:
-        vectors = halve(vectors.reshape(grid.nz, 2, 2, 2, -1, 128), grid.core, 2, grid.over_core)
-    sums_qkv[0].step(LONG)
+        vectors = halve(clock(vectors).reshape(grid.nz, 2, 2, 2, -1, 128), grid.core, 2, grid.over_core)
+    sums_qkv[1].step(LONG)
+    sums_qkv[0].step()
     if grid.cube:
         vectors = halve(clock(vectors), grid.y, 1, grid.over_y)
-        sums_qkv[0].wait(clock)
-        vectors = halve(clock(vectors), grid.x, 1, grid.over_x)
     grad_inputs = grad_inputs.result()
     if grid.cube:
+        sums_qkv[1].wait(clock)
+        vectors = halve(clock(vectors), grid.x, 1, grid.over_x)
+        sums_qkv[0].wait(clock)
         parts = [pick(vectors, (grid.z + k) % grid.nz, 0) for k in range(grid.nz)]
         vectors = total(parts[:1] + [grid.along_z(part, k) for k, part in enumerate(parts) if k])
     else:

time: 538 us -> 530 us (0.985)
  starting transfers between devices: 99.8 us -> 77.8 us
  waiting for transfers between devices: 62.8 us -> 76.7 us
    ppermute x11, waiting for transfers between devices: 9.07 us -> 33.2 us  [over_x(): return lax.ppermute(v, SEQ, [(0, 1), (1, 0)])]
    ppermute x21, starting transfers between devices: 74.5 us -> 51.2 us  [along_z(): lax.ppermute(v, DP, [(i, (i + 4 * k) % self.dp) for i in range(self.dp)])]
    ppermute x21, waiting for transfers between devices: 24.7 us -> 16.2 us  [along_z(): lax.ppermute(v, DP, [(i, (i + 4 * k) % self.dp) for i in range(self.dp)])]
  transfers between devices with their start and end apart: 56 -> 56, of which waited for: 14 -> 17; matrix products, arithmetic and copies ran while one was open for 9% -> 10% of each run, Pallas kernels for 51% -> 53%
where the time goes in v3:
time: 530 us; the launch traced here: 524 us
  Pallas kernels  291 us (55%)
  starting transfers between devices  77.8 us (15%)
  waiting for transfers between devices  76.7 us (14%)
  local copies, waits for them, and re-layouts  35.6 us (7%)
  other arithmetic  27.1 us (5%)
  between operations  15.3 us (3%)
    pallas_call x10, Pallas kernels, run(): pl.pallas_call(body, grid_spec=pltpu.PrefetchScalarGridSpec(num_scalar_pr...  168 us
    ppermute x21, starting transfers between devices, along_z(): lax.ppermute(v, DP, [(i, (i + 4 * k) % self.dp) for i in range(self.dp)])  51.2 us
    pallas_call x12, Pallas kernels, split_sum(): pl.pallas_call(kernel, grid_spec=pltpu.PrefetchScalarGridSpec(num_scalar_...  48.4 us
    pallas_call x2, Pallas kernels, attention_backward(): pl.pallas_call(partial(attention_backward_kernel, head=head, chunk=256),...  44.4 us
    ppermute x11, waiting for transfers between devices, over_x(): return lax.ppermute(v, SEQ, [(0, 1), (1, 0)])  33.2 us
    pallas_call x2, Pallas kernels, attention_forward(): pl.pallas_call(partial(attention_forward_kernel, head=head, chunk=512), g...  30.3 us
    ppermute x21, waiting for transfers between devices, along_z(): lax.ppermute(v, DP, [(i, (i + 4 * k) % self.dp) for i in range(self.dp)])  16.2 us
    ppermute x11, starting transfers between devices, over_x(): return lax.ppermute(v, SEQ, [(0, 1), (1, 0)])  15.4 us
  transfers between devices with their start and end apart: 56, of which 17 were waited for; matrix products, arithmetic and copies ran while one was open for 10% of the time, Pallas kernels for 53%

profile of v3, /device:TPU:0, one launch (start us, length us, event | category | flops | bytes accessed | tf_op | source)
XLA Modules:
  0.0 523.9 jit_solution(17279422067849146927)
XLA Ops:
  24.8 8.6 %collective-permute-done.4 = bf16[1,32,2176]{2,1,0:T(8,128)(2,1)S(1)} collective-permute-done((bf16[1,32,2176]{2,1,0:T(8,128)(2,1)S(1)}, bf16[1,32,2176]{2,1,0:T(8,128)(2,1)S(1)}, u32[]{:S(2)}, u32[]{:S(2)}) %collective-permute-start.4) | collective-permute-done | bytes 139296 | tf_op jit(solution)/shard_map/ppermute | solution.py:61
  48.3 6.0 %broadcast_in_dim.49 = pred[1,1024,1024]{2,1,0:T(8,128)(4,1)} reshape(pred[16,64,16,64]{3,2,1,0:T(8,128)(4,1)} %broadcast_in_dim.48) | data formatting | bytes 2097152 | tf_op jit(solution)/shard_map/broadcast_in_dim | solution.py:473
  58.3 7.2 %collective-permute-start = (bf16[1,32,4096]{2,1,0:T(8,128)(2,1)S(1)}, bf16[1,32,4096]{2,1,0:T(8,128)(2,1)}, u32[]{:S(2)}, u32[]{:S(2)}) collective-permute-start(bf16[1,32,4096]{2,1,0:T(8,128)(2,1)S(1)} %bitcast.260), channel_id=1, source_target_pairs={{0,8},{2,10},{4,12},{6,14},{8,16},{10,18},{12,20},{14,22},{16,24},... | collective-permute-start | bytes 786440 | tf_op jit(solution)/shard_map/ppermute | solution.py:61
  65.5 9.6 %collective-permute-done.7.refs_3_.refs_11_.refs_2_.refs_10_ = bf16[4,32,2176]{2,1,0:T(8,128)(2,1)S(1)} collective-permute-done((bf16[4,32,2176]{2,1,0:T(8,128)(2,1)S(1)}, bf16[4,32,2176]{2,1,0:T(8,128)(2,1)S(1)}, u32[]{:S(2)}, u32[]{:S(2)}) %collective-permute-start.7) | collective-permute-done | bytes 557088 | tf_op jit(solution)/shard_map/ppermute | solution.py:55
  88.0 7.4 %all-gather.7.cloned.1.call-done = bf16[1024,2048]{1,0:T(8,128)(2,1)} async-done(((bf16[32,2048]{1,0:T(8,128)(2,1)}), bf16[1024,2048]{1,0:T(8,128)(2,1)}) %all-gather.7.cloned.1.call-update) | async-done | bytes 4194320 | tf_op jit(solution)/shard_map/all_gather | solution.py:102
  95.4 15.3 %project_in.1 = (bf16[1024,3072]{1,0:T(8,128)(2,1)}, bf16[1024,1024]{1,0:T(8,128)(2,1)}, f32[16,1024]{1,0:T(8,128)}) custom-call(s32[96]{0:T(128)} %stack.141.at, bf16[32,32,2048]{2,1,0:T(8,128)(2,1)} %bitcast.224, bf16[4,32,2176]{2,1,0:T(8,128)(2,1)} %copy-done.4, bf16[4,32,2176]{2,1,0:T(8,128)(2,1)} %copy-done.9, bf16[4,32,2176]{2,1,0:T(8,128)(2,1)} %copy-done.8, ...), custom_call_target="tpu_custom_call" | custom-call | flops 322122560 | tf_op jit(solution)/shard_map/project_in/pallas_call | solution.py:213
  110.7 15.1 %attention_forward.2 = (bf16[1,1024,512]{2,1,0:T(8,128)(2,1)}, f32[1,4,2,1024]{3,2,1,0:T(2,128)}, bf16[1,4,2,1024,1024]{4,3,2,1,0:T(8,128)(2,1)}) custom-call(bf16[1,1024,3072]{2,1,0:T(8,128)(2,1)} %bitcast.194, bf16[1,1024,3072]{2,1,0:T(8,128)(2,1)} %bitcast.195, bf16[1,1024,3072]{2,1,0:T(8,128)(2,1)} %bitcast.196, f32[1,1024,1024]{2,1,0:T(8,128)} %and_select_fusion.mask_ref), custom_call_target="tpu_custom_call" | custom-call | flops 6442450944 | tf_op jit(solution)/shard_map/attention_forward/pallas_call | solution.py:431
  125.8 15.1 %attention_forward.3 = (bf16[1,1024,512]{2,1,0:T(8,128)(2,1)}, f32[1,4,2,1024]{3,2,1,0:T(2,128)}, bf16[1,4,2,1024,1024]{4,3,2,1,0:T(8,128)(2,1)}) custom-call(bf16[1,1024,3072]{2,1,0:T(8,128)(2,1)} %bitcast.197, bf16[1,1024,3072]{2,1,0:T(8,128)(2,1)} %bitcast.198, bf16[1,1024,3072]{2,1,0:T(8,128)(2,1)} %bitcast.199, f32[1,1024,1024]{2,1,0:T(8,128)} %and_select_fusion.mask_ref), custom_call_target="tpu_custom_call" | custom-call | flops 6442450944 | tf_op jit(solution)/shard_map/attention_forward/pallas_call | solution.py:431
  141.0 10.6 %project_out.1 = (f32[1024,1024]{1,0:T(8,128)}, bf16[1024,1024]{1,0:T(8,128)(2,1)}, bf16[1024,1024]{1,0:T(8,128)(2,1)}, bf16[1024,1024]{1,0:T(8,128)(2,1)}) custom-call(s32[32]{0:T(128)} %stack.140.at, bf16[4,32,2176]{2,1,0:T(8,128)(2,1)} %copy-done.4, bf16[4,32,2176]{2,1,0:T(8,128)(2,1)} %copy-done.9, bf16[4,32,2176]{2,1,0:T(8,128)(2,1)} %copy-done.8, ...), custom_call_target="tpu_custom_call" | custom-call | flops 107374184 | tf_op jit(solution)/shard_map/project_out/pallas_call | solution.py:213
  161.8 24.1 %feed_up.1 = (bf16[1024,4096]{1,0:T(8,128)(2,1)}, bf16[1024,4096]{1,0:T(8,128)(2,1)}) custom-call(s32[32]{0:T(128)} %stack.140.at, bf16[4,32,4096]{2,1,0:T(8,128)(2,1)} %pad_maximum_fusion.4.refs_0_, bf16[4,32,4096]{2,1,0:T(8,128)(2,1)} %collective-permute-done.17.refs_1_, bf16[4,32,4096]{2,1,0:T(8,128)(2,1)} %collective-permute-done.10.refs_2_, ...), custom_call_target="tpu_custom_call" | custom-call | flops 429496736 | tf_op jit(solution)/shard_map/feed_up/pallas_call | solution.py:213
  185.9 7.3 %collective-permute-done.21 = bf16[512,1024]{1,0:T(8,128)(2,1)S(1)} collective-permute-done((bf16[512,1024]{1,0:T(8,128)(2,1)}, bf16[512,1024]{1,0:T(8,128)(2,1)S(1)}, u32[]{:S(2)}, u32[]{:S(2)}) %collective-permute-start.21) | collective-permute-done | bytes 1048608 | tf_op jit(solution)/shard_map/ppermute | solution.py:48
  194.8 16.0 %weight_grad_turned.1 = (bf16[16,1024,128]{2,1,0:T(8,128)(2,1)}, bf16[16,1024,128]{2,1,0:T(8,128)(2,1)}) custom-call(s32[1]{0:T(128)} %bitcast.48.at, bf16[1024,1024]{1,0:T(8,128)(2,1)} %pad_maximum_fusion.1.refs_0_.refs_4_.refs_18_, bf16[1024,4096]{1,0:T(8,128)(2,1)} %get-tuple-element.354.refs_1_), custom_call_target="tpu_custom_call" | custom-call | flops 429496736 | tf_op jit(solution)/shard_map/weight_grad_turned/pallas_call | solution.py:213
  210.8 30.4 %feed_down.1 = (bf16[1024,1024]{1,0:T(8,128)(2,1)}, bf16[1024,4096]{1,0:T(8,128)(2,1)}, f32[8,4096]{1,0:T(8,128)}, f32[8,1024]{1,0:T(8,128)}) custom-call(s32[32]{0:T(128)} %iota_multiply_fusion.at, bf16[32,128,1024]{2,1,0:T(8,128)(2,1)} %bitcast.271, bf16[1024,4096]{1,0:T(8,128)(2,1)} %get-tuple-element.354.refs_1_, ...), custom_call_target="tpu_custom_call" | custom-call | flops 85899345920 | tf_op jit(solution)/shard_map/feed_down/pallas_call | solution.py:213
  243.8 6.5 %sum_y.4 = (bf16[8192,128]{1,0:T(8,128)(2,1)}, bf16[8192,128]{1,0:T(8,128)(2,1)}) custom-call(s32[2]{0:T(128)} %pad_add_fusion.at, bf16[2,8192,128]{2,1,0:T(8,128)(2,1)} %bitcast.218, bf16[2,8192,128]{2,1,0:T(8,128)(2,1)} %bitcast.219, bf16[2,8192,128]{2,1,0:T(8,128)(2,1)} %bitcast.60.refs_2_.refs_3_, bf16[2,8192,128]{2,1,0:T(8,128)(2,1)} %bitcast.60.refs_2_.refs_3_), custom_call_target="tpu_custom_call" | custom-call | flops 1000000000 | tf_op jit(solution)/shard_map/sum_y/pallas_call | solution.py:259
  252.0 14.3 %weight_grad_4096.1 = (bf16[512,4096]{1,0:T(8,128)(2,1)}, bf16[512,4096]{1,0:T(8,128)(2,1)}) custom-call(s32[1]{0:T(128)} %bitcast.48.at, bf16[1024,1024]{1,0:T(8,128)(2,1)} %get-tuple-element.374.refs_0_, bf16[1,1024,4096]{2,1,0:T(8,128)(2,1)} %bitcast.234), custom_call_target="tpu_custom_call" | custom-call | flops 429496736 | tf_op jit(solution)/shard_map/weight_grad_4096/pallas_call | solution.py:213
  266.2 23.2 %feed_back.1 = (f32[1024,1024]{1,0:T(8,128)}, bf16[1024,1024]{1,0:T(8,128)(2,1)}, bf16[1024,1024]{1,0:T(8,128)(2,1)}, f32[8,1024]{1,0:T(8,128)}) custom-call(s32[64]{0:T(128)} %stack.143.at, bf16[4,32,4096]{2,1,0:T(8,128)(2,1)} %pad_maximum_fusion.4.refs_0_, bf16[4,32,4096]{2,1,0:T(8,128)(2,1)} %collective-permute-done.17.refs_1_, ...), custom_call_target="tpu_custom_call" | custom-call | flops 53687091200 | tf_op jit(solution)/shard_map/feed_back/pallas_call | solution.py:213
  289.5 6.5 %sum_x.4 = (bf16[256,4096]{1,0:T(8,128)(2,1)}, bf16[256,4096]{1,0:T(8,128)(2,1)}) custom-call(s32[2]{0:T(128)} %pad_add_fusion.2.at, bf16[2,256,4096]{2,1,0:T(8,128)(2,1)} %bitcast.216, bf16[2,256,4096]{2,1,0:T(8,128)(2,1)} %bitcast.217, bf16[2,256,4096]{2,1,0:T(8,128)(2,1)} %bitcast.75.refs_2_.refs_3_, bf16[2,256,4096]{2,1,0:T(8,128)(2,1)} %bitcast.75.refs_2_.refs_3_), custom_call_target="tpu_custom_call" | custom-call | flops 1000000000 | tf_op jit(solution)/shard_map/sum_x/pallas_call | solution.py:259
  309.6 22.2 %attention_backward.2 = bf16[3,1,1024,512]{3,2,1,0:T(8,128)(2,1)} custom-call(bf16[1,1024,3072]{2,1,0:T(8,128)(2,1)} %bitcast.200, bf16[1,1024,3072]{2,1,0:T(8,128)(2,1)} %bitcast.201, bf16[1,1024,3072]{2,1,0:T(8,128)(2,1)} %bitcast.202, bf16[1,4,2,1024,1024]{4,3,2,1,0:T(8,128)(2,1)} %get-tuple-element.389.weight_ref, bf16[1,1024,1024]{2,1,0:T(8,128)(2,1)} %bitcast.250, ...), custom_call_target="tpu_custom_call" | custom-call | flops 1395864320 | tf_op jit(solution)/shard_map/attention_backward/pallas_call | solution.py:451
  331.7 11.0 %weight_grad_2560.1 = (bf16[512,2560]{1,0:T(8,128)(2,1)}, bf16[512,2560]{1,0:T(8,128)(2,1)}) custom-call(s32[1]{0:T(128)} %bitcast.48.at, bf16[1024,1024]{1,0:T(8,128)(2,1)} %get-tuple-element.471.refs_0_, bf16[3,1024,512]{2,1,0:T(8,128)(2,1)} %bitcast.214, bf16[1024,1024]{1,0:T(8,128)(2,1)} %get-tuple-element.428.refs_2_, bf16[1,1024,1024]{2,1,0:T(8,128)(2,1)} %bitcast.252), custom_call_target="tpu_custom_call" | custom-call | flops 268435456 | tf_op jit(solution)/shard_map/weight_grad_2560/pallas_call | solution.py:213
  353.3 22.2 %attention_backward.3 = bf16[3,1,1024,512]{3,2,1,0:T(8,128)(2,1)} custom-call(bf16[1,1024,3072]{2,1,0:T(8,128)(2,1)} %bitcast.203, bf16[1,1024,3072]{2,1,0:T(8,128)(2,1)} %bitcast.204, bf16[1,1024,3072]{2,1,0:T(8,128)(2,1)} %bitcast.205, bf16[1,4,2,1024,1024]{4,3,2,1,0:T(8,128)(2,1)} %get-tuple-element.414.weight_ref, bf16[1,1024,1024]{2,1,0:T(8,128)(2,1)} %bitcast.251, ...), custom_call_target="tpu_custom_call" | custom-call | flops 139586437120 | tf_op jit(solution)/shard_map/attention_backward/pallas_call | solution.py:451
  386.9 7.1 %weight_grad_1536.1 = (bf16[512,1536]{1,0:T(8,128)(2,1)}, bf16[512,1536]{1,0:T(8,128)(2,1)}) custom-call(s32[1]{0:T(128)} %bitcast.48.at, bf16[1024,1024]{1,0:T(8,128)(2,1)} %get-tuple-element.471.refs_0_, bf16[3,1024,512]{2,1,0:T(8,128)(2,1)} %bitcast.226), custom_call_target="tpu_custom_call" | custom-call | flops 161061280 | tf_op jit(solution)/shard_map/weight_grad_1536/pallas_call | solution.py:213
  406.4 9.4 %collective-permute-start.35 = (bf16[32,4096]{1,0:T(8,128)(2,1)}, bf16[32,4096]{1,0:T(8,128)(2,1)}, u32[]{:S(2)}, u32[]{:S(2)}) collective-permute-start(bf16[32,4096]{1,0:T(8,128)(2,1)} %get-tuple-element.494), channel_id=1, source_target_pairs={{0,8},{2,10},{4,12},{6,14},{8,16},{10,18},{12,20},{14,22},{16,24},... | collective-permute-start | bytes 786440 | tf_op jit(solution)/shard_map/ppermute | solution.py:61
  421.1 16.4 %project_back.1 = (bf16[1024,1024]{1,0:T(8,128)(2,1)}, f32[8,1024]{1,0:T(8,128)}) custom-call(s32[65]{0:T(128)} %stack.150.at, bf16[32,32,2048]{2,1,0:T(8,128)(2,1)} %bitcast.225, bf16[4,32,2176]{2,1,0:T(8,128)(2,1)} %copy-done.4, bf16[4,32,2176]{2,1,0:T(8,128)(2,1)} %copy-done.9, bf16[4,32,2176]{2,1,0:T(8,128)(2,1)} %copy-done.8, ...), custom_call_target="tpu_custom_call" | custom-call | flops 322122560 | tf_op jit(solution)/shard_map/project_back/pallas_call | solution.py:213
  451.0 17.8 %collective-permute-done.41.refs_4_.refs_5_.refs_6_.refs_7_ = bf16[4,32,1536]{2,1,0:T(8,128)(2,1)S(1)} collective-permute-done((bf16[4,32,1536]{2,1,0:T(8,128)(2,1)}, bf16[4,32,1536]{2,1,0:T(8,128)(2,1)S(1)}, u32[]{:S(2)}, u32[]{:S(2)}) %collective-permute-start.41) | collective-permute-done | bytes 393248 | tf_op jit(solution)/shard_map/ppermute | solution.py:48
  (279 shorter events, 179.3 us)
Async XLA Ops:
  7.4 88.0 %all-gather.7.cloned.1.call-start = ((), (), s32[]{:S(2)}) async-start(), calls=%async_computation.1 | async-start | bytes 4325376 | tf_op jit(solution)/shard_map/all_gather | solution.py:102
  9.2 201.6 %all-gather.5.cloned.1.call-start = ((), (), s32[]{:S(2)}) async-start(), calls=%async_computation | async-start | bytes 8650752 | tf_op jit(solution)/shard_map/all_gather | solution.py:102
  12.2 27.4 %collective-permute-start.6 = (bf16[512,1024]{1,0:T(8,128)(2,1)}, bf16[512,1024]{1,0:T(8,128)(2,1)}, u32[]{:S(2)}, u32[]{:S(2)}) collective-permute-start(bf16[512,1024]{1,0:T(8,128)(2,1)} %dynamic-slice_bitcast_fusion.3), channel_id=1, source_target_pairs={{0,1},{1,0},{2,3},{3,2},{4,5},{5,4},{6,7},{7,6},{8,9},{9,8},{10,11... | collective-permute-start | bytes 3145736 | tf_op jit(solution)/shard_map/ppermute | solution.py:48
  20.2 55.4 %collective-permute-start.2 = (bf16[1,32,4096]{2,1,0:T(8,128)(2,1)S(1)}, bf16[1,32,4096]{2,1,0:T(8,128)(2,1)S(1)}, u32[]{:S(2)}, u32[]{:S(2)}) collective-permute-start(bf16[1,32,4096]{2,1,0:T(8,128)(2,1)S(1)} %bitcast.258), channel_id=1, source_target_pairs={{0,24},{2,26},{4,28},{6,30},{8,0},{10,2},{12,4},{14,6},{16,8},{18,... | collective-permute-start | bytes 786440 | tf_op jit(solution)/shard_map/ppermute | solution.py:61
  23.3 52.3 %collective-permute-start.1 = (bf16[1,32,4096]{2,1,0:T(8,128)(2,1)S(1)}, bf16[1,32,4096]{2,1,0:T(8,128)(2,1)}, u32[]{:S(2)}, u32[]{:S(2)}) collective-permute-start(bf16[1,32,4096]{2,1,0:T(8,128)(2,1)S(1)} %bitcast.259), channel_id=1, source_target_pairs={{0,16},{2,18},{4,20},{6,22},{8,24},{10,26},{12,28},{14,30},{16,0},... | collective-permute-start | bytes 786440 | tf_op jit(solution)/shard_map/ppermute | solution.py:61
  45.8 29.2 %collective-permute-start.7 = (bf16[4,32,2176]{2,1,0:T(8,128)(2,1)S(1)}, bf16[4,32,2176]{2,1,0:T(8,128)(2,1)S(1)}, u32[]{:S(2)}, u32[]{:S(2)}) collective-permute-start(bf16[4,32,2176]{2,1,0:T(8,128)(2,1)S(1)} %pad_maximum_fusion.5.refs_1_.refs_9_.refs_0_.refs_8_), channel_id=1, source_target_pairs={{0,5},{1,4},{2,7},{3,6},{4,1},{5,0},{6,3},{7,2},{8,13},{9,12},{10,... | collective-permute-start | bytes 1671176 | tf_op jit(solution)/shard_map/ppermute | solution.py:55
  84.0 67.5 %collective-permute-start.12 = (bf16[4,32,4096]{2,1,0:T(8,128)(2,1)}, bf16[4,32,4096]{2,1,0:T(8,128)(2,1)}, u32[]{:S(2)}, u32[]{:S(2)}) collective-permute-start(bf16[4,32,4096]{2,1,0:T(8,128)(2,1)} %pad_maximum_fusion.4.refs_0_), channel_id=1, source_target_pairs={{0,4},{2,6},{4,0},{6,2},{8,12},{10,14},{12,8},{14,10},{16,20},{18,... | collective-permute-start | bytes 3145736 | tf_op jit(solution)/shard_map/ppermute | solution.py:51
  84.2 67.4 %collective-permute-start.11 = (bf16[4,32,4096]{2,1,0:T(8,128)(2,1)}, bf16[4,32,4096]{2,1,0:T(8,128)(2,1)}, u32[]{:S(2)}, u32[]{:S(2)}) collective-permute-start(bf16[4,32,4096]{2,1,0:T(8,128)(2,1)} %pad_maximum_fusion.4.refs_0_), channel_id=1, source_target_pairs={{0,1},{1,0},{2,3},{3,2},{4,5},{5,4},{6,7},{7,6},{8,9},{9,8},{10,11... | collective-permute-start | bytes 3145736 | tf_op jit(solution)/shard_map/ppermute | solution.py:48
  88.0 63.6 %collective-permute-start.10 = (bf16[4,32,4096]{2,1,0:T(8,128)(2,1)}, bf16[4,32,4096]{2,1,0:T(8,128)(2,1)}, u32[]{:S(2)}, u32[]{:S(2)}) collective-permute-start(bf16[4,32,4096]{2,1,0:T(8,128)(2,1)} %pad_maximum_fusion.4.refs_0_), channel_id=1, source_target_pairs={{0,5},{1,4},{2,7},{3,6},{4,1},{5,0},{6,3},{7,2},{8,13},{9,12},{10,... | collective-permute-start | bytes 3145736 | tf_op jit(solution)/shard_map/ppermute | solution.py:55
  153.7 39.4 %collective-permute-start.21 = (bf16[512,1024]{1,0:T(8,128)(2,1)}, bf16[512,1024]{1,0:T(8,128)(2,1)S(1)}, u32[]{:S(2)}, u32[]{:S(2)}) collective-permute-start(bf16[512,1024]{1,0:T(8,128)(2,1)} %dynamic-slice_bitcast_fusion.2), channel_id=1, source_target_pairs={{0,1},{1,0},{2,3},{3,2},{4,5},{5,4},{6,7},{7,6},{8,9},{9,8},{10,11... | collective-permute-start | bytes 3145736 | tf_op jit(solution)/shard_map/ppermute | solution.py:48
  210.8 33.0 %collective-permute-start.23 = (bf16[2,4,2,1024,128]{4,3,2,1,0:T(8,128)(2,1)}, bf16[2,4,2,1024,128]{4,3,2,1,0:T(8,128)(2,1)}, u32[]{:S(2)}, u32[]{:S(2)}) collective-permute-start(bf16[2,4,2,1024,128]{4,3,2,1,0:T(8,128)(2,1)} %bitcast.273), channel_id=1, source_target_pairs={{0,2},{2,0},{4,6},{6,4},{8,10},{10,8},{12,14},{14,12},{16,18},{18,... | collective-permute-start | bytes 12582920 | tf_op jit(solution)/shard_map/ppermute | solution.py:58
  243.4 46.0 %collective-permute-start.22 = (bf16[512,1024]{1,0:T(8,128)(2,1)}, bf16[512,1024]{1,0:T(8,128)(2,1)S(1)}, u32[]{:S(2)}, u32[]{:S(2)}) collective-permute-start(bf16[512,1024]{1,0:T(8,128)(2,1)} %dynamic-slice_bitcast_fusion.1), channel_id=1, source_target_pairs={{0,1},{1,0},{2,3},{3,2},{4,5},{5,4},{6,7},{7,6},{8,9},{9,8},{10,11... | collective-permute-start | bytes 3145736 | tf_op jit(solution)/shard_map/ppermute | solution.py:48
  250.3 47.9 %collective-permute-start.24 = (bf16[4,2,1024,128]{3,2,1,0:T(8,128)(2,1)}, bf16[4,2,1024,128]{3,2,1,0:T(8,128)(2,1)S(1)}, u32[]{:S(2)}, u32[]{:S(2)}) collective-permute-start(bf16[4,2,1024,128]{3,2,1,0:T(8,128)(2,1)} %bitcast.276), channel_id=1, source_target_pairs={{0,4},{2,6},{4,0},{6,2},{8,12},{10,14},{12,8},{14,10},{16,20},{18,... | collective-permute-start | bytes 6291464 | tf_op jit(solution)/shard_map/ppermute | solution.py:51
  296.0 51.7 %collective-permute-start.26 = (bf16[2,4,32,4096]{3,2,1,0:T(8,128)(2,1)}, bf16[2,4,32,4096]{3,2,1,0:T(8,128)(2,1)}, u32[]{:S(2)}, u32[]{:S(2)}) collective-permute-start(bf16[2,4,32,4096]{3,2,1,0:T(8,128)(2,1)} %bitcast.275), channel_id=1, source_target_pairs={{0,1},{1,0},{2,3},{3,2},{4,5},{5,4},{6,7},{7,6},{8,9},{9,8},{10,11... | collective-permute-start | bytes 6291464 | tf_op jit(solution)/shard_map/ppermute | solution.py:48
  303.8 39.0 %collective-permute-start.27 = (bf16[2,1024,128]{2,1,0:T(8,128)(2,1)}, bf16[2,1024,128]{2,1,0:T(8,128)(2,1)S(1)}, u32[]{:S(2)}, u32[]{:S(2)}) collective-permute-start(bf16[2,1024,128]{2,1,0:T(8,128)(2,1)} %bitcast.286), channel_id=1, source_target_pairs={{0,8},{2,10},{4,12},{6,14},{8,16},{10,18},{12,20},{14,22},{16,24},... | collective-permute-start | bytes 1572872 | tf_op jit(solution)/shard_map/ppermute | solution.py:61
  305.8 37.1 %collective-permute-start.28 = (bf16[2,1024,128]{2,1,0:T(8,128)(2,1)}, bf16[2,1024,128]{2,1,0:T(8,128)(2,1)S(1)}, u32[]{:S(2)}, u32[]{:S(2)}) collective-permute-start(bf16[2,1024,128]{2,1,0:T(8,128)(2,1)} %bitcast.285), channel_id=1, source_target_pairs={{0,16},{2,18},{4,20},{6,22},{8,24},{10,26},{12,28},{14,30},{16,0},... | collective-permute-start | bytes 1572872 | tf_op jit(solution)/shard_map/ppermute | solution.py:61
  308.0 34.9 %collective-permute-start.29 = (bf16[2,1024,128]{2,1,0:T(8,128)(2,1)}, bf16[2,1024,128]{2,1,0:T(8,128)(2,1)S(1)}, u32[]{:S(2)}, u32[]{:S(2)}) collective-permute-start(bf16[2,1024,128]{2,1,0:T(8,128)(2,1)} %bitcast.284), channel_id=1, source_target_pairs={{0,24},{2,26},{4,28},{6,30},{8,0},{10,2},{12,4},{14,6},{16,8},{18,... | collective-permute-start | bytes 1572872 | tf_op jit(solution)/shard_map/ppermute | solution.py:61
  342.8 39.0 %collective-permute-start.30 = (bf16[2,2,4,32,2560]{4,3,2,1,0:T(8,128)(2,1)}, bf16[2,2,4,32,2560]{4,3,2,1,0:T(8,128)(2,1)}, u32[]{:S(2)}, u32[]{:S(2)}) collective-permute-start(bf16[2,2,4,32,2560]{4,3,2,1,0:T(8,128)(2,1)} %bitcast.274), channel_id=1, source_target_pairs={{0,2},{2,0},{4,6},{6,4},{8,10},{10,8},{12,14},{14,12},{16,18},{18,... | collective-permute-start | bytes 7864328 | tf_op jit(solution)/shard_map/ppermute | solution.py:58
  351.7 25.8 %collective-permute-start.31 = (bf16[4,32,4096]{2,1,0:T(8,128)(2,1)}, bf16[4,32,4096]{2,1,0:T(8,128)(2,1)S(1)}, u32[]{:S(2)}, u32[]{:S(2)}) collective-permute-start(bf16[4,32,4096]{2,1,0:T(8,128)(2,1)} %bitcast.279), channel_id=1, source_target_pairs={{0,4},{2,6},{4,0},{6,2},{8,12},{10,14},{12,8},{14,10},{16,20},{18,... | collective-permute-start | bytes 3145736 | tf_op jit(solution)/shard_map/ppermute | solution.py:51
  394.1 43.5 %collective-permute-start.34 = (bf16[2,4,32,2560]{3,2,1,0:T(8,128)(2,1)}, bf16[2,4,32,2560]{3,2,1,0:T(8,128)(2,1)S(1)}, u32[]{:S(2)}, u32[]{:S(2)}) collective-permute-start(bf16[2,4,32,2560]{3,2,1,0:T(8,128)(2,1)} %bitcast.278), channel_id=1, source_target_pairs={{0,4},{2,6},{4,0},{6,2},{8,12},{10,14},{12,8},{14,10},{16,20},{18,... | collective-permute-start | bytes 3932168 | tf_op jit(solution)/shard_map/ppermute | solution.py:51
  404.2 39.3 %collective-permute-start.33 = (bf16[2,4,32,1536]{3,2,1,0:T(8,128)(2,1)}, bf16[2,4,32,1536]{3,2,1,0:T(8,128)(2,1)}, u32[]{:S(2)}, u32[]{:S(2)}) collective-permute-start(bf16[2,4,32,1536]{3,2,1,0:T(8,128)(2,1)} %bitcast.282), channel_id=1, source_target_pairs={{0,4},{2,6},{4,0},{6,2},{8,12},{10,14},{12,8},{14,10},{16,20},{18,... | collective-permute-start | bytes 2359304 | tf_op jit(solution)/shard_map/ppermute | solution.py:51
  406.4 31.1 %collective-permute-start.35 = (bf16[32,4096]{1,0:T(8,128)(2,1)}, bf16[32,4096]{1,0:T(8,128)(2,1)}, u32[]{:S(2)}, u32[]{:S(2)}) collective-permute-start(bf16[32,4096]{1,0:T(8,128)(2,1)} %get-tuple-element.494), channel_id=1, source_target_pairs={{0,8},{2,10},{4,12},{6,14},{8,16},{10,18},{12,20},{14,22},{16,24},... | collective-permute-start | bytes 786440 | tf_op jit(solution)/shard_map/ppermute | solution.py:61
  442.4 29.8 %collective-permute-start.40 = (bf16[4,32,2560]{2,1,0:T(8,128)(2,1)}, bf16[4,32,2560]{2,1,0:T(8,128)(2,1)S(1)}, u32[]{:S(2)}, u32[]{:S(2)}) collective-permute-start(bf16[4,32,2560]{2,1,0:T(8,128)(2,1)} %bitcast.283), channel_id=1, source_target_pairs={{0,1},{1,0},{2,3},{3,2},{4,5},{5,4},{6,7},{7,6},{8,9},{9,8},{10,11... | collective-permute-start | bytes 1966088 | tf_op jit(solution)/shard_map/ppermute | solution.py:48
  449.9 39.5 %collective-permute-start.38 = (bf16[512,1024]{1,0:T(8,128)(2,1)}, bf16[512,1024]{1,0:T(8,128)(2,1)}, u32[]{:S(2)}, u32[]{:S(2)}) collective-permute-start(bf16[512,1024]{1,0:T(8,128)(2,1)} %dynamic-slice_bitcast_fusion), channel_id=1, source_target_pairs={{0,1},{1,0},{2,3},{3,2},{4,5},{5,4},{6,7},{7,6},{8,9},{9,8},{10,11... | collective-permute-start | bytes 3145736 | tf_op jit(solution)/shard_map/ppermute | solution.py:48
  (75 other events, 832.5 us)
Sparse Core Ops, SparseCore 0:
  11.8 83.5 all-gather.6
  98.4 95.2 all-gather.4

commit v4 on v3

--- a/solution.py
+++ b/solution.py
@@ -243,7 +243,8 @@
     columns = terms[0].shape[-1]
     rows = size // parts // columns
     tile = rows
-    while tile * columns > 2**18 and tile % 32 == 0:
+    limit = min(2**19, max(2**17, rows * columns // 2))
+    while tile * columns > limit and tile % 32 == 0:
         tile //= 2
     flat = [t.reshape(parts, rows, columns) for t in terms]
     wanted = len(order)
@@ -882,7 +883,7 @@
     first = gather(jnp.concatenate([w_q, w_k], axis=1))
     second = Gather(grid, jnp.concatenate([w_v, w_o, extra], axis=1))
     inputs = second.near(clock, inputs)
-    third = Gather(grid, w_up)
+    third = Gather(grid, clock(w_up))
     fourth = gather(w_down)
     if grid.group > 1:
         place = lax.axis_index(SEQ)

time: 530 us -> 521 us (0.983)
  starting transfers between devices: 77.8 us -> 70.7 us
    ppermute x21, waiting for transfers between devices: 16.2 us -> 26.7 us  [along_z(): lax.ppermute(v, DP, [(i, (i + 4 * k) % self.dp) for i in range(self.dp)])]
    all_gather x2, waiting for transfers between devices: 7.38 us -> 0.01 us  [gather(): every = lax.all_gather(shard, BOTH, axis=0)]
    ppermute x21, starting transfers between devices: 51.2 us -> 44.3 us  [along_z(): lax.ppermute(v, DP, [(i, (i + 4 * k) % self.dp) for i in range(self.dp)])]
    unnamed x91 -> x89, local copies, waits for them, and re-layouts: 10.7 us -> 10.1 us
  transfers between devices with their start and end apart: 56 -> 56, of which waited for: 17 -> 15; matrix products, arithmetic and copies ran while one was open for 10% -> 10% of each run, Pallas kernels for 53% -> 54%
where the time goes in v4:
time: 521 us; the launch traced here: 515 us
  Pallas kernels  289 us (55%)
  waiting for transfers between devices  77.9 us (15%)
  starting transfers between devices  70.7 us (14%)
  local copies, waits for them, and re-layouts  35 us (7%)
  other arithmetic  26.3 us (5%)
  between operations  15.3 us (3%)
    pallas_call x10, Pallas kernels, run(): pl.pallas_call(body, grid_spec=pltpu.PrefetchScalarGridSpec(num_scalar_pr...  169 us
    pallas_call x12, Pallas kernels, split_sum(): pl.pallas_call(kernel, grid_spec=pltpu.PrefetchScalarGridSpec(num_scalar_...  46.1 us
    pallas_call x2, Pallas kernels, attention_backward(): pl.pallas_call(partial(attention_backward_kernel, head=head, chunk=256),...  44.4 us
    ppermute x21, starting transfers between devices, along_z(): lax.ppermute(v, DP, [(i, (i + 4 * k) % self.dp) for i in range(self.dp)])  44.3 us
    ppermute x11, waiting for transfers between devices, over_x(): return lax.ppermute(v, SEQ, [(0, 1), (1, 0)])  35.3 us
    pallas_call x2, Pallas kernels, attention_forward(): pl.pallas_call(partial(attention_forward_kernel, head=head, chunk=512), g...  30.3 us
    ppermute x21, waiting for transfers between devices, along_z(): lax.ppermute(v, DP, [(i, (i + 4 * k) % self.dp) for i in range(self.dp)])  26.7 us
    ppermute x11, starting transfers between devices, over_x(): return lax.ppermute(v, SEQ, [(0, 1), (1, 0)])  13.2 us
  transfers between devices with their start and end apart: 56, of which 15 were waited for; matrix products, arithmetic and copies ran while one was open for 10% of the time, Pallas kernels for 54%

profile of v4, /device:TPU:0, one launch (start us, length us, event | category | flops | bytes accessed | tf_op | source)
XLA Modules:
  0.0 514.5 jit_solution(10510076718319947951)
XLA Ops:
  23.3 9.2 %collective-permute-done.1 = bf16[1,32,2176]{2,1,0:T(8,128)(2,1)S(1)} collective-permute-done((bf16[1,32,2176]{2,1,0:T(8,128)(2,1)S(1)}, bf16[1,32,2176]{2,1,0:T(8,128)(2,1)S(1)}, u32[]{:S(2)}, u32[]{:S(2)}) %collective-permute-start.1) | collective-permute-done | bytes 139296 | tf_op jit(solution)/shard_map/ppermute | solution.py:61
  32.6 6.9 %collective-permute-done.3 = bf16[512,1024]{1,0:T(8,128)(2,1)} collective-permute-done((bf16[512,1024]{1,0:T(8,128)(2,1)}, bf16[512,1024]{1,0:T(8,128)(2,1)}, u32[]{:S(2)}, u32[]{:S(2)}) %collective-permute-start.3) | collective-permute-done | bytes 1048608 | tf_op jit(solution)/shard_map/ppermute | solution.py:48
  52.2 6.0 %broadcast_in_dim.49 = pred[1,1024,1024]{2,1,0:T(8,128)(4,1)} reshape(pred[16,64,16,64]{3,2,1,0:T(8,128)(4,1)} %broadcast_in_dim.48) | data formatting | bytes 2097152 | tf_op jit(solution)/shard_map/broadcast_in_dim | solution.py:474
  59.8 11.7 %collective-permute-done.7.refs_3_.refs_11_.refs_2_.refs_10_ = bf16[4,32,2176]{2,1,0:T(8,128)(2,1)S(1)} collective-permute-done((bf16[4,32,2176]{2,1,0:T(8,128)(2,1)S(1)}, bf16[4,32,2176]{2,1,0:T(8,128)(2,1)S(1)}, u32[]{:S(2)}, u32[]{:S(2)}) %collective-permute-start.7) | collective-permute-done | bytes 557088 | tf_op jit(solution)/shard_map/ppermute | solution.py:55
  72.1 7.7 %collective-permute-done.5 = bf16[1,32,4096]{2,1,0:T(8,128)(2,1)} collective-permute-done((bf16[1,32,4096]{2,1,0:T(8,128)(2,1)S(1)}, bf16[1,32,4096]{2,1,0:T(8,128)(2,1)}, u32[]{:S(2)}, u32[]{:S(2)}) %collective-permute-start.5) | collective-permute-done | bytes 262176 | tf_op jit(solution)/shard_map/ppermute | solution.py:61
  91.4 15.3 %project_in.1 = (bf16[1024,3072]{1,0:T(8,128)(2,1)}, bf16[1024,1024]{1,0:T(8,128)(2,1)}, f32[16,1024]{1,0:T(8,128)}) custom-call(s32[96]{0:T(128)} %stack.141.at, bf16[32,32,2048]{2,1,0:T(8,128)(2,1)} %bitcast.224, bf16[4,32,2176]{2,1,0:T(8,128)(2,1)} %copy-done.4, bf16[4,32,2176]{2,1,0:T(8,128)(2,1)} %copy-done.9, bf16[4,32,2176]{2,1,0:T(8,128)(2,1)} %copy-done.8, ...), custom_call_target="tpu_custom_call" | custom-call | flops 322122560 | tf_op jit(solution)/shard_map/project_in/pallas_call | solution.py:213
  106.7 15.1 %attention_forward.2 = (bf16[1,1024,512]{2,1,0:T(8,128)(2,1)}, f32[1,4,2,1024]{3,2,1,0:T(2,128)}, bf16[1,4,2,1024,1024]{4,3,2,1,0:T(8,128)(2,1)}) custom-call(bf16[1,1024,3072]{2,1,0:T(8,128)(2,1)} %bitcast.194, bf16[1,1024,3072]{2,1,0:T(8,128)(2,1)} %bitcast.195, bf16[1,1024,3072]{2,1,0:T(8,128)(2,1)} %bitcast.196, f32[1,1024,1024]{2,1,0:T(8,128)} %and_select_fusion.mask_ref), custom_call_target="tpu_custom_call" | custom-call | flops 6442450944 | tf_op jit(solution)/shard_map/attention_forward/pallas_call | solution.py:432
  121.8 15.1 %attention_forward.3 = (bf16[1,1024,512]{2,1,0:T(8,128)(2,1)}, f32[1,4,2,1024]{3,2,1,0:T(2,128)}, bf16[1,4,2,1024,1024]{4,3,2,1,0:T(8,128)(2,1)}) custom-call(bf16[1,1024,3072]{2,1,0:T(8,128)(2,1)} %bitcast.197, bf16[1,1024,3072]{2,1,0:T(8,128)(2,1)} %bitcast.198, bf16[1,1024,3072]{2,1,0:T(8,128)(2,1)} %bitcast.199, f32[1,1024,1024]{2,1,0:T(8,128)} %and_select_fusion.mask_ref), custom_call_target="tpu_custom_call" | custom-call | flops 6442450944 | tf_op jit(solution)/shard_map/attention_forward/pallas_call | solution.py:432
  136.9 10.6 %project_out.1 = (f32[1024,1024]{1,0:T(8,128)}, bf16[1024,1024]{1,0:T(8,128)(2,1)}, bf16[1024,1024]{1,0:T(8,128)(2,1)}, bf16[1024,1024]{1,0:T(8,128)(2,1)}) custom-call(s32[32]{0:T(128)} %stack.140.at, bf16[4,32,2176]{2,1,0:T(8,128)(2,1)} %copy-done.4, bf16[4,32,2176]{2,1,0:T(8,128)(2,1)} %copy-done.9, bf16[4,32,2176]{2,1,0:T(8,128)(2,1)} %copy-done.8, ...), custom_call_target="tpu_custom_call" | custom-call | flops 107374184 | tf_op jit(solution)/shard_map/project_out/pallas_call | solution.py:213
  155.9 24.1 %feed_up.1 = (bf16[1024,4096]{1,0:T(8,128)(2,1)}, bf16[1024,4096]{1,0:T(8,128)(2,1)}) custom-call(s32[32]{0:T(128)} %stack.140.at, bf16[4,32,4096]{2,1,0:T(8,128)(2,1)} %pad_maximum_fusion.4.refs_0_, bf16[4,32,4096]{2,1,0:T(8,128)(2,1)} %collective-permute-done.17.refs_1_, bf16[4,32,4096]{2,1,0:T(8,128)(2,1)} %collective-permute-done.10.refs_2_, ...), custom_call_target="tpu_custom_call" | custom-call | flops 429496736 | tf_op jit(solution)/shard_map/feed_up/pallas_call | solution.py:213
  180.0 6.1 %collective-permute-done.21 = bf16[512,1024]{1,0:T(8,128)(2,1)S(1)} collective-permute-done((bf16[512,1024]{1,0:T(8,128)(2,1)}, bf16[512,1024]{1,0:T(8,128)(2,1)S(1)}, u32[]{:S(2)}, u32[]{:S(2)}) %collective-permute-start.21) | collective-permute-done | bytes 1048608 | tf_op jit(solution)/shard_map/ppermute | solution.py:48
  187.7 16.3 %weight_grad_turned.1 = (bf16[16,1024,128]{2,1,0:T(8,128)(2,1)}, bf16[16,1024,128]{2,1,0:T(8,128)(2,1)}) custom-call(s32[1]{0:T(128)} %bitcast.48.at, bf16[1024,1024]{1,0:T(8,128)(2,1)} %pad_maximum_fusion.1.refs_0_.refs_4_.refs_18_, bf16[1024,4096]{1,0:T(8,128)(2,1)} %get-tuple-element.358.refs_1_), custom_call_target="tpu_custom_call" | custom-call | flops 429496736 | tf_op jit(solution)/shard_map/weight_grad_turned/pallas_call | solution.py:213
  204.0 30.3 %feed_down.1 = (bf16[1024,1024]{1,0:T(8,128)(2,1)}, bf16[1024,4096]{1,0:T(8,128)(2,1)}, f32[8,4096]{1,0:T(8,128)}, f32[8,1024]{1,0:T(8,128)}) custom-call(s32[32]{0:T(128)} %iota_multiply_fusion.at, bf16[32,128,1024]{2,1,0:T(8,128)(2,1)} %bitcast.271, bf16[1024,4096]{1,0:T(8,128)(2,1)} %get-tuple-element.358.refs_1_, ...), custom_call_target="tpu_custom_call" | custom-call | flops 85899345920 | tf_op jit(solution)/shard_map/feed_down/pallas_call | solution.py:213
  236.7 5.8 %sum_y.4 = (bf16[8192,128]{1,0:T(8,128)(2,1)}, bf16[8192,128]{1,0:T(8,128)(2,1)}) custom-call(s32[2]{0:T(128)} %pad_add_fusion.at, bf16[2,8192,128]{2,1,0:T(8,128)(2,1)} %bitcast.218, bf16[2,8192,128]{2,1,0:T(8,128)(2,1)} %bitcast.219, bf16[2,8192,128]{2,1,0:T(8,128)(2,1)} %bitcast.60.refs_2_.refs_3_, bf16[2,8192,128]{2,1,0:T(8,128)(2,1)} %bitcast.60.refs_2_.refs_3_), custom_call_target="tpu_custom_call" | custom-call | flops 1000000000 | tf_op jit(solution)/shard_map/sum_y/pallas_call | solution.py:260
  244.4 14.3 %weight_grad_4096.1 = (bf16[512,4096]{1,0:T(8,128)(2,1)}, bf16[512,4096]{1,0:T(8,128)(2,1)}) custom-call(s32[1]{0:T(128)} %bitcast.48.at, bf16[1024,1024]{1,0:T(8,128)(2,1)} %get-tuple-element.378.refs_0_, bf16[1,1024,4096]{2,1,0:T(8,128)(2,1)} %bitcast.234), custom_call_target="tpu_custom_call" | custom-call | flops 429496736 | tf_op jit(solution)/shard_map/weight_grad_4096/pallas_call | solution.py:213
  258.7 23.2 %feed_back.1 = (f32[1024,1024]{1,0:T(8,128)}, bf16[1024,1024]{1,0:T(8,128)(2,1)}, bf16[1024,1024]{1,0:T(8,128)(2,1)}, f32[8,1024]{1,0:T(8,128)}) custom-call(s32[64]{0:T(128)} %stack.143.at, bf16[4,32,4096]{2,1,0:T(8,128)(2,1)} %pad_maximum_fusion.4.refs_0_, bf16[4,32,4096]{2,1,0:T(8,128)(2,1)} %collective-permute-done.17.refs_1_, ...), custom_call_target="tpu_custom_call" | custom-call | flops 53687091200 | tf_op jit(solution)/shard_map/feed_back/pallas_call | solution.py:213
  282.0 5.9 %sum_x.4 = (bf16[256,4096]{1,0:T(8,128)(2,1)}, bf16[256,4096]{1,0:T(8,128)(2,1)}) custom-call(s32[2]{0:T(128)} %pad_add_fusion.2.at, bf16[2,256,4096]{2,1,0:T(8,128)(2,1)} %bitcast.216, bf16[2,256,4096]{2,1,0:T(8,128)(2,1)} %bitcast.217, bf16[2,256,4096]{2,1,0:T(8,128)(2,1)} %bitcast.75.refs_2_.refs_3_, bf16[2,256,4096]{2,1,0:T(8,128)(2,1)} %bitcast.75.refs_2_.refs_3_), custom_call_target="tpu_custom_call" | custom-call | flops 1000000000 | tf_op jit(solution)/shard_map/sum_x/pallas_call | solution.py:260
  301.6 22.1 %attention_backward.2 = bf16[3,1,1024,512]{3,2,1,0:T(8,128)(2,1)} custom-call(bf16[1,1024,3072]{2,1,0:T(8,128)(2,1)} %bitcast.200, bf16[1,1024,3072]{2,1,0:T(8,128)(2,1)} %bitcast.201, bf16[1,1024,3072]{2,1,0:T(8,128)(2,1)} %bitcast.202, bf16[1,4,2,1024,1024]{4,3,2,1,0:T(8,128)(2,1)} %get-tuple-element.393.weight_ref, bf16[1,1024,1024]{2,1,0:T(8,128)(2,1)} %bitcast.250, ...), custom_call_target="tpu_custom_call" | custom-call | flops 1395864320 | tf_op jit(solution)/shard_map/attention_backward/pallas_call | solution.py:452
  323.7 11.0 %weight_grad_2560.1 = (bf16[512,2560]{1,0:T(8,128)(2,1)}, bf16[512,2560]{1,0:T(8,128)(2,1)}) custom-call(s32[1]{0:T(128)} %bitcast.48.at, bf16[1024,1024]{1,0:T(8,128)(2,1)} %get-tuple-element.475.refs_0_, bf16[3,1024,512]{2,1,0:T(8,128)(2,1)} %bitcast.214, bf16[1024,1024]{1,0:T(8,128)(2,1)} %get-tuple-element.432.refs_2_, bf16[1,1024,1024]{2,1,0:T(8,128)(2,1)} %bitcast.252), custom_call_target="tpu_custom_call" | custom-call | flops 268435456 | tf_op jit(solution)/shard_map/weight_grad_2560/pallas_call | solution.py:213
  345.2 22.2 %attention_backward.3 = bf16[3,1,1024,512]{3,2,1,0:T(8,128)(2,1)} custom-call(bf16[1,1024,3072]{2,1,0:T(8,128)(2,1)} %bitcast.203, bf16[1,1024,3072]{2,1,0:T(8,128)(2,1)} %bitcast.204, bf16[1,1024,3072]{2,1,0:T(8,128)(2,1)} %bitcast.205, bf16[1,4,2,1024,1024]{4,3,2,1,0:T(8,128)(2,1)} %get-tuple-element.418.weight_ref, bf16[1,1024,1024]{2,1,0:T(8,128)(2,1)} %bitcast.251, ...), custom_call_target="tpu_custom_call" | custom-call | flops 139586437120 | tf_op jit(solution)/shard_map/attention_backward/pallas_call | solution.py:452
  378.1 7.1 %weight_grad_1536.1 = (bf16[512,1536]{1,0:T(8,128)(2,1)}, bf16[512,1536]{1,0:T(8,128)(2,1)}) custom-call(s32[1]{0:T(128)} %bitcast.48.at, bf16[1024,1024]{1,0:T(8,128)(2,1)} %get-tuple-element.475.refs_0_, bf16[3,1024,512]{2,1,0:T(8,128)(2,1)} %bitcast.226), custom_call_target="tpu_custom_call" | custom-call | flops 161061280 | tf_op jit(solution)/shard_map/weight_grad_1536/pallas_call | solution.py:213
  397.5 9.8 %collective-permute-start.35 = (bf16[32,4096]{1,0:T(8,128)(2,1)}, bf16[32,4096]{1,0:T(8,128)(2,1)}, u32[]{:S(2)}, u32[]{:S(2)}) collective-permute-start(bf16[32,4096]{1,0:T(8,128)(2,1)} %get-tuple-element.498), channel_id=1, source_target_pairs={{0,8},{2,10},{4,12},{6,14},{8,16},{10,18},{12,20},{14,22},{16,24},... | collective-permute-start | bytes 786440 | tf_op jit(solution)/shard_map/ppermute | solution.py:61
  412.6 16.4 %project_back.1 = (bf16[1024,1024]{1,0:T(8,128)(2,1)}, f32[8,1024]{1,0:T(8,128)}) custom-call(s32[65]{0:T(128)} %stack.150.at, bf16[32,32,2048]{2,1,0:T(8,128)(2,1)} %bitcast.225, bf16[4,32,2176]{2,1,0:T(8,128)(2,1)} %copy-done.4, bf16[4,32,2176]{2,1,0:T(8,128)(2,1)} %copy-done.9, bf16[4,32,2176]{2,1,0:T(8,128)(2,1)} %copy-done.8, ...), custom_call_target="tpu_custom_call" | custom-call | flops 322122560 | tf_op jit(solution)/shard_map/project_back/pallas_call | solution.py:213
  442.1 18.2 %collective-permute-done.41.refs_4_.refs_5_.refs_6_.refs_7_ = bf16[4,32,1536]{2,1,0:T(8,128)(2,1)S(1)} collective-permute-done((bf16[4,32,1536]{2,1,0:T(8,128)(2,1)}, bf16[4,32,1536]{2,1,0:T(8,128)(2,1)S(1)}, u32[]{:S(2)}, u32[]{:S(2)}) %collective-permute-start.41) | collective-permute-done | bytes 393248 | tf_op jit(solution)/shard_map/ppermute | solution.py:48
  (277 shorter events, 168.6 us)
Async XLA Ops:
  7.4 84.0 %all-gather.7.cloned.1.call-start = ((), (), s32[]{:S(2)}) async-start(), calls=%async_computation.1 | async-start | bytes 4325376 | tf_op jit(solution)/shard_map/all_gather | solution.py:102
  9.1 194.8 %all-gather.5.cloned.1.call-start = ((), (), s32[]{:S(2)}) async-start(), calls=%async_computation | async-start | bytes 8650752 | tf_op jit(solution)/shard_map/all_gather | solution.py:102
  12.1 27.4 %collective-permute-start.3 = (bf16[512,1024]{1,0:T(8,128)(2,1)}, bf16[512,1024]{1,0:T(8,128)(2,1)}, u32[]{:S(2)}, u32[]{:S(2)}) collective-permute-start(bf16[512,1024]{1,0:T(8,128)(2,1)} %dynamic-slice_bitcast_fusion.3), channel_id=1, source_target_pairs={{0,1},{1,0},{2,3},{3,2},{4,5},{5,4},{6,7},{7,6},{8,9},{9,8},{10,11... | collective-permute-start | bytes 3145736 | tf_op jit(solution)/shard_map/ppermute | solution.py:48
  45.8 25.8 %collective-permute-start.7 = (bf16[4,32,2176]{2,1,0:T(8,128)(2,1)S(1)}, bf16[4,32,2176]{2,1,0:T(8,128)(2,1)S(1)}, u32[]{:S(2)}, u32[]{:S(2)}) collective-permute-start(bf16[4,32,2176]{2,1,0:T(8,128)(2,1)S(1)} %pad_maximum_fusion.5.refs_1_.refs_9_.refs_0_.refs_8_), channel_id=1, source_target_pairs={{0,5},{1,4},{2,7},{3,6},{4,1},{5,0},{6,3},{7,2},{8,13},{9,12},{10,... | collective-permute-start | bytes 1671176 | tf_op jit(solution)/shard_map/ppermute | solution.py:55
  46.2 25.9 %collective-permute-start.6 = (bf16[1,32,4096]{2,1,0:T(8,128)(2,1)S(1)}, bf16[1,32,4096]{2,1,0:T(8,128)(2,1)S(1)}, u32[]{:S(2)}, u32[]{:S(2)}) collective-permute-start(bf16[1,32,4096]{2,1,0:T(8,128)(2,1)S(1)} %bitcast.258), channel_id=1, source_target_pairs={{0,24},{2,26},{4,28},{6,30},{8,0},{10,2},{12,4},{14,6},{16,8},{18,... | collective-permute-start | bytes 786440 | tf_op jit(solution)/shard_map/ppermute | solution.py:61
  50.1 29.8 %collective-permute-start.5 = (bf16[1,32,4096]{2,1,0:T(8,128)(2,1)S(1)}, bf16[1,32,4096]{2,1,0:T(8,128)(2,1)}, u32[]{:S(2)}, u32[]{:S(2)}) collective-permute-start(bf16[1,32,4096]{2,1,0:T(8,128)(2,1)S(1)} %bitcast.259), channel_id=1, source_target_pairs={{0,16},{2,18},{4,20},{6,22},{8,24},{10,26},{12,28},{14,30},{16,0},... | collective-permute-start | bytes 786440 | tf_op jit(solution)/shard_map/ppermute | solution.py:61
  58.2 27.5 %collective-permute-start.4 = (bf16[1,32,4096]{2,1,0:T(8,128)(2,1)S(1)}, bf16[1,32,4096]{2,1,0:T(8,128)(2,1)}, u32[]{:S(2)}, u32[]{:S(2)}) collective-permute-start(bf16[1,32,4096]{2,1,0:T(8,128)(2,1)S(1)} %bitcast.260), channel_id=1, source_target_pairs={{0,8},{2,10},{4,12},{6,14},{8,16},{10,18},{12,20},{14,22},{16,24},... | collective-permute-start | bytes 786440 | tf_op jit(solution)/shard_map/ppermute | solution.py:61
  87.8 59.7 %collective-permute-start.12 = (bf16[4,32,4096]{2,1,0:T(8,128)(2,1)}, bf16[4,32,4096]{2,1,0:T(8,128)(2,1)}, u32[]{:S(2)}, u32[]{:S(2)}) collective-permute-start(bf16[4,32,4096]{2,1,0:T(8,128)(2,1)} %pad_maximum_fusion.4.refs_0_), channel_id=1, source_target_pairs={{0,4},{2,6},{4,0},{6,2},{8,12},{10,14},{12,8},{14,10},{16,20},{18,... | collective-permute-start | bytes 3145736 | tf_op jit(solution)/shard_map/ppermute | solution.py:51
  89.2 58.3 %collective-permute-start.11 = (bf16[4,32,4096]{2,1,0:T(8,128)(2,1)}, bf16[4,32,4096]{2,1,0:T(8,128)(2,1)}, u32[]{:S(2)}, u32[]{:S(2)}) collective-permute-start(bf16[4,32,4096]{2,1,0:T(8,128)(2,1)} %pad_maximum_fusion.4.refs_0_), channel_id=1, source_target_pairs={{0,1},{1,0},{2,3},{3,2},{4,5},{5,4},{6,7},{7,6},{8,9},{9,8},{10,11... | collective-permute-start | bytes 3145736 | tf_op jit(solution)/shard_map/ppermute | solution.py:48
  90.3 57.3 %collective-permute-start.10 = (bf16[4,32,4096]{2,1,0:T(8,128)(2,1)}, bf16[4,32,4096]{2,1,0:T(8,128)(2,1)}, u32[]{:S(2)}, u32[]{:S(2)}) collective-permute-start(bf16[4,32,4096]{2,1,0:T(8,128)(2,1)} %pad_maximum_fusion.4.refs_0_), channel_id=1, source_target_pairs={{0,5},{1,4},{2,7},{3,6},{4,1},{5,0},{6,3},{7,2},{8,13},{9,12},{10,... | collective-permute-start | bytes 3145736 | tf_op jit(solution)/shard_map/ppermute | solution.py:55
  149.8 36.3 %collective-permute-start.21 = (bf16[512,1024]{1,0:T(8,128)(2,1)}, bf16[512,1024]{1,0:T(8,128)(2,1)S(1)}, u32[]{:S(2)}, u32[]{:S(2)}) collective-permute-start(bf16[512,1024]{1,0:T(8,128)(2,1)} %dynamic-slice_bitcast_fusion.2), channel_id=1, source_target_pairs={{0,1},{1,0},{2,3},{3,2},{4,5},{5,4},{6,7},{7,6},{8,9},{9,8},{10,11... | collective-permute-start | bytes 3145736 | tf_op jit(solution)/shard_map/ppermute | solution.py:48
  204.0 32.8 %collective-permute-start.23 = (bf16[2,4,2,1024,128]{4,3,2,1,0:T(8,128)(2,1)}, bf16[2,4,2,1024,128]{4,3,2,1,0:T(8,128)(2,1)}, u32[]{:S(2)}, u32[]{:S(2)}) collective-permute-start(bf16[2,4,2,1024,128]{4,3,2,1,0:T(8,128)(2,1)} %bitcast.273), channel_id=1, source_target_pairs={{0,2},{2,0},{4,6},{6,4},{8,10},{10,8},{12,14},{14,12},{16,18},{18,... | collective-permute-start | bytes 12582920 | tf_op jit(solution)/shard_map/ppermute | solution.py:58
  236.6 45.3 %collective-permute-start.22 = (bf16[512,1024]{1,0:T(8,128)(2,1)}, bf16[512,1024]{1,0:T(8,128)(2,1)S(1)}, u32[]{:S(2)}, u32[]{:S(2)}) collective-permute-start(bf16[512,1024]{1,0:T(8,128)(2,1)} %dynamic-slice_bitcast_fusion.1), channel_id=1, source_target_pairs={{0,1},{1,0},{2,3},{3,2},{4,5},{5,4},{6,7},{7,6},{8,9},{9,8},{10,11... | collective-permute-start | bytes 3145736 | tf_op jit(solution)/shard_map/ppermute | solution.py:48
  242.6 48.2 %collective-permute-start.24 = (bf16[4,2,1024,128]{3,2,1,0:T(8,128)(2,1)}, bf16[4,2,1024,128]{3,2,1,0:T(8,128)(2,1)S(1)}, u32[]{:S(2)}, u32[]{:S(2)}) collective-permute-start(bf16[4,2,1024,128]{3,2,1,0:T(8,128)(2,1)} %bitcast.276), channel_id=1, source_target_pairs={{0,4},{2,6},{4,0},{6,2},{8,12},{10,14},{12,8},{14,10},{16,20},{18,... | collective-permute-start | bytes 6291464 | tf_op jit(solution)/shard_map/ppermute | solution.py:51
  287.9 51.8 %collective-permute-start.26 = (bf16[2,4,32,4096]{3,2,1,0:T(8,128)(2,1)}, bf16[2,4,32,4096]{3,2,1,0:T(8,128)(2,1)}, u32[]{:S(2)}, u32[]{:S(2)}) collective-permute-start(bf16[2,4,32,4096]{3,2,1,0:T(8,128)(2,1)} %bitcast.275), channel_id=1, source_target_pairs={{0,1},{1,0},{2,3},{3,2},{4,5},{5,4},{6,7},{7,6},{8,9},{9,8},{10,11... | collective-permute-start | bytes 6291464 | tf_op jit(solution)/shard_map/ppermute | solution.py:48
  296.0 38.7 %collective-permute-start.27 = (bf16[2,1024,128]{2,1,0:T(8,128)(2,1)}, bf16[2,1024,128]{2,1,0:T(8,128)(2,1)S(1)}, u32[]{:S(2)}, u32[]{:S(2)}) collective-permute-start(bf16[2,1024,128]{2,1,0:T(8,128)(2,1)} %bitcast.286), channel_id=1, source_target_pairs={{0,8},{2,10},{4,12},{6,14},{8,16},{10,18},{12,20},{14,22},{16,24},... | collective-permute-start | bytes 1572872 | tf_op jit(solution)/shard_map/ppermute | solution.py:61
  297.7 37.0 %collective-permute-start.28 = (bf16[2,1024,128]{2,1,0:T(8,128)(2,1)}, bf16[2,1024,128]{2,1,0:T(8,128)(2,1)S(1)}, u32[]{:S(2)}, u32[]{:S(2)}) collective-permute-start(bf16[2,1024,128]{2,1,0:T(8,128)(2,1)} %bitcast.285), channel_id=1, source_target_pairs={{0,16},{2,18},{4,20},{6,22},{8,24},{10,26},{12,28},{14,30},{16,0},... | collective-permute-start | bytes 1572872 | tf_op jit(solution)/shard_map/ppermute | solution.py:61
  300.0 34.8 %collective-permute-start.29 = (bf16[2,1024,128]{2,1,0:T(8,128)(2,1)}, bf16[2,1024,128]{2,1,0:T(8,128)(2,1)S(1)}, u32[]{:S(2)}, u32[]{:S(2)}) collective-permute-start(bf16[2,1024,128]{2,1,0:T(8,128)(2,1)} %bitcast.284), channel_id=1, source_target_pairs={{0,24},{2,26},{4,28},{6,30},{8,0},{10,2},{12,4},{14,6},{16,8},{18,... | collective-permute-start | bytes 1572872 | tf_op jit(solution)/shard_map/ppermute | solution.py:61
  334.7 38.9 %collective-permute-start.30 = (bf16[2,2,4,32,2560]{4,3,2,1,0:T(8,128)(2,1)}, bf16[2,2,4,32,2560]{4,3,2,1,0:T(8,128)(2,1)}, u32[]{:S(2)}, u32[]{:S(2)}) collective-permute-start(bf16[2,2,4,32,2560]{4,3,2,1,0:T(8,128)(2,1)} %bitcast.274), channel_id=1, source_target_pairs={{0,2},{2,0},{4,6},{6,4},{8,10},{10,8},{12,14},{14,12},{16,18},{18,... | collective-permute-start | bytes 7864328 | tf_op jit(solution)/shard_map/ppermute | solution.py:58
  385.2 43.9 %collective-permute-start.34 = (bf16[2,4,32,2560]{3,2,1,0:T(8,128)(2,1)}, bf16[2,4,32,2560]{3,2,1,0:T(8,128)(2,1)S(1)}, u32[]{:S(2)}, u32[]{:S(2)}) collective-permute-start(bf16[2,4,32,2560]{3,2,1,0:T(8,128)(2,1)} %bitcast.278), channel_id=1, source_target_pairs={{0,4},{2,6},{4,0},{6,2},{8,12},{10,14},{12,8},{14,10},{16,20},{18,... | collective-permute-start | bytes 3932168 | tf_op jit(solution)/shard_map/ppermute | solution.py:51
  395.3 39.3 %collective-permute-start.33 = (bf16[2,4,32,1536]{3,2,1,0:T(8,128)(2,1)}, bf16[2,4,32,1536]{3,2,1,0:T(8,128)(2,1)}, u32[]{:S(2)}, u32[]{:S(2)}) collective-permute-start(bf16[2,4,32,1536]{3,2,1,0:T(8,128)(2,1)} %bitcast.282), channel_id=1, source_target_pairs={{0,4},{2,6},{4,0},{6,2},{8,12},{10,14},{12,8},{14,10},{16,20},{18,... | collective-permute-start | bytes 2359304 | tf_op jit(solution)/shard_map/ppermute | solution.py:51
  397.5 31.5 %collective-permute-start.35 = (bf16[32,4096]{1,0:T(8,128)(2,1)}, bf16[32,4096]{1,0:T(8,128)(2,1)}, u32[]{:S(2)}, u32[]{:S(2)}) collective-permute-start(bf16[32,4096]{1,0:T(8,128)(2,1)} %get-tuple-element.498), channel_id=1, source_target_pairs={{0,8},{2,10},{4,12},{6,14},{8,16},{10,18},{12,20},{14,22},{16,24},... | collective-permute-start | bytes 786440 | tf_op jit(solution)/shard_map/ppermute | solution.py:61
  433.9 29.8 %collective-permute-start.40 = (bf16[4,32,2560]{2,1,0:T(8,128)(2,1)}, bf16[4,32,2560]{2,1,0:T(8,128)(2,1)S(1)}, u32[]{:S(2)}, u32[]{:S(2)}) collective-permute-start(bf16[4,32,2560]{2,1,0:T(8,128)(2,1)} %bitcast.283), channel_id=1, source_target_pairs={{0,1},{1,0},{2,3},{3,2},{4,5},{5,4},{6,7},{7,6},{8,9},{9,8},{10,11... | collective-permute-start | bytes 1966088 | tf_op jit(solution)/shard_map/ppermute | solution.py:48
  441.4 39.5 %collective-permute-start.38 = (bf16[512,1024]{1,0:T(8,128)(2,1)}, bf16[512,1024]{1,0:T(8,128)(2,1)}, u32[]{:S(2)}, u32[]{:S(2)}) collective-permute-start(bf16[512,1024]{1,0:T(8,128)(2,1)} %dynamic-slice_bitcast_fusion), channel_id=1, source_target_pairs={{0,1},{1,0},{2,3},{3,2},{4,5},{5,4},{6,7},{7,6},{8,9},{9,8},{10,11... | collective-permute-start | bytes 3145736 | tf_op jit(solution)/shard_map/ppermute | solution.py:48
  (74 other events, 842.9 us)
Sparse Core Ops, SparseCore 0:
  11.8 76.3 all-gather.6
  91.2 99.5 all-gather.4
